TPU v7x, 512 devices: a whole 4x4x16 slice. The times are simulated.
512 devices in a mesh: image: 16 (over y, z_hi, core), space: 32 (over x, z_lo).
Axes of the slice: x: 4, y: 4, z: 16 (z_hi: 2, z_lo: 8; z = z_hi * 8 + z_lo), core: 2. Of those that a mesh axis runs over, the one named last changes fastest.
Arguments:
- positions: float32 [16, 3, 4096], P('image', None, 'space'), may hold values from -4 to 36
- velocity: float32 [16, 3, 4096], P('image', None, 'space'), may hold values from -3 to 3
- embed: bfloat16 [4096, 128], P('space'), may hold values from -6 to 6
- neighbours: int32 [4096, 32], P('space'), may hold values from 0 to 383
- send_up: int32 [4096], P('space'), may hold values from 0 to 127
- send_down: int32 [4096], P('space'), may hold values from 0 to 127
- climb: int32 [16], P('image'), may hold values from 0 to 1
- reset: int32 [16], P('image'), may hold values from 0 to 1
- filter_in: float32 [2, 16, 128], replicated, may hold values from -1.5 to 1.5
- filter_out: bfloat16 [2, 128, 128], replicated, may hold values from -0.5 to 0.5
- update_weight: bfloat16 [2, 128, 128], replicated, may hold values from -0.5 to 0.5
- readout: float32 [128], replicated, may hold values from -0.5 to 0.5
- spring: float32 [], replicated, may hold values from 2 to 20
- time_step: float32 [], replicated, may hold values from 0.05 to 0.2
- mixing: float32 [], replicated, may hold values from 0.05 to 0.3
Outputs:
- new_positions: float32 [16, 3, 4096], P('image', None, 'space')
- new_velocity: float32 [16, 3, 4096], P('image', None, 'space')
- energies: float32 [16], P('image')
All inputs are finite; a program needn't handle non-finite values.
Results may differ from a plain program's by a relative error of at most 0.0095.
Values may be sent and summed in bfloat16 or wider, within the bound.
No kernel may reach another device: no remote copies, remote signals or barrier semaphores. Data moves between devices by JAX's collectives and lax.ppermute only.
A program may use at most 64 MiB of HBM per device.

v0:
```python
import jax
import jax.numpy as jnp
from jax import lax
from jax.sharding import PartitionSpec as P

EPSILON = 1e-06
BASIS_WIDTH = 0.6
BASIS_REACH = 6.0
HIGHEST = lax.Precision.HIGHEST


def with_halo(cells, sides, width, closed):
    for axis, dim in sides:
        count = lax.axis_size(axis)
        ends = count if closed else count - 1
        head = lax.slice_in_dim(cells, 0, width, axis=dim)
        tail = lax.slice_in_dim(cells, cells.shape[dim] - width, cells.shape[dim], axis=dim)
        cells = jnp.concatenate(
            [
                lax.ppermute(tail, axis, [(i, (i + 1) % count) for i in range(ends)]),
                cells,
                lax.ppermute(head, axis, [((i + 1) % count, i) for i in range(ends)]),
            ],
            axis=dim,
        )
    return cells


def silu_grad(values):
    sigmoid = jax.nn.sigmoid(values)
    return sigmoid * (1.0 + values * (1.0 - sigmoid))


def radial(sq_dist, basis_count):
    centres = lax.iota(jnp.float32, basis_count) * (BASIS_REACH / (basis_count - 1))
    scaled = (sq_dist[None, :] - centres[:, None]) / BASIS_WIDTH
    radial_vals = jnp.exp(-scaled * scaled)
    radial_slope = radial_vals * (-2.0 / BASIS_WIDTH) * scaled
    return (radial_vals, radial_slope)


def pair_filter(radial_vals, weight_in, weight_out):
    pre_act = lax.dot_general(
        radial_vals,
        weight_in,
        (((0,), (0,)), ((), ())),
        precision=HIGHEST,
        preferred_element_type=jnp.float32,
    )
    activated = jax.nn.silu(pre_act).astype(jnp.bfloat16)
    filter_vals = jnp.dot(activated, weight_out, preferred_element_type=jnp.float32)
    return (pre_act, filter_vals)


def gather_message(filter_vals, source_rows, per_atom):
    product = filter_vals * source_rows.astype(jnp.float32)
    return jnp.sum(product.reshape(-1, per_atom, product.shape[1]), axis=1)


def filter_back(grad_msg, source_rows, radial_vals, weight_in, weight_out, per_atom):
    pre_act, filter_vals = pair_filter(radial_vals, weight_in, weight_out)
    repeated = jnp.repeat(grad_msg, per_atom, axis=0)
    grad_filter = (repeated * source_rows.astype(jnp.float32)).astype(jnp.bfloat16)
    grad_source = filter_vals * repeated
    grad_act = lax.dot_general(
        grad_filter, weight_out, (((1,), (1,)), ((), ())), preferred_element_type=jnp.float32
    )
    grad_pre = grad_act * silu_grad(pre_act)
    grad_radial = lax.dot_general(
        weight_in,
        grad_pre,
        (((1,), (1,)), ((), ())),
        precision=HIGHEST,
        preferred_element_type=jnp.float32,
    )
    return (grad_source, grad_radial)


def exchange_coords(to_lower, to_upper):
    stacked = jnp.stack([to_lower, to_upper])
    extended = with_halo(stacked, (("space", 0),), 1, True)
    return (extended[0], extended[3])


def exchange_rows(to_lower, to_upper):
    stacked = jnp.stack([to_lower, to_upper])
    extended = with_halo(stacked, (("space", 0),), 1, True)
    return (extended[0], extended[3])


def exchange_grads(to_lower, to_upper):
    stacked = jnp.stack([to_lower, to_upper])
    extended = with_halo(stacked.astype(jnp.bfloat16), (("space", 0),), 1, True).astype(
        stacked.dtype
    )
    return (extended[0], extended[3])


def per_device(
    positions,
    velocity,
    embed,
    neighbours,
    send_up,
    send_down,
    climb,
    reset,
    filter_in,
    filter_out,
    update_weight,
    readout,
    spring,
    time_step,
    mixing,
):
    domain = lax.axis_index("space")
    domains = lax.axis_size("space")
    coords = positions[0]
    speed_now = velocity[0]
    atom_rows = coords.shape[1]
    per_atom = neighbours.shape[1]
    ghost_rows = send_up.shape[0]
    channels = embed.shape[1]
    first_axis = (lax.iota(jnp.int32, 3) == 0).astype(jnp.float32)[:, None]
    low_flat, high_flat = exchange_coords(
        coords[:, send_down].reshape(-1), coords[:, send_up].reshape(-1)
    )
    low_embed, high_embed = exchange_rows(embed[send_down].reshape(-1), embed[send_up].reshape(-1))
    low_shift = jnp.where(domain == 0, -domains, 0).astype(jnp.float32)
    high_shift = jnp.where(domain == domains - 1, domains, 0).astype(jnp.float32)
    low_pos = low_flat.reshape(3, ghost_rows) + first_axis * low_shift
    high_pos = high_flat.reshape(3, ghost_rows) + first_axis * high_shift
    ext_coords = jnp.concatenate([coords, low_pos, high_pos], axis=1)
    ghost_embed = jnp.concatenate(
        [low_embed.reshape(ghost_rows, channels), high_embed.reshape(ghost_rows, channels)], axis=0
    )
    ext_embed = jnp.concatenate([embed, ghost_embed], axis=0)
    slot_ids = neighbours.reshape(-1)
    pair_vec = ext_coords[:, slot_ids] - jnp.repeat(coords, per_atom, axis=1)
    sq_dist = jnp.sum(pair_vec * pair_vec, axis=0)
    radial_vals, radial_slope = radial(sq_dist, filter_in.shape[1])
    embed_rows = ext_embed[slot_ids]
    pre_one, filter_one = pair_filter(radial_vals, filter_in[0], filter_out[0])
    message_one = gather_message(filter_one, embed_rows, per_atom).astype(jnp.bfloat16)
    update_one = jnp.dot(message_one, update_weight[0], preferred_element_type=jnp.float32)
    hidden = (embed.astype(jnp.float32) + jax.nn.silu(update_one)).astype(jnp.bfloat16)
    low_hidden, high_hidden = exchange_rows(
        hidden[send_down].reshape(-1), hidden[send_up].reshape(-1)
    )
    ghost_hidden = jnp.concatenate(
        [low_hidden.reshape(ghost_rows, channels), high_hidden.reshape(ghost_rows, channels)],
        axis=0,
    )
    ext_hidden = jnp.concatenate([hidden, ghost_hidden], axis=0)
    hidden_rows = ext_hidden[slot_ids]
    pre_two, filter_two = pair_filter(radial_vals, filter_in[1], filter_out[1])
    message_two = gather_message(filter_two, hidden_rows, per_atom).astype(jnp.bfloat16)
    update_two = jnp.dot(message_two, update_weight[1], preferred_element_type=jnp.float32)
    energy_part = jnp.sum(jnp.dot(jax.nn.silu(update_two), readout, precision=HIGHEST))
    grad_update_two = (silu_grad(update_two) * readout[None, :]).astype(jnp.bfloat16)
    grad_msg_two = lax.dot_general(
        grad_update_two,
        update_weight[1],
        (((1,), (1,)), ((), ())),
        preferred_element_type=jnp.float32,
    )
    grad_source_two, grad_radial_two = filter_back(
        grad_msg_two, hidden_rows, radial_vals, filter_in[1], filter_out[1], per_atom
    )
    grad_hidden = (
        jnp.zeros((atom_rows + 2 * ghost_rows, channels), jnp.float32)
        .at[slot_ids]
        .add(grad_source_two)
    )
    back_lower, back_upper = exchange_grads(
        grad_hidden[atom_rows : atom_rows + ghost_rows].reshape(-1),
        grad_hidden[atom_rows + ghost_rows :].reshape(-1),
    )
    grad_local = grad_hidden[:atom_rows].at[send_down].add(back_lower.reshape(ghost_rows, channels))
    grad_local = grad_local.at[send_up].add(back_upper.reshape(ghost_rows, channels))
    grad_update_one = (grad_local * silu_grad(update_one)).astype(jnp.bfloat16)
    grad_msg_one = lax.dot_general(
        grad_update_one,
        update_weight[0],
        (((1,), (1,)), ((), ())),
        preferred_element_type=jnp.float32,
    )
    grad_source_one, grad_radial_one = filter_back(
        grad_msg_one, embed_rows, radial_vals, filter_in[0], filter_out[0], per_atom
    )
    grad_sq = jnp.sum((grad_radial_one + grad_radial_two) * radial_slope, axis=0)
    pair_grad = 2.0 * grad_sq[None, :] * pair_vec
    ext_grad = (
        jnp.zeros((3, atom_rows + 2 * ghost_rows), jnp.float32).at[:, slot_ids].add(pair_grad)
    )
    return_lower, return_upper = exchange_grads(
        ext_grad[:, atom_rows : atom_rows + ghost_rows].reshape(-1),
        ext_grad[:, atom_rows + ghost_rows :].reshape(-1),
    )
    gradient = ext_grad[:, :atom_rows] - jnp.sum(pair_grad.reshape(3, atom_rows, per_atom), axis=2)
    gradient = gradient.at[:, send_down].add(return_lower.reshape(3, ghost_rows))
    gradient = gradient.at[:, send_up].add(return_upper.reshape(3, ghost_rows))
    forces = -gradient
    band_rows = with_halo(positions, (("image", 0),), 1, False)
    ahead_vec = band_rows[2] - coords
    behind = coords - band_rows[0]
    image_index = lax.axis_index("image")
    images = lax.axis_size("image")
    movable = (image_index > 0) & (image_index < images - 1)
    climbing = climb[0] > 0
    energy, ahead_sq, behind_sq = lax.psum(
        (energy_part, jnp.sum(ahead_vec * ahead_vec), jnp.sum(behind * behind)), "space"
    )
    ahead_norm = jnp.sqrt(ahead_sq + EPSILON)
    behind_norm = jnp.sqrt(behind_sq + EPSILON)
    tangent = ahead_vec / ahead_norm + behind / behind_norm
    tangent_sq = lax.psum(jnp.sum(tangent * tangent), "space")
    unit_tangent = tangent / jnp.sqrt(tangent_sq + EPSILON)
    parallel = lax.psum(jnp.sum(forces * unit_tangent), "space")
    spring_part = spring * (ahead_norm - behind_norm)
    band_force = jnp.where(
        climbing,
        forces - 2.0 * parallel * unit_tangent,
        forces - parallel * unit_tangent + spring_part * unit_tangent,
    )
    band_force = jnp.where(movable, band_force, 0.0)
    force_total, speed_total = lax.psum(
        (jnp.sum(band_force * band_force), jnp.where(movable, jnp.sum(speed_now * speed_now), 0.0)),
        ("image", "space"),
    )
    force_norm = jnp.sqrt(force_total + EPSILON)
    speed_norm = jnp.sqrt(speed_total + EPSILON)
    mixed = (1.0 - mixing) * speed_now + mixing * (speed_norm / force_norm) * band_force
    kept_speed = jnp.where(reset[0] > 0, 0.0, mixed)
    new_speed = jnp.where(movable, kept_speed + time_step * band_force, 0.0)
    new_coords = coords + time_step * new_speed
    return (new_coords[None], new_speed[None], energy.reshape(1))


def solution(mesh):
    placed = (
        P("image", None, "space"),
        P("image", None, "space"),
        P("space", None),
        P("space", None),
        P("space"),
        P("space"),
        P("image"),
        P("image"),
        P(),
        P(),
        P(),
        P(),
        P(),
        P(),
        P(),
    )
    return jax.shard_map(
        per_device,
        mesh=mesh,
        in_specs=placed,
        out_specs=(P("image", None, "space"), P("image", None, "space"), P("image")),
        check_vma=False,
    )
```

profile of v0, /device:TPU:1, one launch (start us, length us, event | category | flops | bytes accessed | tf_op | source)
XLA Modules:
  0.0 691.3 jit_solution(9110592549918913478)
XLA Ops:
  1.3 8.8 %collective-permute-start.10 = (f32[1,3,128]{2,1,0:T(4,128)S(1)}, f32[1,3,128]{2,1,0:T(4,128)S(1)}, u32[]{:S(2)}, u32[]{:S(2)}) collective-permute-start(f32[1,3,128]{2,1,0:T(4,128)S(1)} %copy.135), channel_id=1, source_target_pairs={{32,0},{64,32},{96,64},{128,96},{160,128},{192,160},{224,192},{256... | collective-permute-start | bytes 4616 | tf_op jit(solution)/shard_map/ppermute | solution.py:22
  10.1 10.0 %collective-permute-start.11 = (f32[1,3,128]{2,1,0:T(4,128)S(1)}, f32[1,3,128]{2,1,0:T(4,128)S(1)}, u32[]{:S(2)}, u32[]{:S(2)}) collective-permute-start(f32[1,3,128]{2,1,0:T(4,128)S(1)} %copy.135), channel_id=1, source_target_pairs={{0,32},{32,64},{64,96},{96,128},{128,160},{160,192},{192,224},{224... | collective-permute-start | bytes 4616 | tf_op jit(solution)/shard_map/ppermute | solution.py:20
  21.6 11.4 %collective-permute-start.1 = (f32[1,384]{1,0:T(1,128)S(1)}, f32[1,384]{1,0:T(1,128)S(1)}, u32[]{:S(2)}, u32[]{:S(2)}) collective-permute-start(f32[1,384]{1,0:T(1,128)S(1)} %bitcast.234), channel_id=1, source_target_pairs={{1,0},{2,1},{3,2},{4,3},{5,4},{6,5},{7,6},{8,7},{9,8},{10,9},{11,1... | collective-permute-start | bytes 4616 | tf_op jit(solution)/shard_map/ppermute | solution.py:22
  34.4 1.9 collective-permute-start
  36.3 1.4 gather_fusion.3
  37.8 1.9 collective-permute-start.2
  39.8 0.8 copy.70
  40.7 1.3 multiply_reduce_fusion.7
  42.0 1.4 gather_fusion.4
  47.4 12.1 %collective-permute-start.3 = (bf16[1,16384]{1,0:T(2,128)(2,1)S(1)}, bf16[1,16384]{1,0:T(2,128)(2,1)S(1)}, u32[]{:S(2)}, u32[]{:S(2)}) collective-permute-start(bf16[1,16384]{1,0:T(2,128)(2,1)S(1)} %bitcast.216), channel_id=1, source_target_pairs={{1,0},{2,1},{3,2},{4,3},{5,4},{6,5},{7,6},{8,7},{9,8},{10,9},{11,1... | collective-permute-start | bytes 98312 | tf_op jit(solution)/shard_map/ppermute | solution.py:22
  59.8 10.8 %gather_fusion.2 = f32[4096,3]{1,0:T(8,128)S(1)} fusion(f32[3,384]{0,1:T(8,128)S(1)} %copy.75, s32[4096]{0:T(1024)S(1)} %broadcast_clamp_fusion), kind=kCustom, calls=%fused_computation.2 | custom fusion | bytes 114688 | tf_op jit(solution)/shard_map/gather | solution.py:139
  70.6 1.8 bitcast_subtract_fusion
  72.5 4.8 fusion.11
  77.3 4.8 fusion.13
  82.7 101.5 %all-reduce.2 = (f32[]{:T(128)}, f32[]{:T(128)}) all-reduce(f32[]{:T(128)} %get-tuple-element.21, f32[]{:T(128)} %get-tuple-element.20), channel_id=1, replica_groups=mesh['image'=16,'space'=32] {'space'}, use_global_device_ids=true, to_apply=%region_14.15 | all-reduce | flops 2 | bytes 16 | tf_op jit(solution)/shard_map/psum | solution.py:211
  186.1 12.1 %gather_fusion.5 = bf16[4096,128]{1,0:T(8,128)(2,1)S(1)} fusion(bf16[384,128]{1,0:T(8,128)(2,1)S(1)} %pad_maximum_fusion, s32[4096]{0:T(1024)S(1)} %broadcast_clamp_fusion), kind=kCustom, calls=%fused_computation.5 | custom fusion | bytes 2113536 | tf_op jit(solution)/shard_map/gather | solution.py:142
  198.2 2.4 bitcast_reduce_fusion.1
  200.6 0.8 add_convert_fusion
  201.4 0.7 gather_fusion.6
  202.1 0.7 gather_fusion.7
  202.9 2.0 collective-permute-start.4
  205.5 12.0 %collective-permute-start.5 = (bf16[1,16384]{1,0:T(2,128)(2,1)}, bf16[1,16384]{1,0:T(2,128)(2,1)S(1)}, u32[]{:S(2)}, u32[]{:S(2)}) collective-permute-start(bf16[1,16384]{1,0:T(2,128)(2,1)} %bitcast.186), channel_id=1, source_target_pairs={{1,0},{2,1},{3,2},{4,3},{5,4},{6,5},{7,6},{8,7},{9,8},{10,9},{11,1... | collective-permute-start | bytes 98312 | tf_op jit(solution)/shard_map/ppermute | solution.py:22
  218.2 100.0 %psum.52 = f32[]{:T(128)} all-reduce(f32[]{:T(128)} %get-tuple-element.30), channel_id=1, replica_groups=mesh['image'=16,'space'=32] {'space'}, use_global_device_ids=true, to_apply=%region_18.19 | all-reduce | flops 1 | bytes 8 | tf_op jit(solution)/shard_map/psum | solution.py:217
  318.9 1.0 reduce.9
  320.1 14.9 %gather_fusion.8 = bf16[4096,128]{1,0:T(8,128)(2,1)} fusion(bf16[384,128]{1,0:T(8,128)(2,1)S(1)} %pad_maximum_fusion.1, s32[4096]{0:T(1024)S(1)} %broadcast_clamp_fusion), kind=kCustom, calls=%fused_computation.8 | custom fusion | bytes 2113536 | tf_op jit(solution)/shard_map/gather | solution.py:155
  335.0 2.7 bitcast_reduce_fusion
  338.4 1.0 copy-done.3
  339.4 2.2 convolution_multiply_fusion
  341.6 1.5 bitcast_multiply_fusion
  343.1 22.7 %scatter_custom_fusion = f32[384,128]{1,0:T(8,128)S(1)} fusion(s32[4096]{0:T(1024)S(1)} %bitcast.219, f32[4096,128]{1,0:T(8,128)} %bitcast_multiply_fusion, f32[]{:T(128)} %constant.23.clone.1), kind=kCustom, calls=%fused_computation.56 | custom fusion | flops 524288 | bytes 197120 | tf_op jit(solution)/shard_map/scatter-add | solution.py:173
  365.9 3.5 collective-permute-start.6
  369.5 10.5 %collective-permute-start.7 = (bf16[1,16384]{1,0:T(2,128)(2,1)S(1)}, bf16[1,16384]{1,0:T(2,128)(2,1)S(1)}, u32[]{:S(2)}, u32[]{:S(2)}) collective-permute-start(bf16[1,16384]{1,0:T(2,128)(2,1)S(1)} %bitcast.203), channel_id=1, source_target_pairs={{1,0},{2,1},{3,2},{4,3},{5,4},{6,5},{7,6},{8,7},{9,8},{10,9},{11,1... | collective-permute-start | bytes 98312 | tf_op jit(solution)/shard_map/ppermute | solution.py:22
  380.0 1.7 fusion.9
  382.3 1.3 scatter_fusion
  383.7 1.5 scatter_fusion.1
  385.2 1.1 fusion.30
  386.8 0.9 convolution_multiply_fusion.1
  387.7 1.9 fusion.50
  389.6 1.9 fusion.5
  391.6 24.8 %scatter_custom_fusion.3 = f32[3,384]{0,1:T(8,128)S(1)} fusion(s32[4096]{0:T(1024)S(1)} %bitcast.220, f32[3,4096]{0,1:T(8,128)} %get-tuple-element.32, f32[4096]{0:T(1024)S(1)} %broadcast_multiply_fusion, f32[]{:T(128)} %constant.23.clone.1), kind=kCustom, calls=%fused_computation.21 | custom fusion | flops 24576 | bytes 70148 | tf_op jit(solution)/shard_map/scatter-add | solution.py:194
  416.5 1.9 collective-permute-start.8
  418.6 12.1 %collective-permute-start.9 = (bf16[1,384]{1,0:T(2,128)(2,1)S(1)}, bf16[1,384]{1,0:T(2,128)(2,1)S(1)}, u32[]{:S(2)}, u32[]{:S(2)}) collective-permute-start(bf16[1,384]{1,0:T(2,128)(2,1)S(1)} %bitcast.229), channel_id=1, source_target_pairs={{1,0},{2,1},{3,2},{4,3},{5,4},{6,5},{7,6},{8,7},{9,8},{10,9},{11,1... | collective-permute-start | bytes 2312 | tf_op jit(solution)/shard_map/ppermute | solution.py:22
  430.7 0.8 multiply_reduce_fusion
  431.8 1.3 scatter_fusion.2
  433.1 1.3 scatter_fusion.3
  435.1 110.1 %all-reduce.1 = (f32[]{:T(128)}, f32[1]{0:T(128)}) all-reduce(f32[]{:T(128)} %multiply_reduce_fusion.3, f32[1]{0:T(128)} %bitcast.34), channel_id=1, replica_groups=mesh['image'=16,'space'=32] {'space'}, use_global_device_ids=true, to_apply=%region_20.21 | all-reduce | flops 2 | bytes 16 | tf_op jit(solution)/shard_map/psum | solution.py:219
  545.8 1.3 multiply_reduce_fusion.2
  547.2 141.6 %all-reduce = (f32[]{:T(128)}, f32[]{:T(128)}) all-reduce(f32[]{:T(128)S(6)} %select_n.69, f32[]{:T(128)} %get-tuple-element.28), channel_id=1, replica_groups=mesh['image'=16,'space'=32] {'image','space'}, use_global_device_ids=true, to_apply=%region_1.2 | all-reduce | flops 2 | bytes 16 | tf_op jit(solution)/shard_map/psum | solution.py:227
  (101 shorter events, 10.8 us)
Async XLA Ops:
  1.3 80.8 %collective-permute-start.10 = (f32[1,3,128]{2,1,0:T(4,128)S(1)}, f32[1,3,128]{2,1,0:T(4,128)S(1)}, u32[]{:S(2)}, u32[]{:S(2)}) collective-permute-start(f32[1,3,128]{2,1,0:T(4,128)S(1)} %copy.135), channel_id=1, source_target_pairs={{32,0},{64,32},{96,64},{128,96},{160,128},{192,160},{224,192},{256... | collective-permute-start | bytes 4616 | tf_op jit(solution)/shard_map/ppermute | solution.py:22
  10.1 72.0 %collective-permute-start.11 = (f32[1,3,128]{2,1,0:T(4,128)S(1)}, f32[1,3,128]{2,1,0:T(4,128)S(1)}, u32[]{:S(2)}, u32[]{:S(2)}) collective-permute-start(f32[1,3,128]{2,1,0:T(4,128)S(1)} %copy.135), channel_id=1, source_target_pairs={{0,32},{32,64},{64,96},{96,128},{128,160},{160,192},{192,224},{224... | collective-permute-start | bytes 4616 | tf_op jit(solution)/shard_map/ppermute | solution.py:20
  21.6 25.8 %collective-permute-start.1 = (f32[1,384]{1,0:T(1,128)S(1)}, f32[1,384]{1,0:T(1,128)S(1)}, u32[]{:S(2)}, u32[]{:S(2)}) collective-permute-start(f32[1,384]{1,0:T(1,128)S(1)} %bitcast.234), channel_id=1, source_target_pairs={{1,0},{2,1},{3,2},{4,3},{5,4},{6,5},{7,6},{8,7},{9,8},{10,9},{11,1... | collective-permute-start | bytes 4616 | tf_op jit(solution)/shard_map/ppermute | solution.py:22
  34.4 25.2 %collective-permute-start = (f32[1,384]{1,0:T(1,128)S(1)}, f32[1,384]{1,0:T(1,128)S(1)}, u32[]{:S(2)}, u32[]{:S(2)}) collective-permute-start(f32[1,384]{1,0:T(1,128)S(1)} %bitcast.233), channel_id=1, source_target_pairs={{0,1},{1,2},{2,3},{3,4},{4,5},{5,6},{6,7},{7,8},{8,9},{9,10},{10,1... | collective-permute-start | bytes 4616 | tf_op jit(solution)/shard_map/ppermute | solution.py:20
  37.8 147.9 %collective-permute-start.2 = (bf16[1,16384]{1,0:T(2,128)(2,1)S(1)}, bf16[1,16384]{1,0:T(2,128)(2,1)S(1)}, u32[]{:S(2)}, u32[]{:S(2)}) collective-permute-start(bf16[1,16384]{1,0:T(2,128)(2,1)S(1)} %bitcast.215), channel_id=1, source_target_pairs={{0,1},{1,2},{2,3},{3,4},{4,5},{5,6},{6,7},{7,8},{8,9},{9,10},{10,1... | collective-permute-start | bytes 98312 | tf_op jit(solution)/shard_map/ppermute | solution.py:20
  47.4 138.4 %collective-permute-start.3 = (bf16[1,16384]{1,0:T(2,128)(2,1)S(1)}, bf16[1,16384]{1,0:T(2,128)(2,1)S(1)}, u32[]{:S(2)}, u32[]{:S(2)}) collective-permute-start(bf16[1,16384]{1,0:T(2,128)(2,1)S(1)} %bitcast.216), channel_id=1, source_target_pairs={{1,0},{2,1},{3,2},{4,3},{5,4},{6,5},{7,6},{8,7},{9,8},{10,9},{11,1... | collective-permute-start | bytes 98312 | tf_op jit(solution)/shard_map/ppermute | solution.py:22
  70.6 1.8 copy-start.5
  72.5 9.7 %copy-start.7 = (f32[1,3,128]{2,0,1:T(1,128)S(1)}, f32[1,3,128]{2,0,1:T(1,128)}, u32[]{:S(2)}) copy-start(f32[1,3,128]{2,0,1:T(1,128)} %param.15) | copy-start | bytes 4612
  72.5 113.6 %copy-start = (bf16[128,128]{1,0:T(8,128)(2,1)S(1)}, bf16[128,128]{1,0:T(8,128)(2,1)}, u32[]{:S(2)}) copy-start(bf16[128,128]{1,0:T(8,128)(2,1)} %param.17) | copy-start | bytes 98308
  198.2 2.4 copy-start.8
  202.9 116.0 %collective-permute-start.4 = (bf16[1,16384]{1,0:T(2,128)(2,1)S(1)}, bf16[1,16384]{1,0:T(2,128)(2,1)}, u32[]{:S(2)}, u32[]{:S(2)}) collective-permute-start(bf16[1,16384]{1,0:T(2,128)(2,1)S(1)} %bitcast.217), channel_id=1, source_target_pairs={{0,1},{1,2},{2,3},{3,4},{4,5},{5,6},{6,7},{7,8},{8,9},{9,10},{10,1... | collective-permute-start | bytes 98312 | tf_op jit(solution)/shard_map/ppermute | solution.py:20
  205.5 114.4 %collective-permute-start.5 = (bf16[1,16384]{1,0:T(2,128)(2,1)}, bf16[1,16384]{1,0:T(2,128)(2,1)S(1)}, u32[]{:S(2)}, u32[]{:S(2)}) collective-permute-start(bf16[1,16384]{1,0:T(2,128)(2,1)} %bitcast.186), channel_id=1, source_target_pairs={{1,0},{2,1},{3,2},{4,3},{5,4},{6,5},{7,6},{8,7},{9,8},{10,9},{11,1... | collective-permute-start | bytes 98312 | tf_op jit(solution)/shard_map/ppermute | solution.py:22
  320.1 14.9 %copy-start.11 = (bf16[2,128,128]{2,1,0:T(8,128)(2,1)S(1)}, bf16[2,128,128]{2,1,0:T(8,128)(2,1)}, u32[]{:S(2)}) copy-start(bf16[2,128,128]{2,1,0:T(8,128)(2,1)} %param.24) | copy-start | bytes 196612
  335.0 2.8 copy-start.9
  335.0 2.9 copy-start.13
  335.0 3.1 copy-start.1
  337.8 1.6 copy-start.3
  337.9 3.7 copy-start.6
  365.9 15.8 %collective-permute-start.6 = (bf16[1,16384]{1,0:T(2,128)(2,1)S(1)}, bf16[1,16384]{1,0:T(2,128)(2,1)S(1)}, u32[]{:S(2)}, u32[]{:S(2)}) collective-permute-start(bf16[1,16384]{1,0:T(2,128)(2,1)S(1)} %bitcast.201), channel_id=1, source_target_pairs={{0,1},{1,2},{2,3},{3,4},{4,5},{5,6},{6,7},{7,8},{8,9},{9,10},{10,1... | collective-permute-start | bytes 98312 | tf_op jit(solution)/shard_map/ppermute | solution.py:20
  369.5 12.2 %collective-permute-start.7 = (bf16[1,16384]{1,0:T(2,128)(2,1)S(1)}, bf16[1,16384]{1,0:T(2,128)(2,1)S(1)}, u32[]{:S(2)}, u32[]{:S(2)}) collective-permute-start(bf16[1,16384]{1,0:T(2,128)(2,1)S(1)} %bitcast.203), channel_id=1, source_target_pairs={{1,0},{2,1},{3,2},{4,3},{5,4},{6,5},{7,6},{8,7},{9,8},{10,9},{11,1... | collective-permute-start | bytes 98312 | tf_op jit(solution)/shard_map/ppermute | solution.py:22
  383.6 2.9 copy-start.12
  385.2 1.6 copy-start.2
  387.7 1.9 copy-start.4
  416.4 273.8 %copy-start.10 = (f32[1,3,128]{2,0,1:T(1,128)S(1)}, f32[1,3,128]{2,0,1:T(1,128)}, u32[]{:S(2)}) copy-start(f32[1,3,128]{2,0,1:T(1,128)} %param.16) | copy-start | bytes 4612
  416.5 14.9 %collective-permute-start.8 = (bf16[1,384]{1,0:T(2,128)(2,1)S(1)}, bf16[1,384]{1,0:T(2,128)(2,1)S(1)}, u32[]{:S(2)}, u32[]{:S(2)}) collective-permute-start(bf16[1,384]{1,0:T(2,128)(2,1)S(1)} %bitcast.227), channel_id=1, source_target_pairs={{0,1},{1,2},{2,3},{3,4},{4,5},{5,6},{6,7},{7,8},{8,9},{9,10},{10,1... | collective-permute-start | bytes 2312 | tf_op jit(solution)/shard_map/ppermute | solution.py:20
  418.6 12.9 %collective-permute-start.9 = (bf16[1,384]{1,0:T(2,128)(2,1)S(1)}, bf16[1,384]{1,0:T(2,128)(2,1)S(1)}, u32[]{:S(2)}, u32[]{:S(2)}) collective-permute-start(bf16[1,384]{1,0:T(2,128)(2,1)S(1)} %bitcast.229), channel_id=1, source_target_pairs={{1,0},{2,1},{3,2},{4,3},{5,4},{6,5},{7,6},{8,7},{9,8},{10,9},{11,1... | collective-permute-start | bytes 2312 | tf_op jit(solution)/shard_map/ppermute | solution.py:22
where the time goes:
time: 692 us; the launch traced here: 691 us
  blocking collectives  453 us (65%)
  starting transfers between devices  88.1 us (13%)
  other arithmetic  65.9 us (10%)
  local copies, waits for them, and re-layouts  49.3 us (7%)
  matrix products  25.5 us (4%)
  between operations  9.27 us (1%)
    psum x1, blocking collectives, per_device(): lax.psum((jnp.sum(band_force * band_force), jnp.where(movable, jnp.sum(sp...  142 us
    psum x1, blocking collectives, per_device(): parallel = lax.psum(jnp.sum(forces * unit_tangent), 'space')  110 us
    psum x1, blocking collectives, per_device(): lax.psum((energy_part, jnp.sum(ahead_vec * ahead_vec), jnp.sum(behind * b...  102 us
    psum x1, blocking collectives, per_device(): tangent_sq = lax.psum(jnp.sum(tangent * tangent), 'space')  100 us
    ppermute x6, starting transfers between devices, with_halo(): lax.ppermute(head, axis, [((i + 1) % count, i) for i in range(ends)])  66.9 us
    scatter-add x1, other arithmetic, per_device(): jnp.zeros((3, atom_rows + 2 * ghost_rows), jnp.float32).at[:, slot_ids]  24.8 us
    scatter-add x1, other arithmetic, per_device(): grad_hidden = jnp.zeros((atom_rows + 2 * ghost_rows, channels), jnp.float...  22.7 us
    ppermute x6, starting transfers between devices, with_halo(): lax.ppermute(tail, axis, [(i, (i + 1) % count) for i in range(ends)])  21.2 us
  transfers between devices with their start and end apart: 12, of which 0 were waited for; matrix products, arithmetic and copies ran while one was open for 5% of the time, Pallas kernels for 0%

commit v1 on v0

v1 whole, which is shorter than its diff:
```python
import jax
import jax.numpy as jnp
from jax import lax
from jax.experimental import pallas as pl
from jax.experimental.pallas import tpu as pltpu
from jax.sharding import PartitionSpec as P

EPSILON = 1e-06
BASIS_WIDTH = 0.6
BASIS_REACH = 6.0
BASIS = 16
IMAGES = 16
DOMAINS = 32
ATOMS = 128
CHANNELS = 128
SLOTS = 32
PAIRS = ATOMS * SLOTS
CHUNK = 512
PER_CHUNK = CHUNK // ATOMS
CHUNKS = PAIRS // CHUNK
EXT = 3 * ATOMS
AXES = ("image", "space")
F32 = jnp.float32
BF16 = jnp.bfloat16

ROW_POS = 128
ROW_AUX = 152
ROW_NEAR = 160
PACK_ROWS = 192
HALO_ROWS = 160


def device_at(x, y, z, core):
    return ((y * 2 + z // 8) * 2 + core) * DOMAINS + x * 8 + z % 8


def home(image, domain):
    return image * DOMAINS + domain


def worker(image, domain):
    x, rest = divmod(domain, 8)
    pair, core = divmod(rest, 2)
    return device_at(x, pair if x % 2 == 0 else 3 - pair, image, core)


CELLS = [(i, d) for i in range(IMAGES) for d in range(DOMAINS)]
TO_WORKER = [(home(i, d), worker(i, d)) for i, d in CELLS]
TO_HOME = [(worker(i, d), home(i, d)) for i, d in CELLS]
SWAP_A = [(worker(i, d), worker(i, d ^ 1)) for i, d in CELLS]
SWAP_B = [(worker(i, d), worker(i, (d + 1) % DOMAINS if d % 2 else (d - 1) % DOMAINS)) for i, d in CELLS]
IMAGE_UP = [(worker(i, d), worker(i + 1, d)) for i, d in CELLS if i + 1 < IMAGES]
IMAGE_DOWN = [(worker(i + 1, d), worker(i, d)) for i, d in CELLS if i + 1 < IMAGES]
LAYERS = [[worker(i, d) for d in range(DOMAINS)] for i in range(IMAGES)]
COLUMNS = [[worker(i, d) for i in range(IMAGES)] for d in range(DOMAINS)]


def move(values, pairs):
    return lax.ppermute(values, AXES, pairs)


def place():
    image, space = lax.axis_index("image"), lax.axis_index("space")
    x, y = lax.shift_right_logical(space, 3), lax.shift_right_logical(image, 2)
    layer = ((image & 2) << 2) + (space & 7)
    pair = jnp.where((x & 1) == 0, y, 3 - y)
    return image, layer, x * 8 + pair * 2 + (image & 1)


def dot(a, b):
    return jnp.dot(a, b, preferred_element_type=F32)


def dot_nt(a, b):
    return lax.dot_general(a, b, (((1,), (1,)), ((), ())), preferred_element_type=F32)


def gate(v):
    return 0.5 * jnp.tanh(0.5 * v) + 0.5


def halves(v):
    high = v.astype(BF16)
    return high, (v - high.astype(F32)).astype(BF16)


def thirds(v):
    high = v.astype(BF16)
    rest = v - high.astype(F32)
    middle = rest.astype(BF16)
    return high, middle, (rest - middle.astype(F32)).astype(BF16)


def centres():
    step = BASIS_REACH / (BASIS - 1)
    return lax.broadcasted_iota(jnp.int32, (BASIS, CHUNK), 0).astype(F32) * step


def stacked(v):
    high, low = halves(v)
    return jnp.concatenate([high, low, high], axis=0)


def chunk(c):
    return pl.ds(c * CHUNK, CHUNK)


def fold(v):
    total = v[:, :ATOMS]
    for k in range(1, PER_CHUNK):
        total = total + v[:, k * ATOMS : (k + 1) * ATOMS]
    return total


def spread(v):
    return jnp.concatenate([v] * PER_CHUNK, axis=1)


def coords_of(block):
    b = block[ROW_POS : ROW_POS + 24].astype(F32)
    return b[0:8] + b[8:16] + b[16:24]


def pack_kernel(pos, embed, near, up, down, climb, out):
    out[0:CHANNELS, :] = embed[...].astype(F32).T.astype(BF16)
    zeros = jnp.zeros((5, ATOMS), F32)
    parts = [jnp.concatenate([p.astype(F32), zeros], axis=0) for p in thirds(pos[0])]
    level = jnp.full((1, ATOMS), climb[0].astype(F32) * (1.0 / DOMAINS), F32)
    aux = jnp.concatenate([level, up[...].astype(F32), down[...].astype(F32), zeros], axis=0)
    out[ROW_POS:ROW_NEAR, :] = jnp.concatenate(parts + [aux], axis=0).astype(BF16)
    slots = near[...].astype(F32) - float(ATOMS)
    square = jnp.concatenate([slots, jnp.zeros((ATOMS, ATOMS - SLOTS), F32)], axis=1)
    out[ROW_NEAR:PACK_ROWS, :] = square.T[:SLOTS].astype(BF16)


def weights_kernel(after, filter_in, filter_out, update, readout, in_t, out_t, update_t, read):
    for l in range(2):
        rows = pl.ds(l * 128, 128)
        high, low = halves(filter_in[l])
        filler = jnp.zeros((128 - 3 * BASIS, CHANNELS), F32)
        tall = jnp.concatenate(
            [high.astype(F32), high.astype(F32), low.astype(F32), filler], axis=0
        )
        in_t[rows, :] = tall.T.astype(BF16)
        out_t[rows, :] = filter_out[l].astype(F32).T.astype(BF16)
        update_t[rows, :] = update[l].astype(F32).T.astype(BF16)
    read[...] = jnp.broadcast_to(readout[...], (CHANNELS, ATOMS)).T


def lists_kernel(pack, list_a, list_b, send_a, send_b):
    _, _, domain = place()
    even = (domain & 1) == 0
    aux = pack[ROW_AUX : ROW_AUX + 8, :].astype(F32)
    up, down = aux[1:2], aux[2:3]
    rows = lax.broadcasted_iota(jnp.int32, (ATOMS, ATOMS), 0).astype(F32)
    block = pack[0:HALO_ROWS, :]
    for ids, chosen, send in (
        (jnp.where(even, up, down), list_a, send_a),
        (jnp.where(even, down, up), list_b, send_b),
    ):
        hot = jnp.where(rows == ids, 1.0, 0.0).astype(BF16)
        chosen[...] = hot
        send[...] = dot(block, hot).astype(BF16)


def slots_kernel(pack, hot):
    _, _, domain = place()
    even = (domain & 1) == 0
    slots = pack[ROW_NEAR:PACK_ROWS, :].astype(F32)
    swapped = jnp.where(slots < 0.0, slots, jnp.where(slots < 128.0, slots + 128.0, slots - 128.0))
    slots = jnp.where(even, swapped, slots)
    rows = lax.broadcasted_iota(jnp.int32, (EXT, ATOMS), 0).astype(F32) - float(ATOMS)
    for k in range(SLOTS):
        hot[:, k * ATOMS : (k + 1) * ATOMS] = jnp.where(rows == slots[k : k + 1], 1.0, 0.0).astype(BF16)


def first_kernel(
    pack, from_a, from_b, hot, list_a, list_b, in_t, out_t, update_t,
    hidden, send_a, send_b, update_one, pairs, rows_one,
):
    _, _, domain = place()
    shift = jnp.where(domain == 0, -DOMAINS, jnp.where(domain == DOMAINS - 1, DOMAINS, 0)).astype(F32)
    own = coords_of(pack[0:HALO_ROWS, :])
    first = lax.broadcasted_iota(jnp.int32, (8, ATOMS), 0) == 0
    far = coords_of(from_b[...]) + jnp.where(first, shift, 0.0)
    far_rows = jnp.concatenate([p.astype(F32) for p in thirds(far)], axis=0).astype(BF16)
    ext_embed = jnp.concatenate([pack[0:CHANNELS, :], from_a[0:CHANNELS, :], from_b[0:CHANNELS, :]], axis=1)
    f32_rows = lambda ref: ref[ROW_POS:HALO_ROWS, :].astype(F32)
    far_full = jnp.concatenate([far_rows.astype(F32), jnp.zeros((8, ATOMS), F32)], axis=0)
    ext_pos = jnp.concatenate([f32_rows(pack), f32_rows(from_a), far_full], axis=1).astype(BF16)
    ext = jnp.concatenate([ext_embed, ext_pos], axis=0)
    own_wide = spread(own)
    centre = centres()
    message = jnp.zeros((CHANNELS, ATOMS), F32)
    for c in range(CHUNKS):
        got = dot(ext, hot[:, chunk(c)])
        vec = got[128:136] + got[136:144] + got[144:152] - own_wide
        pairs[:, chunk(c)] = vec
        sq = jnp.sum(vec * vec, axis=0, keepdims=True)
        scaled = (sq - centre) * (1.0 / BASIS_WIDTH)
        radial = jnp.exp(-scaled * scaled)
        pre = dot(in_t[0:128, 0 : 3 * BASIS], stacked(radial))
        act = (pre * gate(pre)).astype(BF16)
        filt = dot(out_t[0:128, :], act)
        rows = got[0:CHANNELS]
        rows_one[:, chunk(c)] = rows.astype(BF16)
        message = message + fold(filt * rows)
    upd = dot(update_t[0:128, :], message.astype(BF16))
    update_one[...] = upd
    hid = (pack[0:CHANNELS, :].astype(F32) + upd * gate(upd)).astype(BF16)
    hidden[...] = hid
    send_a[...] = dot(hid, list_a[...]).astype(BF16)
    send_b[...] = dot(hid, list_b[...]).astype(BF16)


def filters_kernel(pack, pairs, in_t, out_t, slope_one, slope_two, filter_two, own):
    own[...] = coords_of(pack[0:HALO_ROWS, :])
    centre = centres()
    for c in range(CHUNKS):
        vec = pairs[:, chunk(c)]
        sq = jnp.sum(vec * vec, axis=0, keepdims=True)
        scaled = (sq - centre) * (1.0 / BASIS_WIDTH)
        radial = jnp.exp(-scaled * scaled)
        tall = stacked(radial)
        steep = stacked(radial * scaled * (-2.0 / BASIS_WIDTH))
        for l, slope in ((0, slope_one), (1, slope_two)):
            weight = in_t[l * 128 : (l + 1) * 128, 0 : 3 * BASIS]
            pre = dot(weight, tall)
            change = dot(weight, steep)
            g = gate(pre)
            act = pre * g
            slope[:, chunk(c)] = ((g + act * (1.0 - g)) * change).astype(slope.dtype)
            if l == 1:
                filter_two[:, chunk(c)] = dot(out_t[128:256, :], act.astype(BF16))


def second_kernel(
    hidden, from_a, from_b, hot, filter_two, update_t, update, read,
    energy, grad_two, rows_two, grad_own, grad_a, grad_b,
):
    ext = jnp.concatenate([hidden[...], from_a[...], from_b[...]], axis=1)
    message = jnp.zeros((CHANNELS, ATOMS), F32)
    for c in range(CHUNKS):
        rows = dot(ext, hot[:, chunk(c)])
        rows_two[:, chunk(c)] = rows.astype(BF16)
        message = message + fold(filter_two[:, chunk(c)] * rows)
    upd = dot(update_t[128:256, :], message.astype(BF16))
    g = gate(upd)
    act = upd * g
    weight = read[...]
    energy[...] = jnp.broadcast_to(jnp.sum(act * weight, axis=0, keepdims=True), (8, ATOMS))
    dupd = ((g + act * (1.0 - g)) * weight).astype(BF16)
    grad = dot(update[1], dupd)
    grad_two[...] = grad
    wide = spread(grad)
    total = jnp.zeros((CHANNELS, EXT), F32)
    for c in range(CHUNKS):
        part = (filter_two[:, chunk(c)] * wide).astype(BF16)
        total = total + dot_nt(part, hot[:, chunk(c)])
    grad_own[...] = total[:, 0:ATOMS]
    grad_a[...] = total[:, ATOMS : 2 * ATOMS].astype(BF16)
    grad_b[...] = total[:, 2 * ATOMS :].astype(BF16)


def slope_kernel(grad_two, rows_two, slope_two, filter_out, out):
    wide = spread(grad_two[...])
    for c in range(CHUNKS):
        dfilt = (wide * rows_two[:, chunk(c)].astype(F32)).astype(BF16)
        dact = dot(filter_out[1], dfilt)
        part = jnp.sum(dact * slope_two[:, chunk(c)].astype(F32), axis=0, keepdims=True)
        out[:, chunk(c)] = jnp.broadcast_to(part, (8, CHUNK))


def third_kernel(
    grad_own, from_a, from_b, list_a, list_b, update_one, update, rows_one, slope_one,
    filter_out, dsq_two, pairs, hot,
    force, send_a, send_b,
):
    dhidden = grad_own[...] + dot_nt(from_a[...], list_a[...]) + dot_nt(from_b[...], list_b[...])
    upd = update_one[...]
    g = gate(upd)
    dupd = (dhidden * (g + upd * g * (1.0 - g))).astype(BF16)
    wide = spread(dot(update[0], dupd))
    own = jnp.zeros((8, ATOMS), F32)
    total = jnp.zeros((16, EXT), F32)
    for c in range(CHUNKS):
        dfilt = (wide * rows_one[:, chunk(c)].astype(F32)).astype(BF16)
        dact = dot(filter_out[0], dfilt)
        part = jnp.sum(dact * slope_one[:, chunk(c)].astype(F32), axis=0, keepdims=True)
        pull = 2.0 * (part + dsq_two[:, chunk(c)]) * pairs[:, chunk(c)]
        own = own + fold(pull)
        high, low = halves(pull)
        both = jnp.concatenate([high.astype(F32), low.astype(F32)], axis=0).astype(BF16)
        total = total + dot_nt(both, hot[:, chunk(c)])
    ext = total[0:8] + total[8:16]
    force[...] = own - ext[:, 0:ATOMS]
    send_a[...] = -ext[:, ATOMS : 2 * ATOMS]
    send_b[...] = -ext[:, 2 * ATOMS :]


def sums_kernel(force, from_a, from_b, list_a, list_b, own, prev, following, energy, pack, velocity, back, vec):
    image, _, _ = place()

    def returned(block, chosen):
        both = jnp.concatenate([p.astype(F32) for p in halves(block)], axis=0).astype(BF16)
        got = dot_nt(both, chosen)
        return got[0:8] + got[8:16]

    f = force[...] + returned(from_a[...], list_a[...]) + returned(from_b[...], list_b[...])
    ahead = following[...] - own[...]
    behind = own[...] - prev[...]
    back[0:8, :] = f
    back[8:16, :] = ahead
    back[16:24, :] = behind
    speed = velocity[0]
    movable = (image > 0) & (image < IMAGES - 1)
    down = lambda v: jnp.sum(v, axis=0, keepdims=True)
    level = pack[ROW_AUX : ROW_AUX + 8, :].astype(F32)[0:1] * (1.0 / ATOMS)
    rows = (
        energy[0:1, :],
        down(ahead * ahead),
        down(behind * behind),
        down(ahead * behind),
        down(f * ahead),
        down(f * behind),
        down(f * f),
        jnp.where(movable, down(speed * speed), 0.0),
        level,
    )
    lane = lax.broadcasted_iota(jnp.int32, (1, ATOMS), 1)
    total = jnp.zeros((1, ATOMS), F32)
    for j, row in enumerate(rows):
        total = jnp.where(lane == j, jnp.sum(row, axis=1, keepdims=True), total)
    vec[...] = jnp.broadcast_to(total, (DOMAINS, ATOMS))


def layer_kernel(parts, out):
    out[...] = jnp.broadcast_to(jnp.sum(parts[...], axis=0, keepdims=True), (IMAGES, ATOMS))


def final_kernel(table, back, pos, velocity, reset, spring, time_step, mixing, new_pos, new_speed, energy):
    image, _, _ = place()
    t = table[...]
    e, a, b, ab, fa, fb, ff, vv, level = (t[:, j : j + 1] for j in range(9))
    ahead_norm = jnp.sqrt(a + EPSILON)
    behind_norm = jnp.sqrt(b + EPSILON)
    tangent_sq = jnp.maximum(
        a / (ahead_norm * ahead_norm)
        + b / (behind_norm * behind_norm)
        + 2.0 * ab / (ahead_norm * behind_norm),
        0.0,
    )
    length = jnp.sqrt(tangent_sq + EPSILON)
    unit_sq = tangent_sq / (tangent_sq + EPSILON)
    parallel = (fa / ahead_norm + fb / behind_norm) / length
    tension = spring[0] * (ahead_norm - behind_norm)
    along = jnp.where(level > 0.5, -2.0 * parallel, tension - parallel)
    band_sq = ff + 2.0 * along * parallel + along * along * unit_sq
    row = lax.broadcasted_iota(jnp.int32, (IMAGES, 1), 0)
    inner = (row > 0) & (row < IMAGES - 1)
    down = lambda v: jnp.sum(v, axis=0, keepdims=True)
    force_norm = jnp.sqrt(down(jnp.where(inner, jnp.maximum(band_sq, 0.0), 0.0)) + EPSILON)
    speed_norm = jnp.sqrt(down(vv) + EPSILON)
    mine = row == image
    pick = lambda v: down(jnp.where(mine, v, 0.0))
    shape = (3, ATOMS)
    wide = lambda v: jnp.broadcast_to(jnp.broadcast_to(v, (1, ATOMS)), shape)
    energy[0] = jnp.sum(jnp.where(mine, e, 0.0))
    tangent = back[8:11, :] / wide(pick(ahead_norm)) + back[16:19, :] / wide(pick(behind_norm))
    band = back[0:3, :] + wide(pick(along / length)) * tangent
    speed = velocity[0]
    mix = mixing[0]
    mixed = (1.0 - mix) * speed + wide(mix * speed_norm / force_norm) * band
    kept = jnp.where(reset[0] > 0, 0.0, mixed)
    movable = (image > 0) & (image < IMAGES - 1)
    speed = jnp.where(movable, kept + time_step[0] * band, 0.0)
    new_speed[0] = speed
    new_pos[0] = pos[0] + time_step[0] * speed


VMEM = pl.BlockSpec(memory_space=pltpu.VMEM)
SMEM = pl.BlockSpec(memory_space=pltpu.SMEM)


def call(kernel, outs, args, scalars=(), scalar_outs=(), flops=0, limit=16 << 20):
    specs = [SMEM if i in scalars else VMEM for i in range(len(args))]
    moved = sum(a.size * a.dtype.itemsize for a in args)
    return pl.pallas_call(
        kernel,
        out_shape=[jax.ShapeDtypeStruct(s, t) for s, t in outs],
        in_specs=specs,
        out_specs=[SMEM if i in scalar_outs else VMEM for i in range(len(outs))],
        compiler_params=pltpu.CompilerParams(vmem_limit_bytes=limit),
        cost_estimate=pl.CostEstimate(flops=flops, bytes_accessed=moved, transcendentals=0),
        name=kernel.__name__,
    )(*args)


def per_device(
    positions, velocity, embed, neighbours, send_up, send_down, climb, reset,
    filter_in, filter_out, update_weight, readout, spring, time_step, mixing,
):
    square = (ATOMS, ATOMS)
    wide = (CHANNELS, PAIRS)
    (packed,) = call(
        pack_kernel,
        [((PACK_ROWS, ATOMS), BF16)],
        (positions, embed, neighbours, send_up.reshape(1, ATOMS), send_down.reshape(1, ATOMS), climb),
        scalars=(5,),
    )
    pack = move(packed, TO_WORKER)
    in_t, out_t, update_t, read = call(
        weights_kernel,
        [((256, 128), BF16), ((256, 128), BF16), ((256, 128), BF16), (square, F32)],
        (packed, filter_in, filter_out, update_weight, readout.reshape(1, CHANNELS)),
        flops=10**8,
    )
    list_a, list_b, send_a, send_b = call(
        lists_kernel,
        [(square, BF16), (square, BF16), ((HALO_ROWS, ATOMS), BF16), ((HALO_ROWS, ATOMS), BF16)],
        (pack,),
    )
    from_a, from_b = move(send_a, SWAP_A), move(send_b, SWAP_B)
    (hot,) = call(slots_kernel, [((EXT, PAIRS), BF16)], (pack,), flops=10**9)
    hidden, send_a, send_b, update_one, pairs, rows_one = call(
        first_kernel,
        [(square, BF16), (square, BF16), (square, BF16), (square, F32), ((8, PAIRS), F32), (wide, BF16)],
        (pack, from_a, from_b, hot, list_a, list_b, in_t, out_t, update_t),
        flops=10**9,
    )
    from_a, from_b = move(send_a, SWAP_A), move(send_b, SWAP_B)
    slope_one, slope_two, filter_two, own = call(
        filters_kernel,
        [(wide, BF16), (wide, BF16), (wide, F32), ((8, ATOMS), F32)],
        (pack, pairs, in_t, out_t),
        flops=10**9,
    )
    energy, grad_two, rows_two, grad_own, send_a, send_b = call(
        second_kernel,
        [((8, ATOMS), F32), (square, F32), (wide, BF16), (square, F32), (square, BF16), (square, BF16)],
        (hidden, from_a, from_b, hot, filter_two, update_t, update_weight, read),
        flops=10**9,
    )
    from_a, from_b = move(send_a, SWAP_A), move(send_b, SWAP_B)
    prev, following = move(own, IMAGE_UP), move(own, IMAGE_DOWN)
    (dsq_two,) = call(
        slope_kernel,
        [((8, PAIRS), F32)],
        (grad_two, rows_two, slope_two, filter_out),
        flops=10**9,
    )
    force, send_a, send_b = call(
        third_kernel,
        [((8, ATOMS), F32)] * 3,
        (
            grad_own, from_a, from_b, list_a, list_b, update_one, update_weight, rows_one,
            slope_one, filter_out, dsq_two, pairs, hot,
        ),
        flops=10**9,
    )
    from_a, from_b = move(send_a, SWAP_A), move(send_b, SWAP_B)
    back, vec = call(
        sums_kernel,
        [((24, ATOMS), F32), ((DOMAINS, ATOMS), F32)],
        (force, from_a, from_b, list_a, list_b, own, prev, following, energy, pack, velocity),
    )
    back = move(back, TO_HOME)
    parts = lax.all_to_all(vec, AXES, 0, 0, tiled=True, axis_index_groups=LAYERS)
    (layer,) = call(layer_kernel, [((IMAGES, ATOMS), F32)], (parts,))
    table = lax.all_to_all(layer, AXES, 0, 0, tiled=True, axis_index_groups=COLUMNS)
    new_pos, new_speed, energies = call(
        final_kernel,
        [((1, 3, ATOMS), F32), ((1, 3, ATOMS), F32), ((1,), F32)],
        (
            table, back, positions, velocity, reset,
            spring.reshape(1), time_step.reshape(1), mixing.reshape(1),
        ),
        scalars=(4, 5, 6, 7),
        scalar_outs=(2,),
    )
    return new_pos, new_speed, energies


def solution(mesh):
    placed = (
        P("image", None, "space"),
        P("image", None, "space"),
        P("space", None),
        P("space", None),
        P("space"),
        P("space"),
        P("image"),
        P("image"),
    ) + (P(),) * 7
    return jax.shard_map(
        per_device,
        mesh=mesh,
        in_specs=placed,
        out_specs=(P("image", None, "space"), P("image", None, "space"), P("image")),
        check_vma=False,
    )
```

time: 692 us -> 113 us (0.16)
  the two profiles are of different devices: /device:TPU:1 before, /device:TPU:16 now
where the time goes in v1:
time: 113 us; the launch traced here: 112 us
  starting transfers between devices  61.4 us (54%)
  Pallas kernels  14.8 us (13%)
  blocking collectives  13.7 us (12%)
  waiting for transfers between devices  10.4 us (9%)
  local copies, waits for them, and re-layouts  7.75 us (7%)
  between operations  4.16 us (4%)
    ppermute x12, starting transfers between devices, move(): return lax.ppermute(values, AXES, pairs)  49.6 us
    pallas_call x12, Pallas kernels, call(): pl.pallas_call(kernel, out_shape=[jax.ShapeDtypeStruct(s, t) for s, t in...  14.8 us
    all_to_all x1, blocking collectives, per_device(): lax.all_to_all(vec, AXES, 0, 0, tiled=True, axis_index_groups=LAYERS)  13.7 us
    all_to_all x1, starting transfers between devices, per_device(): lax.all_to_all(layer, AXES, 0, 0, tiled=True, axis_index_groups=COLUMNS)  11.8 us
    ppermute x12, waiting for transfers between devices, move(): return lax.ppermute(values, AXES, pairs)  10.4 us
    unnamed x23, local copies, waits for them, and re-layouts  6.62 us
  transfers between devices with their start and end apart: 13, of which 4 were waited for; matrix products, arithmetic and copies ran while one was open for 0% of the time, Pallas kernels for 8%

profile of v1, /device:TPU:16, one launch (start us, length us, event | category | flops | bytes accessed | tf_op | source)
XLA Modules:
  0.0 112.2 jit_solution(11749835768660392940)
XLA Ops:
  0.6 0.7 copy.25.pos
  1.3 0.8 copy.26.near
  2.8 0.0 copy-start.4
  2.8 0.7 copy-done.4
  3.5 0.7 copy-done.5
  4.2 0.7 copy-done.6
  4.9 0.1 pack_kernel.1.after
  5.0 15.5 %collective-permute-start = (bf16[192,128]{1,0:T(8,128)(2,1)S(1)}, bf16[192,128]{1,0:T(8,128)(2,1)S(1)}, u32[]{:S(2)}, u32[]{:S(2)}) collective-permute-start(bf16[192,128]{1,0:T(8,128)(2,1)S(1)} %pack_kernel.1.after), channel_id=1, source_target_pairs={{0,0},{1,32},{2,128},{3,160},{4,256},{5,288},{6,384},{7,416},{8,39... | collective-permute-start | bytes 147464 | tf_op jit(solution)/shard_map/ppermute | solution.py:59
  20.5 0.0 copy-start
  20.5 0.8 copy-done
  21.3 0.8 copy-done.2
  22.1 0.7 copy-done.7
  22.9 0.7 copy-done.8
  23.5 0.1 weights_kernel.1
  23.7 0.0 collective-permute-done.pack
  23.7 0.2 lists_kernel.1
  23.8 1.9 %collective-permute-start.1 = (bf16[160,128]{1,0:T(8,128)(2,1)S(1)}, bf16[160,128]{1,0:T(8,128)(2,1)S(1)}, u32[]{:S(2)}, u32[]{:S(2)}) collective-permute-start(bf16[160,128]{1,0:T(8,128)(2,1)S(1)} %get-tuple-element.32), channel_id=1, source_target_pairs={{0,32},{32,0},{128,160},{160,128},{256,288},{288,256},{384,416},{4... | collective-permute-start | bytes 122888 | tf_op jit(solution)/shard_map/ppermute | solution.py:59
  25.8 1.9 %collective-permute-start.2 = (bf16[160,128]{1,0:T(8,128)(2,1)S(1)}, bf16[160,128]{1,0:T(8,128)(2,1)S(1)}, u32[]{:S(2)}, u32[]{:S(2)}) collective-permute-start(bf16[160,128]{1,0:T(8,128)(2,1)S(1)} %get-tuple-element.33), channel_id=1, source_target_pairs={{0,56},{32,128},{128,32},{160,256},{256,160},{288,384},{384,288},{... | collective-permute-start | bytes 122888 | tf_op jit(solution)/shard_map/ppermute | solution.py:59
  27.7 1.0 slots_kernel.1.hot
  28.7 0.0 collective-permute-done.1.from_a
  28.7 2.4 %collective-permute-done.2.from_b = bf16[160,128]{1,0:T(8,128)(2,1)S(1)} collective-permute-done((bf16[160,128]{1,0:T(8,128)(2,1)S(1)}, bf16[160,128]{1,0:T(8,128)(2,1)S(1)}, u32[]{:S(2)}, u32[]{:S(2)}) %collective-permute-start.2) | collective-permute-done | bytes 40992 | tf_op jit(solution)/shard_map/ppermute | solution.py:59
  31.1 4.1 %first_kernel.1 = (bf16[128,128]{1,0:T(8,128)(2,1)S(1)}, bf16[128,128]{1,0:T(8,128)(2,1)S(1)}, bf16[128,128]{1,0:T(8,128)(2,1)S(1)}, f32[128,128]{1,0:T(8,128)S(...) custom-call(bf16[192,128]{1,0:T(8,128)(2,1)S(1)} %collective-permute-done.pack, ...), custom_call_target="tpu_custom_call" | custom-call | flops 1000000000 | bytes 3538944 | tf_op jit(solution)/shard_map/first_kernel/pallas_call | solution.py:388
  35.2 2.4 %collective-permute-start.3 = (bf16[128,128]{1,0:T(8,128)(2,1)S(1)}, bf16[128,128]{1,0:T(8,128)(2,1)S(1)}, u32[]{:S(2)}, u32[]{:S(2)}) collective-permute-start(bf16[128,128]{1,0:T(8,128)(2,1)S(1)} %get-tuple-element.40), channel_id=1, source_target_pairs={{0,32},{32,0},{128,160},{160,128},{256,288},{288,256},{384,416},{4... | collective-permute-start | bytes 98312 | tf_op jit(solution)/shard_map/ppermute | solution.py:59
  37.6 1.9 %collective-permute-start.4 = (bf16[128,128]{1,0:T(8,128)(2,1)S(1)}, bf16[128,128]{1,0:T(8,128)(2,1)S(1)}, u32[]{:S(2)}, u32[]{:S(2)}) collective-permute-start(bf16[128,128]{1,0:T(8,128)(2,1)S(1)} %get-tuple-element.41), channel_id=1, source_target_pairs={{0,56},{32,128},{128,32},{160,256},{256,160},{288,384},{384,288},{... | collective-permute-start | bytes 98312 | tf_op jit(solution)/shard_map/ppermute | solution.py:59
  39.5 2.7 %filters_kernel.1 = (bf16[128,4096]{1,0:T(8,128)(2,1)S(1)}, bf16[128,4096]{1,0:T(8,128)(2,1)S(1)}, f32[128,4096]{1,0:T(8,128)S(1)}, f32[8,128]{1,0:T(8,128)S(1)}) custom-call(bf16[192,128]{1,0:T(8,128)(2,1)S(1)} %collective-permute-done.pack, f32[8,4096]{1,0:T(8,128)S(1)} %get-tuple-element.42.pairs, bf16[256,128]{1,0:T(8,128)(2,1)S(1)} %get-tuple-element.36.in_t, ...), custom_call_target="tpu_custom_call" | custom-call | flops 1000000000 | bytes 311296 | tf_op jit(solution)/shard_map/filters_kernel/pallas_call | solution.py:388
  42.3 0.0 copy-start.3
  42.3 1.4 %collective-permute-start.10 = (f32[8,128]{1,0:T(8,128)S(1)}, f32[8,128]{1,0:T(8,128)S(1)}, u32[]{:S(2)}, u32[]{:S(2)}) collective-permute-start(f32[8,128]{1,0:T(8,128)S(1)} %get-tuple-element.57.own), channel_id=1, source_target_pairs={{1,0},{33,32},{129,128},{161,160},{257,256},{289,288},{385,384},{4... | collective-permute-start | bytes 12296 | tf_op jit(solution)/shard_map/ppermute | solution.py:59
  43.7 4.5 %collective-permute-start.9 = (f32[8,128]{1,0:T(8,128)S(1)}, f32[8,128]{1,0:T(8,128)S(1)}, u32[]{:S(2)}, u32[]{:S(2)}) collective-permute-start(f32[8,128]{1,0:T(8,128)S(1)} %get-tuple-element.57.own), channel_id=1, source_target_pairs={{0,1},{32,33},{128,129},{160,161},{256,257},{288,289},{384,385},{4... | collective-permute-start | bytes 12296 | tf_op jit(solution)/shard_map/ppermute | solution.py:59
  48.3 0.0 collective-permute-done.4.from_b
  48.3 2.1 %second_kernel.1 = (f32[8,128]{1,0:T(8,128)S(1)}, f32[128,128]{1,0:T(8,128)S(1)}, bf16[128,4096]{1,0:T(8,128)(2,1)S(1)}, f32[128,128]{1,0:T(8,128)S(1)}, bf16[12...) custom-call(bf16[128,128]{1,0:T(8,128)(2,1)S(1)} %get-tuple-element.39.hidden, ...), custom_call_target="tpu_custom_call" | custom-call | flops 1000000000 | bytes 5537792 | tf_op jit(solution)/shard_map/second_kernel/pallas_call | solution.py:388
  50.4 1.9 %collective-permute-start.5 = (bf16[128,128]{1,0:T(8,128)(2,1)S(1)}, bf16[128,128]{1,0:T(8,128)(2,1)S(1)}, u32[]{:S(2)}, u32[]{:S(2)}) collective-permute-start(bf16[128,128]{1,0:T(8,128)(2,1)S(1)} %get-tuple-element.46), channel_id=1, source_target_pairs={{0,32},{32,0},{128,160},{160,128},{256,288},{288,256},{384,416},{4... | collective-permute-start | bytes 98312 | tf_op jit(solution)/shard_map/ppermute | solution.py:59
  52.3 3.1 %collective-permute-start.6 = (bf16[128,128]{1,0:T(8,128)(2,1)S(1)}, bf16[128,128]{1,0:T(8,128)(2,1)S(1)}, u32[]{:S(2)}, u32[]{:S(2)}) collective-permute-start(bf16[128,128]{1,0:T(8,128)(2,1)S(1)} %get-tuple-element.47), channel_id=1, source_target_pairs={{0,56},{32,128},{128,32},{160,256},{256,160},{288,384},{384,288},{... | collective-permute-start | bytes 98312 | tf_op jit(solution)/shard_map/ppermute | solution.py:59
  55.4 0.5 slope_kernel.1.dsq_two
  55.9 0.0 copy-start.9
  55.9 1.6 %collective-permute-done.6.from_b = bf16[128,128]{1,0:T(8,128)(2,1)S(1)} collective-permute-done((bf16[128,128]{1,0:T(8,128)(2,1)S(1)}, bf16[128,128]{1,0:T(8,128)(2,1)S(1)}, u32[]{:S(2)}, u32[]{:S(2)}) %collective-permute-start.6) | collective-permute-done | bytes 32800 | tf_op jit(solution)/shard_map/ppermute | solution.py:59
  57.5 2.1 %third_kernel.1 = (f32[8,128]{1,0:T(8,128)S(1)}, f32[8,128]{1,0:T(8,128)S(1)}, f32[8,128]{1,0:T(8,128)S(1)}) custom-call(f32[128,128]{1,0:T(8,128)S(1)} %get-tuple-element.45.grad_own, bf16[128,128]{1,0:T(8,128)(2,1)S(1)} %collective-permute-done.5.from_a, bf16[128,128]{1,0:T(8,128)(2,1)S(1)} %collective-permute-done.6.from_b, ...), custom_call_target="tpu_custom_call" | custom-call | flops 1000000000 | bytes 5898240 | tf_op jit(solution)/shard_map/third_kernel/pallas_call | solution.py:388
  59.6 2.4 %collective-permute-start.7 = (f32[8,128]{1,0:T(8,128)S(1)}, f32[8,128]{1,0:T(8,128)S(1)}, u32[]{:S(2)}, u32[]{:S(2)}) collective-permute-start(f32[8,128]{1,0:T(8,128)S(1)} %get-tuple-element.55), channel_id=1, source_target_pairs={{0,32},{32,0},{128,160},{160,128},{256,288},{288,256},{384,416},{4... | collective-permute-start | bytes 12296 | tf_op jit(solution)/shard_map/ppermute | solution.py:59
  62.0 3.1 %collective-permute-start.8 = (f32[8,128]{1,0:T(8,128)S(1)}, f32[8,128]{1,0:T(8,128)S(1)}, u32[]{:S(2)}, u32[]{:S(2)}) collective-permute-start(f32[8,128]{1,0:T(8,128)S(1)} %get-tuple-element.56), channel_id=1, source_target_pairs={{0,56},{32,128},{128,32},{160,256},{256,160},{288,384},{384,288},{... | collective-permute-start | bytes 12296 | tf_op jit(solution)/shard_map/ppermute | solution.py:59
  65.2 1.8 %collective-permute-done.8.from_b = f32[8,128]{1,0:T(8,128)S(1)} collective-permute-done((f32[8,128]{1,0:T(8,128)S(1)}, f32[8,128]{1,0:T(8,128)S(1)}, u32[]{:S(2)}, u32[]{:S(2)}) %collective-permute-start.8) | collective-permute-done | bytes 4128 | tf_op jit(solution)/shard_map/ppermute | solution.py:59
  67.0 0.2 sums_kernel.1
  67.2 13.7 %all_to_all.22 = f32[32,1,128]{2,1,0:T(1,128)S(1)} all-to-all(f32[32,1,128]{2,1,0:T(1,128)S(1)} %bitcast.19), channel_id=1, replica_groups={{0,32,128,160,256,288,384,416,392,424,264,296,136,168,8,40,16,48,144,17..., dimensions={0} | all-to-all | bytes 32768 | tf_op jit(solution)/shard_map/all_to_all | solution.py:468
  80.9 0.6 layer_kernel.1
  81.5 11.8 %all-to-all-start.1 = ((f32[16,1,128]{2,1,0:T(1,128)}), f32[16,1,128]{2,1,0:T(1,128)S(1)}, u32[]{:S(2)}, u32[]{:S(2)}) async-start(f32[16,1,128]{2,1,0:T(1,128)} %bitcast.7), calls=%async_computation.1 | async-start | bytes 16384 | tf_op jit(solution)/shard_map/all_to_all | solution.py:470
  93.2 9.5 %collective-permute-start.11 = (f32[24,128]{1,0:T(8,128)S(1)}, f32[24,128]{1,0:T(8,128)S(1)}, u32[]{:S(2)}, u32[]{:S(2)}) collective-permute-start(f32[24,128]{1,0:T(8,128)S(1)} %get-tuple-element.60), channel_id=1, source_target_pairs={{0,0},{32,1},{128,2},{160,3},{256,4},{288,5},{384,6},{416,7},{392,... | collective-permute-start | bytes 36872 | tf_op jit(solution)/shard_map/ppermute | solution.py:59
  105.4 4.6 %collective-permute-done.11.back = f32[24,128]{1,0:T(8,128)S(1)} collective-permute-done((f32[24,128]{1,0:T(8,128)S(1)}, f32[24,128]{1,0:T(8,128)S(1)}, u32[]{:S(2)}, u32[]{:S(2)}) %collective-permute-start.11) | collective-permute-done | bytes 12320 | tf_op jit(solution)/shard_map/ppermute | solution.py:59
  109.9 1.1 final_kernel.1
  111.1 0.6 copy.32
  111.6 0.6 copy.33
  (16 shorter events, 0.0 us)
Async XLA Ops:
  2.8 0.8 copy-start.4
  3.5 0.7 copy-start.5
  4.2 0.7 copy-start.6
  5.0 18.7 %collective-permute-start = (bf16[192,128]{1,0:T(8,128)(2,1)S(1)}, bf16[192,128]{1,0:T(8,128)(2,1)S(1)}, u32[]{:S(2)}, u32[]{:S(2)}) collective-permute-start(bf16[192,128]{1,0:T(8,128)(2,1)S(1)} %pack_kernel.1.after), channel_id=1, source_target_pairs={{0,0},{1,32},{2,128},{3,160},{4,256},{5,288},{6,384},{7,416},{8,39... | collective-permute-start | bytes 147464 | tf_op jit(solution)/shard_map/ppermute | solution.py:59
  20.5 0.8 copy-start
  21.3 0.8 copy-start.2
  22.1 0.7 copy-start.7
  22.9 0.7 copy-start.8
  23.8 4.8 %collective-permute-start.1 = (bf16[160,128]{1,0:T(8,128)(2,1)S(1)}, bf16[160,128]{1,0:T(8,128)(2,1)S(1)}, u32[]{:S(2)}, u32[]{:S(2)}) collective-permute-start(bf16[160,128]{1,0:T(8,128)(2,1)S(1)} %get-tuple-element.32), channel_id=1, source_target_pairs={{0,32},{32,0},{128,160},{160,128},{256,288},{288,256},{384,416},{4... | collective-permute-start | bytes 122888 | tf_op jit(solution)/shard_map/ppermute | solution.py:59
  25.8 5.3 %collective-permute-start.2 = (bf16[160,128]{1,0:T(8,128)(2,1)S(1)}, bf16[160,128]{1,0:T(8,128)(2,1)S(1)}, u32[]{:S(2)}, u32[]{:S(2)}) collective-permute-start(bf16[160,128]{1,0:T(8,128)(2,1)S(1)} %get-tuple-element.33), channel_id=1, source_target_pairs={{0,56},{32,128},{128,32},{160,256},{256,160},{288,384},{384,288},{... | collective-permute-start | bytes 122888 | tf_op jit(solution)/shard_map/ppermute | solution.py:59
  31.1 17.2 %copy-start.1 = (bf16[2,128,128]{2,1,0:T(8,128)(2,1)S(1)}, bf16[2,128,128]{2,1,0:T(8,128)(2,1)}, u32[]{:S(2)}) copy-start(bf16[2,128,128]{2,1,0:T(8,128)(2,1)} %update.5) | copy-start | bytes 196612
  35.2 13.1 %collective-permute-start.3 = (bf16[128,128]{1,0:T(8,128)(2,1)S(1)}, bf16[128,128]{1,0:T(8,128)(2,1)S(1)}, u32[]{:S(2)}, u32[]{:S(2)}) collective-permute-start(bf16[128,128]{1,0:T(8,128)(2,1)S(1)} %get-tuple-element.40), channel_id=1, source_target_pairs={{0,32},{32,0},{128,160},{160,128},{256,288},{288,256},{384,416},{4... | collective-permute-start | bytes 98312 | tf_op jit(solution)/shard_map/ppermute | solution.py:59
  37.6 10.7 %collective-permute-start.4 = (bf16[128,128]{1,0:T(8,128)(2,1)S(1)}, bf16[128,128]{1,0:T(8,128)(2,1)S(1)}, u32[]{:S(2)}, u32[]{:S(2)}) collective-permute-start(bf16[128,128]{1,0:T(8,128)(2,1)S(1)} %get-tuple-element.41), channel_id=1, source_target_pairs={{0,56},{32,128},{128,32},{160,256},{256,160},{288,384},{384,288},{... | collective-permute-start | bytes 98312 | tf_op jit(solution)/shard_map/ppermute | solution.py:59
  42.3 13.1 %copy-start.3 = (bf16[2,128,128]{2,1,0:T(8,128)(2,1)S(1)}, bf16[2,128,128]{2,1,0:T(8,128)(2,1)}, u32[]{:S(2)}) copy-start(bf16[2,128,128]{2,1,0:T(8,128)(2,1)} %filter_out.5) | copy-start | bytes 196612
  42.3 22.9 %collective-permute-start.10 = (f32[8,128]{1,0:T(8,128)S(1)}, f32[8,128]{1,0:T(8,128)S(1)}, u32[]{:S(2)}, u32[]{:S(2)}) collective-permute-start(f32[8,128]{1,0:T(8,128)S(1)} %get-tuple-element.57.own), channel_id=1, source_target_pairs={{1,0},{33,32},{129,128},{161,160},{257,256},{289,288},{385,384},{4... | collective-permute-start | bytes 12296 | tf_op jit(solution)/shard_map/ppermute | solution.py:59
  43.7 21.4 %collective-permute-start.9 = (f32[8,128]{1,0:T(8,128)S(1)}, f32[8,128]{1,0:T(8,128)S(1)}, u32[]{:S(2)}, u32[]{:S(2)}) collective-permute-start(f32[8,128]{1,0:T(8,128)S(1)} %get-tuple-element.57.own), channel_id=1, source_target_pairs={{0,1},{32,33},{128,129},{160,161},{256,257},{288,289},{384,385},{4... | collective-permute-start | bytes 12296 | tf_op jit(solution)/shard_map/ppermute | solution.py:59
  50.4 5.5 %collective-permute-start.5 = (bf16[128,128]{1,0:T(8,128)(2,1)S(1)}, bf16[128,128]{1,0:T(8,128)(2,1)S(1)}, u32[]{:S(2)}, u32[]{:S(2)}) collective-permute-start(bf16[128,128]{1,0:T(8,128)(2,1)S(1)} %get-tuple-element.46), channel_id=1, source_target_pairs={{0,32},{32,0},{128,160},{160,128},{256,288},{288,256},{384,416},{4... | collective-permute-start | bytes 98312 | tf_op jit(solution)/shard_map/ppermute | solution.py:59
  52.3 5.2 %collective-permute-start.6 = (bf16[128,128]{1,0:T(8,128)(2,1)S(1)}, bf16[128,128]{1,0:T(8,128)(2,1)S(1)}, u32[]{:S(2)}, u32[]{:S(2)}) collective-permute-start(bf16[128,128]{1,0:T(8,128)(2,1)S(1)} %get-tuple-element.47), channel_id=1, source_target_pairs={{0,56},{32,128},{128,32},{160,256},{256,160},{288,384},{384,288},{... | collective-permute-start | bytes 98312 | tf_op jit(solution)/shard_map/ppermute | solution.py:59
  55.9 9.2 %copy-start.9 = (f32[1,3,128]{2,0,1:T(1,128)S(1)}, f32[1,3,128]{2,0,1:T(1,128)}, u32[]{:S(2)}) copy-start(f32[1,3,128]{2,0,1:T(1,128)} %param.16) | copy-start | bytes 4612
  59.6 5.5 %collective-permute-start.7 = (f32[8,128]{1,0:T(8,128)S(1)}, f32[8,128]{1,0:T(8,128)S(1)}, u32[]{:S(2)}, u32[]{:S(2)}) collective-permute-start(f32[8,128]{1,0:T(8,128)S(1)} %get-tuple-element.55), channel_id=1, source_target_pairs={{0,32},{32,0},{128,160},{160,128},{256,288},{288,256},{384,416},{4... | collective-permute-start | bytes 12296 | tf_op jit(solution)/shard_map/ppermute | solution.py:59
  62.0 4.9 %collective-permute-start.8 = (f32[8,128]{1,0:T(8,128)S(1)}, f32[8,128]{1,0:T(8,128)S(1)}, u32[]{:S(2)}, u32[]{:S(2)}) collective-permute-start(f32[8,128]{1,0:T(8,128)S(1)} %get-tuple-element.56), channel_id=1, source_target_pairs={{0,56},{32,128},{128,32},{160,256},{256,160},{288,384},{384,288},{... | collective-permute-start | bytes 12296 | tf_op jit(solution)/shard_map/ppermute | solution.py:59
  81.5 28.5 %all-to-all-start.1 = ((f32[16,1,128]{2,1,0:T(1,128)}), f32[16,1,128]{2,1,0:T(1,128)S(1)}, u32[]{:S(2)}, u32[]{:S(2)}) async-start(f32[16,1,128]{2,1,0:T(1,128)} %bitcast.7), calls=%async_computation.1 | async-start | bytes 16384 | tf_op jit(solution)/shard_map/all_to_all | solution.py:470
  93.2 16.7 %collective-permute-start.11 = (f32[24,128]{1,0:T(8,128)S(1)}, f32[24,128]{1,0:T(8,128)S(1)}, u32[]{:S(2)}, u32[]{:S(2)}) collective-permute-start(f32[24,128]{1,0:T(8,128)S(1)} %get-tuple-element.60), channel_id=1, source_target_pairs={{0,0},{32,1},{128,2},{160,3},{256,4},{288,5},{384,6},{416,7},{392,... | collective-permute-start | bytes 36872 | tf_op jit(solution)/shard_map/ppermute | solution.py:59

commit v2 on v1

--- a/solution.py
+++ b/solution.py
@@ -28,6 +28,7 @@
 ROW_NEAR = 160
 PACK_ROWS = 192
 HALO_ROWS = 160
+BLOCK = 5
 
 
 def device_at(x, y, z, core):
@@ -41,16 +42,14 @@
 def worker(image, domain):
     x, rest = divmod(domain, 8)
     pair, core = divmod(rest, 2)
-    return device_at(x, pair if x % 2 == 0 else 3 - pair, image, core)
+    y, half, side = image // 4, image // 2 % 2, image % 2
+    return device_at(x, pair if x % 2 else 3 - pair, half * 8 + y * 2 + side, core)
 
 
 CELLS = [(i, d) for i in range(IMAGES) for d in range(DOMAINS)]
 TO_WORKER = [(home(i, d), worker(i, d)) for i, d in CELLS]
-TO_HOME = [(worker(i, d), home(i, d)) for i, d in CELLS]
 SWAP_A = [(worker(i, d), worker(i, d ^ 1)) for i, d in CELLS]
 SWAP_B = [(worker(i, d), worker(i, (d + 1) % DOMAINS if d % 2 else (d - 1) % DOMAINS)) for i, d in CELLS]
-IMAGE_UP = [(worker(i, d), worker(i + 1, d)) for i, d in CELLS if i + 1 < IMAGES]
-IMAGE_DOWN = [(worker(i + 1, d), worker(i, d)) for i, d in CELLS if i + 1 < IMAGES]
 LAYERS = [[worker(i, d) for d in range(DOMAINS)] for i in range(IMAGES)]
 COLUMNS = [[worker(i, d) for i in range(IMAGES)] for d in range(DOMAINS)]
 
@@ -62,9 +61,8 @@
 def place():
     image, space = lax.axis_index("image"), lax.axis_index("space")
     x, y = lax.shift_right_logical(space, 3), lax.shift_right_logical(image, 2)
-    layer = ((image & 2) << 2) + (space & 7)
-    pair = jnp.where((x & 1) == 0, y, 3 - y)
-    return image, layer, x * 8 + pair * 2 + (image & 1)
+    pair = jnp.where((x & 1) == 0, 3 - y, y)
+    return image, lax.shift_right_logical(image, 1) & 1, x * 8 + pair * 2 + (image & 1)
 
 
 def dot(a, b):
@@ -116,24 +114,42 @@
     return jnp.concatenate([v] * PER_CHUNK, axis=1)
 
 
+def flat(ref):
+    return jnp.concatenate([ref[0], ref[1], ref[2]], axis=0)
+
+
 def coords_of(block):
     b = block[ROW_POS : ROW_POS + 24].astype(F32)
     return b[0:8] + b[8:16] + b[16:24]
 
 
-def pack_kernel(pos, embed, near, up, down, climb, out):
+def pack_kernel(
+    pos_in, embed_in, near_in, up_in, down_in, out,
+    pos, embed, near, up, down, sems,
+):
+    pairs = ((embed_in, embed), (near_in, near), (pos_in, pos), (up_in, up), (down_in, down))
+    copies = [pltpu.make_async_copy(a, b, sems.at[i]) for i, (a, b) in enumerate(pairs)]
+    for copy in copies:
+        copy.start()
+    copies[0].wait()
     out[0:CHANNELS, :] = embed[...].astype(F32).T.astype(BF16)
+    copies[1].wait()
+    out[ROW_NEAR:PACK_ROWS, :] = (near[...].astype(F32) - float(ATOMS)).astype(BF16)
+    for copy in copies[2:]:
+        copy.wait()
     zeros = jnp.zeros((5, ATOMS), F32)
-    parts = [jnp.concatenate([p.astype(F32), zeros], axis=0) for p in thirds(pos[0])]
-    level = jnp.full((1, ATOMS), climb[0].astype(F32) * (1.0 / DOMAINS), F32)
-    aux = jnp.concatenate([level, up[...].astype(F32), down[...].astype(F32), zeros], axis=0)
+    parts = [jnp.concatenate([p.astype(F32), zeros], axis=0) for p in thirds(flat(pos))]
+    aux = jnp.concatenate([up[...].astype(F32), down[...].astype(F32), zeros, zeros[:1]], axis=0)
     out[ROW_POS:ROW_NEAR, :] = jnp.concatenate(parts + [aux], axis=0).astype(BF16)
-    slots = near[...].astype(F32) - float(ATOMS)
-    square = jnp.concatenate([slots, jnp.zeros((ATOMS, ATOMS - SLOTS), F32)], axis=1)
-    out[ROW_NEAR:PACK_ROWS, :] = square.T[:SLOTS].astype(BF16)
-
-
-def weights_kernel(after, filter_in, filter_out, update, readout, in_t, out_t, update_t, read):
+
+
+def weights_kernel(
+    after, filter_in, filter_out, update, readout, reset, spring, time_step, mixing,
+    in_t, out_t, update_t, read, settings,
+):
+    for j, value in enumerate((reset[0].astype(F32), spring[0], time_step[0], mixing[0])):
+        settings[j : j + 1, :] = jnp.full((1, ATOMS), value, F32)
+    settings[4:8, :] = jnp.zeros((4, ATOMS), F32)
     for l in range(2):
         rows = pl.ds(l * 128, 128)
         high, low = halves(filter_in[l])
@@ -151,7 +167,7 @@
     _, _, domain = place()
     even = (domain & 1) == 0
     aux = pack[ROW_AUX : ROW_AUX + 8, :].astype(F32)
-    up, down = aux[1:2], aux[2:3]
+    up, down = aux[0:1], aux[1:2]
     rows = lax.broadcasted_iota(jnp.int32, (ATOMS, ATOMS), 0).astype(F32)
     block = pack[0:HALO_ROWS, :]
     for ids, chosen, send in (
@@ -163,7 +179,8 @@
         send[...] = dot(block, hot).astype(BF16)
 
 
-def slots_kernel(pack, hot):
+def slots_kernel(pack, hot, own):
+    own[...] = coords_of(pack[0:HALO_ROWS, :])
     _, _, domain = place()
     even = (domain & 1) == 0
     slots = pack[ROW_NEAR:PACK_ROWS, :].astype(F32)
@@ -213,8 +230,7 @@
     send_b[...] = dot(hid, list_b[...]).astype(BF16)
 
 
-def filters_kernel(pack, pairs, in_t, out_t, slope_one, slope_two, filter_two, own):
-    own[...] = coords_of(pack[0:HALO_ROWS, :])
+def filters_kernel(pairs, in_t, out_t, slope_one, slope_two, filter_two):
     centre = centres()
     for c in range(CHUNKS):
         vec = pairs[:, chunk(c)]
@@ -298,7 +314,7 @@
     send_b[...] = -ext[:, 2 * ATOMS :]
 
 
-def sums_kernel(force, from_a, from_b, list_a, list_b, own, prev, following, energy, pack, velocity, back, vec):
+def sums_kernel(force, from_a, from_b, list_a, list_b, own, energy, velocity, climb, out):
     image, _, _ = place()
 
     def returned(block, chosen):
@@ -307,41 +323,63 @@
         return got[0:8] + got[8:16]
 
     f = force[...] + returned(from_a[...], list_a[...]) + returned(from_b[...], list_b[...])
-    ahead = following[...] - own[...]
-    behind = own[...] - prev[...]
-    back[0:8, :] = f
-    back[8:16, :] = ahead
-    back[16:24, :] = behind
-    speed = velocity[0]
+    speed = flat(velocity)
     movable = (image > 0) & (image < IMAGES - 1)
+    speed_sq = jnp.where(movable, jnp.sum(speed * speed), 0.0)
+    lane = lax.broadcasted_iota(jnp.int32, (1, ATOMS), 1)
+    last = jnp.where(lane == 6 * IMAGES, speed_sq, 0.0)
+    last = jnp.where(lane == 7 * IMAGES + image, climb[0].astype(F32), last)
+    block = jnp.concatenate([f[0:3], own[0:3, :], energy[0:1, :], last], axis=0)
+    for j in range(IMAGES):
+        out[j * 8 : (j + 1) * 8, :] = block
+
+
+def column_kernel(blocks, out):
+    _, half, _ = place()
+    part = lambda r: blocks[pl.ds(r, IMAGES, stride=8), :]
+    force = [part(r) for r in range(3)]
+    coords = [part(r + 3) for r in range(3)]
+    ahead = [jnp.concatenate([p[1:], p[-1:]], axis=0) - p for p in coords]
+    behind = [p - jnp.concatenate([p[:1], p[:-1]], axis=0) for p in coords]
+    inner = lambda u, v: u[0] * v[0] + u[1] * v[1] + u[2] * v[2]
+    rows = [
+        part(6),
+        inner(ahead, ahead),
+        inner(ahead, behind),
+        inner(force, ahead),
+        inner(force, behind),
+        inner(force, force),
+        jnp.zeros((2 * IMAGES, ATOMS), F32),
+    ]
+    square = jnp.concatenate(rows, axis=0)
+    table = jnp.sum(square.T, axis=0, keepdims=True) + jnp.sum(part(7), axis=0, keepdims=True)
+    parts = force + ahead + behind
+    for y in range(4):
+        for core in range(2):
+            low = y * 4 + core
+            pick = lambda v: jnp.where(half == 0, v[low : low + 1], v[low + 2 : low + 3])
+            lines = [table] + [pick(v) for v in parts]
+            pairs = [jnp.concatenate(lines[2 * r : 2 * r + 2], axis=0) for r in range(BLOCK)]
+            for x in range(4):
+                target = x * 8 + (y if x % 2 else 3 - y) * 2 + core
+                for r in range(BLOCK):
+                    out[target * BLOCK + r] = pairs[r]
+
+
+def final_kernel(blocks, pos, velocity, settings, new_pos, new_speed, energy):
+    image, _, _ = place()
+    space = lax.axis_index("space")
+    reset, spring, step, mix = (settings[j : j + 1, :] for j in range(4))
+    total = blocks[0]
+    for j in range(1, DOMAINS):
+        total = total + blocks[j * BLOCK]
+    row = lax.broadcasted_iota(jnp.int32, (IMAGES, 1), 0)
+    lane = lax.broadcasted_iota(jnp.int32, (IMAGES, ATOMS), 1)
+    table = jnp.broadcast_to(total[0:1], (IMAGES, ATOMS))
+    column = lambda j: jnp.sum(jnp.where(lane == row + j * IMAGES, table, 0.0), axis=1, keepdims=True)
+    e, a, ab, fa, fb, ff, vv, level = (column(j) for j in range(8))
+    b = jnp.concatenate([a[:1], a[:-1]], axis=0)
     down = lambda v: jnp.sum(v, axis=0, keepdims=True)
-    level = pack[ROW_AUX : ROW_AUX + 8, :].astype(F32)[0:1] * (1.0 / ATOMS)
-    rows = (
-        energy[0:1, :],
-        down(ahead * ahead),
-        down(behind * behind),
-        down(ahead * behind),
-        down(f * ahead),
-        down(f * behind),
-        down(f * f),
-        jnp.where(movable, down(speed * speed), 0.0),
-        level,
-    )
-    lane = lax.broadcasted_iota(jnp.int32, (1, ATOMS), 1)
-    total = jnp.zeros((1, ATOMS), F32)
-    for j, row in enumerate(rows):
-        total = jnp.where(lane == j, jnp.sum(row, axis=1, keepdims=True), total)
-    vec[...] = jnp.broadcast_to(total, (DOMAINS, ATOMS))
-
-
-def layer_kernel(parts, out):
-    out[...] = jnp.broadcast_to(jnp.sum(parts[...], axis=0, keepdims=True), (IMAGES, ATOMS))
-
-
-def final_kernel(table, back, pos, velocity, reset, spring, time_step, mixing, new_pos, new_speed, energy):
-    image, _, _ = place()
-    t = table[...]
-    e, a, b, ab, fa, fb, ff, vv, level = (t[:, j : j + 1] for j in range(9))
     ahead_norm = jnp.sqrt(a + EPSILON)
     behind_norm = jnp.sqrt(b + EPSILON)
     tangent_sq = jnp.maximum(
@@ -353,29 +391,28 @@
     length = jnp.sqrt(tangent_sq + EPSILON)
     unit_sq = tangent_sq / (tangent_sq + EPSILON)
     parallel = (fa / ahead_norm + fb / behind_norm) / length
-    tension = spring[0] * (ahead_norm - behind_norm)
+    tension = spring[:, 0:1] * (ahead_norm - behind_norm)
     along = jnp.where(level > 0.5, -2.0 * parallel, tension - parallel)
     band_sq = ff + 2.0 * along * parallel + along * along * unit_sq
-    row = lax.broadcasted_iota(jnp.int32, (IMAGES, 1), 0)
     inner = (row > 0) & (row < IMAGES - 1)
-    down = lambda v: jnp.sum(v, axis=0, keepdims=True)
     force_norm = jnp.sqrt(down(jnp.where(inner, jnp.maximum(band_sq, 0.0), 0.0)) + EPSILON)
     speed_norm = jnp.sqrt(down(vv) + EPSILON)
     mine = row == image
     pick = lambda v: down(jnp.where(mine, v, 0.0))
-    shape = (3, ATOMS)
-    wide = lambda v: jnp.broadcast_to(jnp.broadcast_to(v, (1, ATOMS)), shape)
+    wide = lambda v: jnp.broadcast_to(jnp.broadcast_to(v, (1, ATOMS)), (3, ATOMS))
     energy[0] = jnp.sum(jnp.where(mine, e, 0.0))
-    tangent = back[8:11, :] / wide(pick(ahead_norm)) + back[16:19, :] / wide(pick(behind_norm))
-    band = back[0:3, :] + wide(pick(along / length)) * tangent
-    speed = velocity[0]
-    mix = mixing[0]
-    mixed = (1.0 - mix) * speed + wide(mix * speed_norm / force_norm) * band
-    kept = jnp.where(reset[0] > 0, 0.0, mixed)
+    back = jnp.concatenate([blocks[space * BLOCK + r] for r in range(BLOCK)], axis=0)
+    tangent = back[4:7] / wide(pick(ahead_norm)) + back[7:10] / wide(pick(behind_norm))
+    band = back[1:4] + wide(pick(along / length)) * tangent
+    speed = flat(velocity)
+    mixed = wide(1.0 - mix) * speed + wide(mix * speed_norm / force_norm) * band
+    kept = jnp.where(wide(reset) > 0.5, 0.0, mixed)
     movable = (image > 0) & (image < IMAGES - 1)
-    speed = jnp.where(movable, kept + time_step[0] * band, 0.0)
-    new_speed[0] = speed
-    new_pos[0] = pos[0] + time_step[0] * speed
+    speed = jnp.where(movable, kept + wide(step) * band, 0.0)
+    moved = flat(pos) + wide(step) * speed
+    for j in range(3):
+        new_speed[j] = speed[j : j + 1]
+        new_pos[j] = moved[j : j + 1]
 
 
 VMEM = pl.BlockSpec(memory_space=pltpu.VMEM)
@@ -396,24 +433,41 @@
     )(*args)
 
 
+def pack_call(*args):
+    return pl.pallas_call(
+        pack_kernel,
+        out_shape=jax.ShapeDtypeStruct((PACK_ROWS, ATOMS), BF16),
+        in_specs=[pl.BlockSpec(memory_space=pltpu.HBM)] * len(args),
+        out_specs=VMEM,
+        scratch_shapes=[pltpu.VMEM(a.shape, a.dtype) for a in args]
+        + [pltpu.SemaphoreType.DMA((len(args),))],
+        compiler_params=pltpu.CompilerParams(vmem_limit_bytes=60 << 20),
+        name="pack_kernel",
+    )(*args)
+
+
 def per_device(
     positions, velocity, embed, neighbours, send_up, send_down, climb, reset,
     filter_in, filter_out, update_weight, readout, spring, time_step, mixing,
 ):
     square = (ATOMS, ATOMS)
     wide = (CHANNELS, PAIRS)
-    (packed,) = call(
-        pack_kernel,
-        [((PACK_ROWS, ATOMS), BF16)],
-        (positions, embed, neighbours, send_up.reshape(1, ATOMS), send_down.reshape(1, ATOMS), climb),
-        scalars=(5,),
+    positions = positions.transpose(1, 0, 2)
+    velocity = velocity.transpose(1, 0, 2)
+    packed = pack_call(
+        positions, embed, neighbours.T, send_up.reshape(1, ATOMS), send_down.reshape(1, ATOMS)
     )
     pack = move(packed, TO_WORKER)
-    in_t, out_t, update_t, read = call(
+    in_t, out_t, update_t, read, settings = call(
         weights_kernel,
-        [((256, 128), BF16), ((256, 128), BF16), ((256, 128), BF16), (square, F32)],
-        (packed, filter_in, filter_out, update_weight, readout.reshape(1, CHANNELS)),
+        [((256, 128), BF16), ((256, 128), BF16), ((256, 128), BF16), (square, F32), ((8, ATOMS), F32)],
+        (
+            packed, filter_in, filter_out, update_weight, readout.reshape(1, CHANNELS),
+            reset, spring.reshape(1), time_step.reshape(1), mixing.reshape(1),
+        ),
+        scalars=(5, 6, 7, 8),
         flops=10**8,
+        limit=60 << 20,
     )
     list_a, list_b, send_a, send_b = call(
         lists_kernel,
@@ -421,7 +475,7 @@
         (pack,),
     )
     from_a, from_b = move(send_a, SWAP_A), move(send_b, SWAP_B)
-    (hot,) = call(slots_kernel, [((EXT, PAIRS), BF16)], (pack,), flops=10**9)
+    hot, own = call(slots_kernel, [((EXT, PAIRS), BF16), ((8, ATOMS), F32)], (pack,), flops=10**9)
     hidden, send_a, send_b, update_one, pairs, rows_one = call(
         first_kernel,
         [(square, BF16), (square, BF16), (square, BF16), (square, F32), ((8, PAIRS), F32), (wide, BF16)],
@@ -429,10 +483,10 @@
         flops=10**9,
     )
     from_a, from_b = move(send_a, SWAP_A), move(send_b, SWAP_B)
-    slope_one, slope_two, filter_two, own = call(
+    slope_one, slope_two, filter_two = call(
         filters_kernel,
-        [(wide, BF16), (wide, BF16), (wide, F32), ((8, ATOMS), F32)],
-        (pack, pairs, in_t, out_t),
+        [(wide, BF16), (wide, BF16), (wide, F32)],
+        (pairs, in_t, out_t),
         flops=10**9,
     )
     energy, grad_two, rows_two, grad_own, send_a, send_b = call(
@@ -442,7 +496,6 @@
         flops=10**9,
     )
     from_a, from_b = move(send_a, SWAP_A), move(send_b, SWAP_B)
-    prev, following = move(own, IMAGE_UP), move(own, IMAGE_DOWN)
     (dsq_two,) = call(
         slope_kernel,
         [((8, PAIRS), F32)],
@@ -459,26 +512,22 @@
         flops=10**9,
     )
     from_a, from_b = move(send_a, SWAP_A), move(send_b, SWAP_B)
-    back, vec = call(
+    (blocks,) = call(
         sums_kernel,
-        [((24, ATOMS), F32), ((DOMAINS, ATOMS), F32)],
-        (force, from_a, from_b, list_a, list_b, own, prev, following, energy, pack, velocity),
-    )
-    back = move(back, TO_HOME)
-    parts = lax.all_to_all(vec, AXES, 0, 0, tiled=True, axis_index_groups=LAYERS)
-    (layer,) = call(layer_kernel, [((IMAGES, ATOMS), F32)], (parts,))
-    table = lax.all_to_all(layer, AXES, 0, 0, tiled=True, axis_index_groups=COLUMNS)
+        [((IMAGES * 8, ATOMS), F32)],
+        (force, from_a, from_b, list_a, list_b, own, energy, velocity, climb),
+        scalars=(8,),
+    )
+    column = lax.all_to_all(blocks, AXES, 0, 0, tiled=True, axis_index_groups=COLUMNS)
+    (blocks,) = call(column_kernel, [((DOMAINS * BLOCK, 2, ATOMS), F32)], (column,))
+    table = lax.all_to_all(blocks, AXES, 0, 0, tiled=True, axis_index_groups=LAYERS)
     new_pos, new_speed, energies = call(
         final_kernel,
-        [((1, 3, ATOMS), F32), ((1, 3, ATOMS), F32), ((1,), F32)],
-        (
-            table, back, positions, velocity, reset,
-            spring.reshape(1), time_step.reshape(1), mixing.reshape(1),
-        ),
-        scalars=(4, 5, 6, 7),
+        [((3, 1, ATOMS), F32), ((3, 1, ATOMS), F32), ((1,), F32)],
+        (table, positions, velocity, settings),
         scalar_outs=(2,),
     )
-    return new_pos, new_speed, energies
+    return new_pos.transpose(1, 0, 2), new_speed.transpose(1, 0, 2), energies
 
 
 def solution(mesh):

time: 113 us -> 103 us (0.912)
  the two profiles are of different devices: /device:TPU:16 before, /device:TPU:1 now
where the time goes in v2:
time: 103 us; the launch traced here: 102 us
  blocking collectives  42.3 us (41%)
  starting transfers between devices  27.8 us (27%)
  Pallas kernels  17.1 us (17%)
  waiting for transfers between devices  10.6 us (10%)
  between operations  4.07 us (4%)
    ppermute x9, starting transfers between devices, move(): return lax.ppermute(values, AXES, pairs)  27.8 us
    all_to_all x1, blocking collectives, per_device(): lax.all_to_all(blocks, AXES, 0, 0, tiled=True, axis_index_groups=COLUMNS)  24.7 us
    all_to_all x1, blocking collectives, per_device(): lax.all_to_all(blocks, AXES, 0, 0, tiled=True, axis_index_groups=LAYERS)  17.6 us
    pallas_call x11, Pallas kernels, call(): pl.pallas_call(kernel, out_shape=[jax.ShapeDtypeStruct(s, t) for s, t in...  15.6 us
    ppermute x9, waiting for transfers between devices, move(): return lax.ppermute(values, AXES, pairs)  10.6 us
  transfers between devices with their start and end apart: 9, of which 5 were waited for; matrix products, arithmetic and copies ran while one was open for 0% of the time, Pallas kernels for 6%

profile of v2, /device:TPU:1, one launch (start us, length us, event | category | flops | bytes accessed | tf_op | source)
XLA Modules:
  0.0 101.9 jit_solution(14879424102725036170)
XLA Ops:
  0.6 1.5 %pack_kernel.1.after = bf16[192,128]{1,0:T(8,128)(2,1)} custom-call(f32[3,1,128]{2,1,0:T(1,128)} %bitcast.20, bf16[128,128]{1,0:T(8,128)(2,1)} %embed_in.1, s32[32,128]{1,0:T(8,128)} %bitcast.22, s32[1,128]{1,0:T(1,128)} %bitcast.23, s32[1,128]{1,0:T(1,128)} %bitcast.24), custom_call_target="tpu_custom_call" | custom-call | tf_op jit(solution)/shard_map/pack_kernel/pallas_call | solution.py:437
  2.2 7.4 %collective-permute-start = (bf16[192,128]{1,0:T(8,128)(2,1)}, bf16[192,128]{1,0:T(8,128)(2,1)S(1)}, u32[]{:S(2)}, u32[]{:S(2)}) collective-permute-start(bf16[192,128]{1,0:T(8,128)(2,1)} %pack_kernel.1.after), channel_id=1, source_target_pairs={{0,384},{1,416},{2,256},{3,288},{4,128},{5,160},{6,0},{7,32},{8,8}... | collective-permute-start | bytes 147464 | tf_op jit(solution)/shard_map/ppermute | solution.py:58
  12.2 1.7 %weights_kernel.1 = (bf16[256,128]{1,0:T(8,128)(2,1)}, bf16[256,128]{1,0:T(8,128)(2,1)}, bf16[256,128]{1,0:T(8,128)(2,1)}, f32[128,128]{1,0:T(8,128)}, f32[8,128]{1,0:T(8,128)}) custom-call(bf16[192,128]{1,0:T(8,128)(2,1)} %pack_kernel.1.after, f32[2,16,128]{2,1,0:T(8,128)} %filter_in.1, bf16[2,128,128]{2,1,0:T(8,128)(2,1)} %filter_out.5, ...), custom_call_target="tpu_custom_call" | custom-call | flops 100000000 | bytes 197136 | tf_op jit(solution)/shard_map/weights_kernel/pallas_call | solution.py:425
  13.9 0.0 copy-start.2
  13.9 0.0 copy-start.7
  13.9 0.0 copy-start.8
  13.9 4.5 %collective-permute-done.pack = bf16[192,128]{1,0:T(8,128)(2,1)S(1)} collective-permute-done((bf16[192,128]{1,0:T(8,128)(2,1)}, bf16[192,128]{1,0:T(8,128)(2,1)S(1)}, u32[]{:S(2)}, u32[]{:S(2)}) %collective-permute-start) | collective-permute-done | bytes 49184 | tf_op jit(solution)/shard_map/ppermute | solution.py:58
  18.4 0.2 lists_kernel.1
  18.6 4.4 %collective-permute-start.1 = (bf16[160,128]{1,0:T(8,128)(2,1)S(1)}, bf16[160,128]{1,0:T(8,128)(2,1)S(1)}, u32[]{:S(2)}, u32[]{:S(2)}) collective-permute-start(bf16[160,128]{1,0:T(8,128)(2,1)S(1)} %get-tuple-element.35), channel_id=1, source_target_pairs={{384,416},{416,384},{256,288},{288,256},{128,160},{160,128},{0,32}... | collective-permute-start | bytes 122888 | tf_op jit(solution)/shard_map/ppermute | solution.py:58
  23.0 1.9 %collective-permute-start.2 = (bf16[160,128]{1,0:T(8,128)(2,1)S(1)}, bf16[160,128]{1,0:T(8,128)(2,1)S(1)}, u32[]{:S(2)}, u32[]{:S(2)}) collective-permute-start(bf16[160,128]{1,0:T(8,128)(2,1)S(1)} %get-tuple-element.36), channel_id=1, source_target_pairs={{384,440},{416,256},{256,416},{288,128},{128,288},{160,0},{0,160},... | collective-permute-start | bytes 122888 | tf_op jit(solution)/shard_map/ppermute | solution.py:58
  25.0 1.0 %slots_kernel.1 = (bf16[384,4096]{1,0:T(8,128)(2,1)S(1)}, f32[8,128]{1,0:T(8,128)S(1)}) custom-call(bf16[192,128]{1,0:T(8,128)(2,1)S(1)} %collective-permute-done.pack), custom_call_target="tpu_custom_call" | custom-call | flops 1000000000 | bytes 49152 | tf_op jit(solution)/shard_map/slots_kernel/pallas_call | solution.py:425
  26.0 0.0 collective-permute-done.1.from_a
  26.0 2.4 %collective-permute-done.2.from_b = bf16[160,128]{1,0:T(8,128)(2,1)S(1)} collective-permute-done((bf16[160,128]{1,0:T(8,128)(2,1)S(1)}, bf16[160,128]{1,0:T(8,128)(2,1)S(1)}, u32[]{:S(2)}, u32[]{:S(2)}) %collective-permute-start.2) | collective-permute-done | bytes 40992 | tf_op jit(solution)/shard_map/ppermute | solution.py:58
  28.4 0.0 copy-done.2
  28.4 0.0 copy-done.7
  28.4 0.0 copy-done.8
  28.4 0.0 copy-start
  28.4 0.0 copy-start.3
  28.4 4.1 %first_kernel.1 = (bf16[128,128]{1,0:T(8,128)(2,1)S(1)}, bf16[128,128]{1,0:T(8,128)(2,1)S(1)}, bf16[128,128]{1,0:T(8,128)(2,1)S(1)}, f32[128,128]{1,0:T(8,128)S(...) custom-call(bf16[192,128]{1,0:T(8,128)(2,1)S(1)} %collective-permute-done.pack, ...), custom_call_target="tpu_custom_call" | custom-call | flops 1000000000 | bytes 3538944 | tf_op jit(solution)/shard_map/first_kernel/pallas_call | solution.py:425
  32.5 1.9 %collective-permute-start.3 = (bf16[128,128]{1,0:T(8,128)(2,1)S(1)}, bf16[128,128]{1,0:T(8,128)(2,1)S(1)}, u32[]{:S(2)}, u32[]{:S(2)}) collective-permute-start(bf16[128,128]{1,0:T(8,128)(2,1)S(1)} %get-tuple-element.44), channel_id=1, source_target_pairs={{384,416},{416,384},{256,288},{288,256},{128,160},{160,128},{0,32}... | collective-permute-start | bytes 98312 | tf_op jit(solution)/shard_map/ppermute | solution.py:58
  34.4 1.9 %collective-permute-start.4 = (bf16[128,128]{1,0:T(8,128)(2,1)S(1)}, bf16[128,128]{1,0:T(8,128)(2,1)S(1)}, u32[]{:S(2)}, u32[]{:S(2)}) collective-permute-start(bf16[128,128]{1,0:T(8,128)(2,1)S(1)} %get-tuple-element.45), channel_id=1, source_target_pairs={{384,440},{416,256},{256,416},{288,128},{128,288},{160,0},{0,160},... | collective-permute-start | bytes 98312 | tf_op jit(solution)/shard_map/ppermute | solution.py:58
  36.4 2.7 %filters_kernel.1 = (bf16[128,4096]{1,0:T(8,128)(2,1)S(1)}, bf16[128,4096]{1,0:T(8,128)(2,1)S(1)}, f32[128,4096]{1,0:T(8,128)S(1)}) custom-call(f32[8,4096]{1,0:T(8,128)S(1)} %get-tuple-element.46.pairs, bf16[256,128]{1,0:T(8,128)(2,1)S(1)} %copy-done.7, bf16[256,128]{1,0:T(8,128)(2,1)S(1)} %copy-done.8), custom_call_target="tpu_custom_call" | custom-call | flops 1000000000 | bytes 262144 | tf_op jit(solution)/shard_map/filters_kernel/pallas_call | solution.py:425
  39.1 0.0 copy-start.1
  39.1 0.0 collective-permute-done.3.from_a
  39.1 0.6 collective-permute-done.4.from_b
  39.7 0.0 copy-done
  39.8 0.0 copy-done.3
  39.8 2.1 %second_kernel.1 = (f32[8,128]{1,0:T(8,128)S(1)}, f32[128,128]{1,0:T(8,128)S(1)}, bf16[128,4096]{1,0:T(8,128)(2,1)S(1)}, f32[128,128]{1,0:T(8,128)S(1)}, bf16[12...) custom-call(bf16[128,128]{1,0:T(8,128)(2,1)S(1)} %get-tuple-element.43.hidden, ...), custom_call_target="tpu_custom_call" | custom-call | flops 1000000000 | bytes 5537792 | tf_op jit(solution)/shard_map/second_kernel/pallas_call | solution.py:425
  41.8 2.3 %collective-permute-start.5 = (bf16[128,128]{1,0:T(8,128)(2,1)S(1)}, bf16[128,128]{1,0:T(8,128)(2,1)S(1)}, u32[]{:S(2)}, u32[]{:S(2)}) collective-permute-start(bf16[128,128]{1,0:T(8,128)(2,1)S(1)} %get-tuple-element.50), channel_id=1, source_target_pairs={{384,416},{416,384},{256,288},{288,256},{128,160},{160,128},{0,32}... | collective-permute-start | bytes 98312 | tf_op jit(solution)/shard_map/ppermute | solution.py:58
  44.1 2.7 %collective-permute-start.6 = (bf16[128,128]{1,0:T(8,128)(2,1)S(1)}, bf16[128,128]{1,0:T(8,128)(2,1)S(1)}, u32[]{:S(2)}, u32[]{:S(2)}) collective-permute-start(bf16[128,128]{1,0:T(8,128)(2,1)S(1)} %get-tuple-element.51), channel_id=1, source_target_pairs={{384,440},{416,256},{256,416},{288,128},{128,288},{160,0},{0,160},... | collective-permute-start | bytes 98312 | tf_op jit(solution)/shard_map/ppermute | solution.py:58
  46.8 0.0 copy-done.1
  46.8 0.5 slope_kernel.1.dsq_two
  47.3 0.0 copy-start.4
  47.3 0.0 collective-permute-done.5.from_a
  47.4 2.0 %collective-permute-done.6.from_b = bf16[128,128]{1,0:T(8,128)(2,1)S(1)} collective-permute-done((bf16[128,128]{1,0:T(8,128)(2,1)S(1)}, bf16[128,128]{1,0:T(8,128)(2,1)S(1)}, u32[]{:S(2)}, u32[]{:S(2)}) %collective-permute-start.6) | collective-permute-done | bytes 32800 | tf_op jit(solution)/shard_map/ppermute | solution.py:58
  49.4 2.1 %third_kernel.1 = (f32[8,128]{1,0:T(8,128)S(1)}, f32[8,128]{1,0:T(8,128)S(1)}, f32[8,128]{1,0:T(8,128)S(1)}) custom-call(f32[128,128]{1,0:T(8,128)S(1)} %get-tuple-element.49.grad_own, bf16[128,128]{1,0:T(8,128)(2,1)S(1)} %collective-permute-done.5.from_a, bf16[128,128]{1,0:T(8,128)(2,1)S(1)} %collective-permute-done.6.from_b, ...), custom_call_target="tpu_custom_call" | custom-call | flops 1000000000 | bytes 5898240 | tf_op jit(solution)/shard_map/third_kernel/pallas_call | solution.py:425
  51.5 2.1 %collective-permute-start.7 = (f32[8,128]{1,0:T(8,128)S(1)}, f32[8,128]{1,0:T(8,128)S(1)}, u32[]{:S(2)}, u32[]{:S(2)}) collective-permute-start(f32[8,128]{1,0:T(8,128)S(1)} %get-tuple-element.59), channel_id=1, source_target_pairs={{384,416},{416,384},{256,288},{288,256},{128,160},{160,128},{0,32}... | collective-permute-start | bytes 12296 | tf_op jit(solution)/shard_map/ppermute | solution.py:58
  53.6 3.2 %collective-permute-start.8 = (f32[8,128]{1,0:T(8,128)S(1)}, f32[8,128]{1,0:T(8,128)S(1)}, u32[]{:S(2)}, u32[]{:S(2)}) collective-permute-start(f32[8,128]{1,0:T(8,128)S(1)} %get-tuple-element.60), channel_id=1, source_target_pairs={{384,440},{416,256},{256,416},{288,128},{128,288},{160,0},{0,160},... | collective-permute-start | bytes 12296 | tf_op jit(solution)/shard_map/ppermute | solution.py:58
  57.4 0.0 collective-permute-done.7.from_a
  57.4 1.1 %collective-permute-done.8.from_b = f32[8,128]{1,0:T(8,128)S(1)} collective-permute-done((f32[8,128]{1,0:T(8,128)S(1)}, f32[8,128]{1,0:T(8,128)S(1)}, u32[]{:S(2)}, u32[]{:S(2)}) %collective-permute-start.8) | collective-permute-done | bytes 4128 | tf_op jit(solution)/shard_map/ppermute | solution.py:58
  58.5 0.0 copy-done.4
  58.5 0.2 sums_kernel.1
  58.6 24.7 %all_to_all.16 = f32[16,8,128]{2,1,0:T(8,128)S(1)} all-to-all(f32[16,8,128]{2,1,0:T(8,128)S(1)} %bitcast.17), channel_id=1, replica_groups={{384,385,448,449,386,387,450,451,388,389,452,453,390,391,454,455},{416,..., dimensions={0} | all-to-all | bytes 131072 | tf_op jit(solution)/shard_map/all_to_all | solution.py:521
  83.3 0.1 column_kernel.1
  83.5 17.6 %all_to_all.17.blocks = f32[160,2,128]{2,1,0:T(2,128)S(1)} all-to-all(f32[160,2,128]{2,1,0:T(2,128)S(1)} %column_kernel.1), channel_id=1, replica_groups={{384,416,256,288,128,160,0,32,8,40,136,168,264,296,392,424,400,432,272,..., dimensions={0} | all-to-all | bytes 327680 | tf_op jit(solution)/shard_map/all_to_all | solution.py:523
  101.1 0.0 copy-done.5
  101.1 0.0 copy-done.6
  101.1 0.8 final_kernel.1
  (2 shorter events, 0.0 us)
Async XLA Ops:
  2.2 16.2 %collective-permute-start = (bf16[192,128]{1,0:T(8,128)(2,1)}, bf16[192,128]{1,0:T(8,128)(2,1)S(1)}, u32[]{:S(2)}, u32[]{:S(2)}) collective-permute-start(bf16[192,128]{1,0:T(8,128)(2,1)} %pack_kernel.1.after), channel_id=1, source_target_pairs={{0,384},{1,416},{2,256},{3,288},{4,128},{5,160},{6,0},{7,32},{8,8}... | collective-permute-start | bytes 147464 | tf_op jit(solution)/shard_map/ppermute | solution.py:58
  13.9 14.5 %copy-start.2 = (bf16[256,128]{1,0:T(8,128)(2,1)S(1)}, bf16[256,128]{1,0:T(8,128)(2,1)}, u32[]{:S(2)}) copy-start(bf16[256,128]{1,0:T(8,128)(2,1)} %get-tuple-element.42.update_t) | copy-start | bytes 196612
  13.9 14.5 %copy-start.7 = (bf16[256,128]{1,0:T(8,128)(2,1)S(1)}, bf16[256,128]{1,0:T(8,128)(2,1)}, u32[]{:S(2)}) copy-start(bf16[256,128]{1,0:T(8,128)(2,1)} %get-tuple-element.40.in_t) | copy-start | bytes 196612
  13.9 14.5 %copy-start.8 = (bf16[256,128]{1,0:T(8,128)(2,1)S(1)}, bf16[256,128]{1,0:T(8,128)(2,1)}, u32[]{:S(2)}) copy-start(bf16[256,128]{1,0:T(8,128)(2,1)} %get-tuple-element.41.out_t) | copy-start | bytes 196612
  18.6 7.4 %collective-permute-start.1 = (bf16[160,128]{1,0:T(8,128)(2,1)S(1)}, bf16[160,128]{1,0:T(8,128)(2,1)S(1)}, u32[]{:S(2)}, u32[]{:S(2)}) collective-permute-start(bf16[160,128]{1,0:T(8,128)(2,1)S(1)} %get-tuple-element.35), channel_id=1, source_target_pairs={{384,416},{416,384},{256,288},{288,256},{128,160},{160,128},{0,32}... | collective-permute-start | bytes 122888 | tf_op jit(solution)/shard_map/ppermute | solution.py:58
  23.0 5.3 %collective-permute-start.2 = (bf16[160,128]{1,0:T(8,128)(2,1)S(1)}, bf16[160,128]{1,0:T(8,128)(2,1)S(1)}, u32[]{:S(2)}, u32[]{:S(2)}) collective-permute-start(bf16[160,128]{1,0:T(8,128)(2,1)S(1)} %get-tuple-element.36), channel_id=1, source_target_pairs={{384,440},{416,256},{256,416},{288,128},{128,288},{160,0},{0,160},... | collective-permute-start | bytes 122888 | tf_op jit(solution)/shard_map/ppermute | solution.py:58
  28.4 11.4 %copy-start = (bf16[2,128,128]{2,1,0:T(8,128)(2,1)S(1)}, bf16[2,128,128]{2,1,0:T(8,128)(2,1)}, u32[]{:S(2)}) copy-start(bf16[2,128,128]{2,1,0:T(8,128)(2,1)} %update.5) | copy-start | bytes 196612
  28.4 11.4 %copy-start.3 = (f32[128,128]{1,0:T(8,128)S(1)}, f32[128,128]{1,0:T(8,128)}, u32[]{:S(2)}) copy-start(f32[128,128]{1,0:T(8,128)} %get-tuple-element.48.read) | copy-start | bytes 196612
  32.5 6.6 %collective-permute-start.3 = (bf16[128,128]{1,0:T(8,128)(2,1)S(1)}, bf16[128,128]{1,0:T(8,128)(2,1)S(1)}, u32[]{:S(2)}, u32[]{:S(2)}) collective-permute-start(bf16[128,128]{1,0:T(8,128)(2,1)S(1)} %get-tuple-element.44), channel_id=1, source_target_pairs={{384,416},{416,384},{256,288},{288,256},{128,160},{160,128},{0,32}... | collective-permute-start | bytes 98312 | tf_op jit(solution)/shard_map/ppermute | solution.py:58
  34.4 5.3 %collective-permute-start.4 = (bf16[128,128]{1,0:T(8,128)(2,1)S(1)}, bf16[128,128]{1,0:T(8,128)(2,1)S(1)}, u32[]{:S(2)}, u32[]{:S(2)}) collective-permute-start(bf16[128,128]{1,0:T(8,128)(2,1)S(1)} %get-tuple-element.45), channel_id=1, source_target_pairs={{384,440},{416,256},{256,416},{288,128},{128,288},{160,0},{0,160},... | collective-permute-start | bytes 98312 | tf_op jit(solution)/shard_map/ppermute | solution.py:58
  39.1 7.7 %copy-start.1 = (bf16[2,128,128]{2,1,0:T(8,128)(2,1)S(1)}, bf16[2,128,128]{2,1,0:T(8,128)(2,1)}, u32[]{:S(2)}) copy-start(bf16[2,128,128]{2,1,0:T(8,128)(2,1)} %filter_out.5) | copy-start | bytes 196612
  41.8 5.5 %collective-permute-start.5 = (bf16[128,128]{1,0:T(8,128)(2,1)S(1)}, bf16[128,128]{1,0:T(8,128)(2,1)S(1)}, u32[]{:S(2)}, u32[]{:S(2)}) collective-permute-start(bf16[128,128]{1,0:T(8,128)(2,1)S(1)} %get-tuple-element.50), channel_id=1, source_target_pairs={{384,416},{416,384},{256,288},{288,256},{128,160},{160,128},{0,32}... | collective-permute-start | bytes 98312 | tf_op jit(solution)/shard_map/ppermute | solution.py:58
  44.1 5.2 %collective-permute-start.6 = (bf16[128,128]{1,0:T(8,128)(2,1)S(1)}, bf16[128,128]{1,0:T(8,128)(2,1)S(1)}, u32[]{:S(2)}, u32[]{:S(2)}) collective-permute-start(bf16[128,128]{1,0:T(8,128)(2,1)S(1)} %get-tuple-element.51), channel_id=1, source_target_pairs={{384,440},{416,256},{256,416},{288,128},{128,288},{160,0},{0,160},... | collective-permute-start | bytes 98312 | tf_op jit(solution)/shard_map/ppermute | solution.py:58
  47.3 11.1 %copy-start.4 = (f32[1,3,128]{2,0,1:T(1,128)S(1)}, f32[1,3,128]{2,0,1:T(1,128)}, u32[]{:S(2)}) copy-start(f32[1,3,128]{2,0,1:T(1,128)} %param.16) | copy-start | bytes 4612
  49.4 51.7 %copy-start.5 = (f32[1,3,128]{2,0,1:T(1,128)S(1)}, f32[1,3,128]{2,0,1:T(1,128)}, u32[]{:S(2)}) copy-start(f32[1,3,128]{2,0,1:T(1,128)} %param.15) | copy-start | bytes 4612
  49.4 51.7 %copy-start.6 = (f32[8,128]{1,0:T(8,128)S(1)}, f32[8,128]{1,0:T(8,128)}, u32[]{:S(2)}) copy-start(f32[8,128]{1,0:T(8,128)} %get-tuple-element.63.settings) | copy-start | bytes 12292
  51.5 5.9 %collective-permute-start.7 = (f32[8,128]{1,0:T(8,128)S(1)}, f32[8,128]{1,0:T(8,128)S(1)}, u32[]{:S(2)}, u32[]{:S(2)}) collective-permute-start(f32[8,128]{1,0:T(8,128)S(1)} %get-tuple-element.59), channel_id=1, source_target_pairs={{384,416},{416,384},{256,288},{288,256},{128,160},{160,128},{0,32}... | collective-permute-start | bytes 12296 | tf_op jit(solution)/shard_map/ppermute | solution.py:58
  53.6 4.9 %collective-permute-start.8 = (f32[8,128]{1,0:T(8,128)S(1)}, f32[8,128]{1,0:T(8,128)S(1)}, u32[]{:S(2)}, u32[]{:S(2)}) collective-permute-start(f32[8,128]{1,0:T(8,128)S(1)} %get-tuple-element.60), channel_id=1, source_target_pairs={{384,440},{416,256},{256,416},{288,128},{128,288},{160,0},{0,160},... | collective-permute-start | bytes 12296 | tf_op jit(solution)/shard_map/ppermute | solution.py:58

commit v3 on v2

--- a/solution.py
+++ b/solution.py
@@ -15,7 +15,7 @@
 CHANNELS = 128
 SLOTS = 32
 PAIRS = ATOMS * SLOTS
-CHUNK = 512
+CHUNK = 2048
 PER_CHUNK = CHUNK // ATOMS
 CHUNKS = PAIRS // CHUNK
 EXT = 3 * ATOMS
@@ -39,11 +39,17 @@
     return image * DOMAINS + domain
 
 
+RING = [
+    (1, 2), (1, 3), (0, 3), (0, 2), (0, 1), (0, 0), (1, 0), (1, 1),
+    (2, 1), (2, 0), (3, 0), (3, 1), (3, 2), (3, 3), (2, 3), (2, 2),
+]
+LAYER_PAIR = (1, 0, 3, 2)
+
+
 def worker(image, domain):
-    x, rest = divmod(domain, 8)
-    pair, core = divmod(rest, 2)
-    y, half, side = image // 4, image // 2 % 2, image % 2
-    return device_at(x, pair if x % 2 else 3 - pair, half * 8 + y * 2 + side, core)
+    x, y = RING[domain // 2]
+    home_y, half, side = image // 4, image // 2 % 2, image % 2
+    return device_at(x, y, half * 8 + LAYER_PAIR[home_y] * 2 + side, domain % 2)
 
 
 CELLS = [(i, d) for i in range(IMAGES) for d in range(DOMAINS)]
@@ -60,9 +66,11 @@
 
 def place():
     image, space = lax.axis_index("image"), lax.axis_index("space")
-    x, y = lax.shift_right_logical(space, 3), lax.shift_right_logical(image, 2)
-    pair = jnp.where((x & 1) == 0, 3 - y, y)
-    return image, lax.shift_right_logical(image, 1) & 1, x * 8 + pair * 2 + (image & 1)
+    cell = (lax.shift_right_logical(space, 3) << 2) + lax.shift_right_logical(image, 2)
+    pair = jnp.int32(0)
+    for step, (x, y) in enumerate(RING):
+        pair = jnp.where(cell == x * 4 + y, step, pair)
+    return image, lax.shift_right_logical(image, 1) & 1, pair * 2 + (image & 1)
 
 
 def dot(a, b):
@@ -152,7 +160,7 @@
     settings[4:8, :] = jnp.zeros((4, ATOMS), F32)
     for l in range(2):
         rows = pl.ds(l * 128, 128)
-        high, low = halves(filter_in[l])
+        high, low = halves(0.5 * filter_in[l])
         filler = jnp.zeros((128 - 3 * BASIS, CHANNELS), F32)
         tall = jnp.concatenate(
             [high.astype(F32), high.astype(F32), low.astype(F32), filler], axis=0
@@ -216,8 +224,8 @@
         sq = jnp.sum(vec * vec, axis=0, keepdims=True)
         scaled = (sq - centre) * (1.0 / BASIS_WIDTH)
         radial = jnp.exp(-scaled * scaled)
-        pre = dot(in_t[0:128, 0 : 3 * BASIS], stacked(radial))
-        act = (pre * gate(pre)).astype(BF16)
+        half = dot(in_t[0:128, 0 : 3 * BASIS], stacked(radial))
+        act = (half + half * jnp.tanh(half)).astype(BF16)
         filt = dot(out_t[0:128, :], act)
         rows = got[0:CHANNELS]
         rows_one[:, chunk(c)] = rows.astype(BF16)
@@ -241,13 +249,13 @@
         steep = stacked(radial * scaled * (-2.0 / BASIS_WIDTH))
         for l, slope in ((0, slope_one), (1, slope_two)):
             weight = in_t[l * 128 : (l + 1) * 128, 0 : 3 * BASIS]
-            pre = dot(weight, tall)
+            half = dot(weight, tall)
             change = dot(weight, steep)
-            g = gate(pre)
-            act = pre * g
-            slope[:, chunk(c)] = ((g + act * (1.0 - g)) * change).astype(slope.dtype)
+            t = jnp.tanh(half)
+            bent = half * t
+            slope[:, chunk(c)] = ((1.0 + t) * (1.0 + half - bent) * change).astype(slope.dtype)
             if l == 1:
-                filter_two[:, chunk(c)] = dot(out_t[128:256, :], act.astype(BF16))
+                filter_two[:, chunk(c)] = dot(out_t[128:256, :], (half + bent).astype(BF16))
 
 
 def second_kernel(
@@ -361,7 +369,7 @@
             lines = [table] + [pick(v) for v in parts]
             pairs = [jnp.concatenate(lines[2 * r : 2 * r + 2], axis=0) for r in range(BLOCK)]
             for x in range(4):
-                target = x * 8 + (y if x % 2 else 3 - y) * 2 + core
+                target = RING.index((x, y)) * 2 + core
                 for r in range(BLOCK):
                     out[target * BLOCK + r] = pairs[r]
 

time: 103 us -> 96.7 us (0.939)
  starting transfers between devices: 27.8 us -> 32.4 us
  blocking collectives: 42.3 us -> 37.8 us
  Pallas kernels: 17.1 us -> 14 us
  waiting for transfers between devices: 10.6 us -> 7.72 us
    ppermute x9, starting transfers between devices: 27.8 us -> 32.4 us  [move(): return lax.ppermute(values, AXES, pairs)]
    pallas_call x11, Pallas kernels: 15.6 us -> 12.5 us  [call(): pl.pallas_call(kernel, out_shape=[jax.ShapeDtypeStruct(s, t) for s, t in...]
    ppermute x9, waiting for transfers between devices: 10.6 us -> 7.72 us  [move(): return lax.ppermute(values, AXES, pairs)]
    all_to_all x1, blocking collectives: 17.6 us -> 15.3 us  [per_device(): lax.all_to_all(blocks, AXES, 0, 0, tiled=True, axis_index_groups=LAYERS)]
    all_to_all x1, blocking collectives: 24.7 us -> 22.5 us  [per_device(): lax.all_to_all(blocks, AXES, 0, 0, tiled=True, axis_index_groups=COLUMNS)]
  transfers between devices with their start and end apart: 9 -> 9, of which waited for: 5 -> 4; matrix products, arithmetic and copies ran while one was open for 0% -> 0% of each run, Pallas kernels for 6% -> 6%
where the time goes in v3:
time: 96.7 us; the launch traced here: 96.1 us
  blocking collectives  37.8 us (39%)
  starting transfers between devices  32.4 us (34%)
  Pallas kernels  14 us (14%)
  waiting for transfers between devices  7.72 us (8%)
  between operations  4.07 us (4%)
    ppermute x9, starting transfers between devices, move(): return lax.ppermute(values, AXES, pairs)  32.4 us
    all_to_all x1, blocking collectives, per_device(): lax.all_to_all(blocks, AXES, 0, 0, tiled=True, axis_index_groups=COLUMNS)  22.5 us
    all_to_all x1, blocking collectives, per_device(): lax.all_to_all(blocks, AXES, 0, 0, tiled=True, axis_index_groups=LAYERS)  15.3 us
    pallas_call x11, Pallas kernels, call(): pl.pallas_call(kernel, out_shape=[jax.ShapeDtypeStruct(s, t) for s, t in...  12.5 us
    ppermute x9, waiting for transfers between devices, move(): return lax.ppermute(values, AXES, pairs)  7.72 us
  transfers between devices with their start and end apart: 9, of which 4 were waited for; matrix products, arithmetic and copies ran while one was open for 0% of the time, Pallas kernels for 6%

profile of v3, /device:TPU:1, one launch (start us, length us, event | category | flops | bytes accessed | tf_op | source)
XLA Modules:
  0.0 96.1 jit_solution(15185927959948736702)
XLA Ops:
  0.6 1.5 %pack_kernel.1.after = bf16[192,128]{1,0:T(8,128)(2,1)} custom-call(f32[3,1,128]{2,1,0:T(1,128)} %bitcast.20, bf16[128,128]{1,0:T(8,128)(2,1)} %embed_in.1, s32[32,128]{1,0:T(8,128)} %bitcast.22, s32[1,128]{1,0:T(1,128)} %bitcast.23, s32[1,128]{1,0:T(1,128)} %bitcast.24), custom_call_target="tpu_custom_call" | custom-call | tf_op jit(solution)/shard_map/pack_kernel/pallas_call | solution.py:445
  2.2 11.2 %collective-permute-start = (bf16[192,128]{1,0:T(8,128)(2,1)}, bf16[192,128]{1,0:T(8,128)(2,1)S(1)}, u32[]{:S(2)}, u32[]{:S(2)}) collective-permute-start(bf16[192,128]{1,0:T(8,128)(2,1)} %pack_kernel.1.after), channel_id=1, source_target_pairs={{0,266},{1,298},{2,394},{3,426},{4,386},{5,418},{6,258},{7,290},{8... | collective-permute-start | bytes 147464 | tf_op jit(solution)/shard_map/ppermute | solution.py:64
  16.0 1.7 %weights_kernel.1 = (bf16[256,128]{1,0:T(8,128)(2,1)}, bf16[256,128]{1,0:T(8,128)(2,1)}, bf16[256,128]{1,0:T(8,128)(2,1)}, f32[128,128]{1,0:T(8,128)}, f32[8,128]{1,0:T(8,128)}) custom-call(bf16[192,128]{1,0:T(8,128)(2,1)} %pack_kernel.1.after, f32[2,16,128]{2,1,0:T(8,128)} %filter_in.1, bf16[2,128,128]{2,1,0:T(8,128)(2,1)} %filter_out.5, ...), custom_call_target="tpu_custom_call" | custom-call | flops 100000000 | bytes 197136 | tf_op jit(solution)/shard_map/weights_kernel/pallas_call | solution.py:433
  17.7 0.0 copy-start.2
  17.7 0.0 copy-start.7
  17.7 0.0 copy-start.8
  17.7 0.0 collective-permute-done.pack
  17.7 0.2 lists_kernel.1
  17.9 3.3 %collective-permute-start.1 = (bf16[160,128]{1,0:T(8,128)(2,1)S(1)}, bf16[160,128]{1,0:T(8,128)(2,1)S(1)}, u32[]{:S(2)}, u32[]{:S(2)}) collective-permute-start(bf16[160,128]{1,0:T(8,128)(2,1)S(1)} %get-tuple-element.35), channel_id=1, source_target_pairs={{266,298},{298,266},{394,426},{426,394},{386,418},{418,386},{258,2... | collective-permute-start | bytes 122888 | tf_op jit(solution)/shard_map/ppermute | solution.py:64
  21.2 1.9 %collective-permute-start.2 = (bf16[160,128]{1,0:T(8,128)(2,1)S(1)}, bf16[160,128]{1,0:T(8,128)(2,1)S(1)}, u32[]{:S(2)}, u32[]{:S(2)}) collective-permute-start(bf16[160,128]{1,0:T(8,128)(2,1)S(1)} %get-tuple-element.36), channel_id=1, source_target_pairs={{266,306},{298,394},{394,298},{426,386},{386,426},{418,258},{258,4... | collective-permute-start | bytes 122888 | tf_op jit(solution)/shard_map/ppermute | solution.py:64
  23.1 1.0 %slots_kernel.1 = (bf16[384,4096]{1,0:T(8,128)(2,1)S(1)}, f32[8,128]{1,0:T(8,128)S(1)}) custom-call(bf16[192,128]{1,0:T(8,128)(2,1)S(1)} %collective-permute-done.pack), custom_call_target="tpu_custom_call" | custom-call | flops 1000000000 | bytes 49152 | tf_op jit(solution)/shard_map/slots_kernel/pallas_call | solution.py:433
  24.1 0.0 collective-permute-done.1.from_a
  24.1 2.4 %collective-permute-done.2.from_b = bf16[160,128]{1,0:T(8,128)(2,1)S(1)} collective-permute-done((bf16[160,128]{1,0:T(8,128)(2,1)S(1)}, bf16[160,128]{1,0:T(8,128)(2,1)S(1)}, u32[]{:S(2)}, u32[]{:S(2)}) %collective-permute-start.2) | collective-permute-done | bytes 40992 | tf_op jit(solution)/shard_map/ppermute | solution.py:64
  26.5 0.0 copy-done.2
  26.5 0.0 copy-done.7
  26.5 0.0 copy-done.8
  26.5 0.0 copy-start
  26.5 0.0 copy-start.3
  26.5 1.9 %first_kernel.1 = (bf16[128,128]{1,0:T(8,128)(2,1)S(1)}, bf16[128,128]{1,0:T(8,128)(2,1)S(1)}, bf16[128,128]{1,0:T(8,128)(2,1)S(1)}, f32[128,128]{1,0:T(8,128)S(...) custom-call(bf16[192,128]{1,0:T(8,128)(2,1)S(1)} %collective-permute-done.pack, ...), custom_call_target="tpu_custom_call" | custom-call | flops 1000000000 | bytes 3538944 | tf_op jit(solution)/shard_map/first_kernel/pallas_call | solution.py:433
  28.4 1.9 %collective-permute-start.3 = (bf16[128,128]{1,0:T(8,128)(2,1)S(1)}, bf16[128,128]{1,0:T(8,128)(2,1)S(1)}, u32[]{:S(2)}, u32[]{:S(2)}) collective-permute-start(bf16[128,128]{1,0:T(8,128)(2,1)S(1)} %get-tuple-element.44), channel_id=1, source_target_pairs={{266,298},{298,266},{394,426},{426,394},{386,418},{418,386},{258,2... | collective-permute-start | bytes 98312 | tf_op jit(solution)/shard_map/ppermute | solution.py:64
  30.4 2.8 %collective-permute-start.4 = (bf16[128,128]{1,0:T(8,128)(2,1)S(1)}, bf16[128,128]{1,0:T(8,128)(2,1)S(1)}, u32[]{:S(2)}, u32[]{:S(2)}) collective-permute-start(bf16[128,128]{1,0:T(8,128)(2,1)S(1)} %get-tuple-element.45), channel_id=1, source_target_pairs={{266,306},{298,394},{394,298},{426,386},{386,426},{418,258},{258,4... | collective-permute-start | bytes 98312 | tf_op jit(solution)/shard_map/ppermute | solution.py:64
  33.2 2.3 %filters_kernel.1 = (bf16[128,4096]{1,0:T(8,128)(2,1)S(1)}, bf16[128,4096]{1,0:T(8,128)(2,1)S(1)}, f32[128,4096]{1,0:T(8,128)S(1)}) custom-call(f32[8,4096]{1,0:T(8,128)S(1)} %get-tuple-element.46.pairs, bf16[256,128]{1,0:T(8,128)(2,1)S(1)} %copy-done.7, bf16[256,128]{1,0:T(8,128)(2,1)S(1)} %copy-done.8), custom_call_target="tpu_custom_call" | custom-call | flops 1000000000 | bytes 262144 | tf_op jit(solution)/shard_map/filters_kernel/pallas_call | solution.py:433
  35.4 0.0 copy-start.1
  35.5 0.0 collective-permute-done.3.from_a
  35.5 0.1 collective-permute-done.4.from_b
  35.6 0.0 copy-done
  35.6 0.0 copy-done.3
  35.6 2.1 %second_kernel.1 = (f32[8,128]{1,0:T(8,128)S(1)}, f32[128,128]{1,0:T(8,128)S(1)}, bf16[128,4096]{1,0:T(8,128)(2,1)S(1)}, f32[128,128]{1,0:T(8,128)S(1)}, bf16[12...) custom-call(bf16[128,128]{1,0:T(8,128)(2,1)S(1)} %get-tuple-element.43.hidden, ...), custom_call_target="tpu_custom_call" | custom-call | flops 1000000000 | bytes 5537792 | tf_op jit(solution)/shard_map/second_kernel/pallas_call | solution.py:433
  37.7 5.2 %collective-permute-start.5 = (bf16[128,128]{1,0:T(8,128)(2,1)S(1)}, bf16[128,128]{1,0:T(8,128)(2,1)S(1)}, u32[]{:S(2)}, u32[]{:S(2)}) collective-permute-start(bf16[128,128]{1,0:T(8,128)(2,1)S(1)} %get-tuple-element.50), channel_id=1, source_target_pairs={{266,298},{298,266},{394,426},{426,394},{386,418},{418,386},{258,2... | collective-permute-start | bytes 98312 | tf_op jit(solution)/shard_map/ppermute | solution.py:64
  42.9 1.9 %collective-permute-start.6 = (bf16[128,128]{1,0:T(8,128)(2,1)S(1)}, bf16[128,128]{1,0:T(8,128)(2,1)S(1)}, u32[]{:S(2)}, u32[]{:S(2)}) collective-permute-start(bf16[128,128]{1,0:T(8,128)(2,1)S(1)} %get-tuple-element.51), channel_id=1, source_target_pairs={{266,306},{298,394},{394,298},{426,386},{386,426},{418,258},{258,4... | collective-permute-start | bytes 98312 | tf_op jit(solution)/shard_map/ppermute | solution.py:64
  44.8 0.0 copy-done.1
  44.8 0.5 slope_kernel.1.dsq_two
  45.3 0.0 copy-start.4
  45.4 0.0 collective-permute-done.5.from_a
  45.4 2.9 %collective-permute-done.6.from_b = bf16[128,128]{1,0:T(8,128)(2,1)S(1)} collective-permute-done((bf16[128,128]{1,0:T(8,128)(2,1)S(1)}, bf16[128,128]{1,0:T(8,128)(2,1)S(1)}, u32[]{:S(2)}, u32[]{:S(2)}) %collective-permute-start.6) | collective-permute-done | bytes 32800 | tf_op jit(solution)/shard_map/ppermute | solution.py:64
  48.2 1.6 %third_kernel.1 = (f32[8,128]{1,0:T(8,128)S(1)}, f32[8,128]{1,0:T(8,128)S(1)}, f32[8,128]{1,0:T(8,128)S(1)}) custom-call(f32[128,128]{1,0:T(8,128)S(1)} %get-tuple-element.49.grad_own, bf16[128,128]{1,0:T(8,128)(2,1)S(1)} %collective-permute-done.5.from_a, bf16[128,128]{1,0:T(8,128)(2,1)S(1)} %collective-permute-done.6.from_b, ...), custom_call_target="tpu_custom_call" | custom-call | flops 1000000000 | bytes 5898240 | tf_op jit(solution)/shard_map/third_kernel/pallas_call | solution.py:433
  49.9 2.3 %collective-permute-start.7 = (f32[8,128]{1,0:T(8,128)S(1)}, f32[8,128]{1,0:T(8,128)S(1)}, u32[]{:S(2)}, u32[]{:S(2)}) collective-permute-start(f32[8,128]{1,0:T(8,128)S(1)} %get-tuple-element.59), channel_id=1, source_target_pairs={{266,298},{298,266},{394,426},{426,394},{386,418},{418,386},{258,2... | collective-permute-start | bytes 12296 | tf_op jit(solution)/shard_map/ppermute | solution.py:64
  52.2 1.9 %collective-permute-start.8 = (f32[8,128]{1,0:T(8,128)S(1)}, f32[8,128]{1,0:T(8,128)S(1)}, u32[]{:S(2)}, u32[]{:S(2)}) collective-permute-start(f32[8,128]{1,0:T(8,128)S(1)} %get-tuple-element.60), channel_id=1, source_target_pairs={{266,306},{298,394},{394,298},{426,386},{386,426},{418,258},{258,4... | collective-permute-start | bytes 12296 | tf_op jit(solution)/shard_map/ppermute | solution.py:64
  54.8 0.0 collective-permute-done.7.from_a
  54.8 2.3 %collective-permute-done.8.from_b = f32[8,128]{1,0:T(8,128)S(1)} collective-permute-done((f32[8,128]{1,0:T(8,128)S(1)}, f32[8,128]{1,0:T(8,128)S(1)}, u32[]{:S(2)}, u32[]{:S(2)}) %collective-permute-start.8) | collective-permute-done | bytes 4128 | tf_op jit(solution)/shard_map/ppermute | solution.py:64
  57.1 0.0 copy-done.4
  57.1 0.2 sums_kernel.1
  57.3 22.5 %all_to_all.16 = f32[16,8,128]{2,1,0:T(8,128)S(1)} all-to-all(f32[16,8,128]{2,1,0:T(8,128)S(1)} %bitcast.17), channel_id=1, replica_groups={{266,267,330,331,264,265,328,329,270,271,334,335,268,269,332,333},{298,..., dimensions={0} | all-to-all | bytes 131072 | tf_op jit(solution)/shard_map/all_to_all | solution.py:529
  79.8 0.1 column_kernel.1
  79.9 15.3 %all_to_all.17.blocks = f32[160,2,128]{2,1,0:T(2,128)S(1)} all-to-all(f32[160,2,128]{2,1,0:T(2,128)S(1)} %column_kernel.1), channel_id=1, replica_groups={{266,298,394,426,386,418,258,290,130,162,2,34,10,42,138,170,146,178,18,..., dimensions={0} | all-to-all | bytes 327680 | tf_op jit(solution)/shard_map/all_to_all | solution.py:531
  95.2 0.0 copy-done.5
  95.2 0.0 copy-done.6
  95.2 0.8 final_kernel.1
  (2 shorter events, 0.0 us)
Async XLA Ops:
  2.2 15.5 %collective-permute-start = (bf16[192,128]{1,0:T(8,128)(2,1)}, bf16[192,128]{1,0:T(8,128)(2,1)S(1)}, u32[]{:S(2)}, u32[]{:S(2)}) collective-permute-start(bf16[192,128]{1,0:T(8,128)(2,1)} %pack_kernel.1.after), channel_id=1, source_target_pairs={{0,266},{1,298},{2,394},{3,426},{4,386},{5,418},{6,258},{7,290},{8... | collective-permute-start | bytes 147464 | tf_op jit(solution)/shard_map/ppermute | solution.py:64
  17.7 8.8 %copy-start.2 = (bf16[256,128]{1,0:T(8,128)(2,1)S(1)}, bf16[256,128]{1,0:T(8,128)(2,1)}, u32[]{:S(2)}) copy-start(bf16[256,128]{1,0:T(8,128)(2,1)} %get-tuple-element.42.update_t) | copy-start | bytes 196612
  17.7 8.8 %copy-start.7 = (bf16[256,128]{1,0:T(8,128)(2,1)S(1)}, bf16[256,128]{1,0:T(8,128)(2,1)}, u32[]{:S(2)}) copy-start(bf16[256,128]{1,0:T(8,128)(2,1)} %get-tuple-element.40.in_t) | copy-start | bytes 196612
  17.7 8.8 %copy-start.8 = (bf16[256,128]{1,0:T(8,128)(2,1)S(1)}, bf16[256,128]{1,0:T(8,128)(2,1)}, u32[]{:S(2)}) copy-start(bf16[256,128]{1,0:T(8,128)(2,1)} %get-tuple-element.41.out_t) | copy-start | bytes 196612
  17.9 6.2 %collective-permute-start.1 = (bf16[160,128]{1,0:T(8,128)(2,1)S(1)}, bf16[160,128]{1,0:T(8,128)(2,1)S(1)}, u32[]{:S(2)}, u32[]{:S(2)}) collective-permute-start(bf16[160,128]{1,0:T(8,128)(2,1)S(1)} %get-tuple-element.35), channel_id=1, source_target_pairs={{266,298},{298,266},{394,426},{426,394},{386,418},{418,386},{258,2... | collective-permute-start | bytes 122888 | tf_op jit(solution)/shard_map/ppermute | solution.py:64
  21.2 5.3 %collective-permute-start.2 = (bf16[160,128]{1,0:T(8,128)(2,1)S(1)}, bf16[160,128]{1,0:T(8,128)(2,1)S(1)}, u32[]{:S(2)}, u32[]{:S(2)}) collective-permute-start(bf16[160,128]{1,0:T(8,128)(2,1)S(1)} %get-tuple-element.36), channel_id=1, source_target_pairs={{266,306},{298,394},{394,298},{426,386},{386,426},{418,258},{258,4... | collective-permute-start | bytes 122888 | tf_op jit(solution)/shard_map/ppermute | solution.py:64
  26.5 9.1 %copy-start = (bf16[2,128,128]{2,1,0:T(8,128)(2,1)S(1)}, bf16[2,128,128]{2,1,0:T(8,128)(2,1)}, u32[]{:S(2)}) copy-start(bf16[2,128,128]{2,1,0:T(8,128)(2,1)} %update.5) | copy-start | bytes 196612
  26.5 9.1 %copy-start.3 = (f32[128,128]{1,0:T(8,128)S(1)}, f32[128,128]{1,0:T(8,128)}, u32[]{:S(2)}) copy-start(f32[128,128]{1,0:T(8,128)} %get-tuple-element.48.read) | copy-start | bytes 196612
  28.4 7.0 %collective-permute-start.3 = (bf16[128,128]{1,0:T(8,128)(2,1)S(1)}, bf16[128,128]{1,0:T(8,128)(2,1)S(1)}, u32[]{:S(2)}, u32[]{:S(2)}) collective-permute-start(bf16[128,128]{1,0:T(8,128)(2,1)S(1)} %get-tuple-element.44), channel_id=1, source_target_pairs={{266,298},{298,266},{394,426},{426,394},{386,418},{418,386},{258,2... | collective-permute-start | bytes 98312 | tf_op jit(solution)/shard_map/ppermute | solution.py:64
  30.4 5.2 %collective-permute-start.4 = (bf16[128,128]{1,0:T(8,128)(2,1)S(1)}, bf16[128,128]{1,0:T(8,128)(2,1)S(1)}, u32[]{:S(2)}, u32[]{:S(2)}) collective-permute-start(bf16[128,128]{1,0:T(8,128)(2,1)S(1)} %get-tuple-element.45), channel_id=1, source_target_pairs={{266,306},{298,394},{394,298},{426,386},{386,426},{418,258},{258,4... | collective-permute-start | bytes 98312 | tf_op jit(solution)/shard_map/ppermute | solution.py:64
  35.4 9.4 %copy-start.1 = (bf16[2,128,128]{2,1,0:T(8,128)(2,1)S(1)}, bf16[2,128,128]{2,1,0:T(8,128)(2,1)}, u32[]{:S(2)}) copy-start(bf16[2,128,128]{2,1,0:T(8,128)(2,1)} %filter_out.5) | copy-start | bytes 196612
  37.7 7.7 %collective-permute-start.5 = (bf16[128,128]{1,0:T(8,128)(2,1)S(1)}, bf16[128,128]{1,0:T(8,128)(2,1)S(1)}, u32[]{:S(2)}, u32[]{:S(2)}) collective-permute-start(bf16[128,128]{1,0:T(8,128)(2,1)S(1)} %get-tuple-element.50), channel_id=1, source_target_pairs={{266,298},{298,266},{394,426},{426,394},{386,418},{418,386},{258,2... | collective-permute-start | bytes 98312 | tf_op jit(solution)/shard_map/ppermute | solution.py:64
  42.9 5.4 %collective-permute-start.6 = (bf16[128,128]{1,0:T(8,128)(2,1)S(1)}, bf16[128,128]{1,0:T(8,128)(2,1)S(1)}, u32[]{:S(2)}, u32[]{:S(2)}) collective-permute-start(bf16[128,128]{1,0:T(8,128)(2,1)S(1)} %get-tuple-element.51), channel_id=1, source_target_pairs={{266,306},{298,394},{394,298},{426,386},{386,426},{418,258},{258,4... | collective-permute-start | bytes 98312 | tf_op jit(solution)/shard_map/ppermute | solution.py:64
  45.3 11.8 %copy-start.4 = (f32[1,3,128]{2,0,1:T(1,128)S(1)}, f32[1,3,128]{2,0,1:T(1,128)}, u32[]{:S(2)}) copy-start(f32[1,3,128]{2,0,1:T(1,128)} %param.16) | copy-start | bytes 4612
  48.2 47.0 %copy-start.5 = (f32[1,3,128]{2,0,1:T(1,128)S(1)}, f32[1,3,128]{2,0,1:T(1,128)}, u32[]{:S(2)}) copy-start(f32[1,3,128]{2,0,1:T(1,128)} %param.15) | copy-start | bytes 4612
  48.2 47.0 %copy-start.6 = (f32[8,128]{1,0:T(8,128)S(1)}, f32[8,128]{1,0:T(8,128)}, u32[]{:S(2)}) copy-start(f32[8,128]{1,0:T(8,128)} %get-tuple-element.63.settings) | copy-start | bytes 12292
  49.9 4.9 %collective-permute-start.7 = (f32[8,128]{1,0:T(8,128)S(1)}, f32[8,128]{1,0:T(8,128)S(1)}, u32[]{:S(2)}, u32[]{:S(2)}) collective-permute-start(f32[8,128]{1,0:T(8,128)S(1)} %get-tuple-element.59), channel_id=1, source_target_pairs={{266,298},{298,266},{394,426},{426,394},{386,418},{418,386},{258,2... | collective-permute-start | bytes 12296 | tf_op jit(solution)/shard_map/ppermute | solution.py:64
  52.2 4.9 %collective-permute-start.8 = (f32[8,128]{1,0:T(8,128)S(1)}, f32[8,128]{1,0:T(8,128)S(1)}, u32[]{:S(2)}, u32[]{:S(2)}) collective-permute-start(f32[8,128]{1,0:T(8,128)S(1)} %get-tuple-element.60), channel_id=1, source_target_pairs={{266,306},{298,394},{394,298},{426,386},{386,426},{418,258},{258,4... | collective-permute-start | bytes 12296 | tf_op jit(solution)/shard_map/ppermute | solution.py:64

commit v4 on v3

--- a/solution.py
+++ b/solution.py
@@ -28,6 +28,7 @@
 ROW_NEAR = 160
 PACK_ROWS = 192
 HALO_ROWS = 160
+EXTRA = 16
 BLOCK = 5
 
 
@@ -124,6 +125,11 @@
 
 def flat(ref):
     return jnp.concatenate([ref[0], ref[1], ref[2]], axis=0)
+
+
+def spare(ref):
+    rows = ref.shape[0]
+    ref[rows - EXTRA : rows, :] = jnp.zeros((EXTRA, ATOMS), ref.dtype)
 
 
 def coords_of(block):
@@ -184,7 +190,10 @@
     ):
         hot = jnp.where(rows == ids, 1.0, 0.0).astype(BF16)
         chosen[...] = hot
-        send[...] = dot(block, hot).astype(BF16)
+        send[0:HALO_ROWS, :] = dot(block, hot).astype(BF16)
+
+
+    spare(send_b)
 
 
 def slots_kernel(pack, hot, own):
@@ -207,7 +216,7 @@
     shift = jnp.where(domain == 0, -DOMAINS, jnp.where(domain == DOMAINS - 1, DOMAINS, 0)).astype(F32)
     own = coords_of(pack[0:HALO_ROWS, :])
     first = lax.broadcasted_iota(jnp.int32, (8, ATOMS), 0) == 0
-    far = coords_of(from_b[...]) + jnp.where(first, shift, 0.0)
+    far = coords_of(from_b[0:HALO_ROWS, :]) + jnp.where(first, shift, 0.0)
     far_rows = jnp.concatenate([p.astype(F32) for p in thirds(far)], axis=0).astype(BF16)
     ext_embed = jnp.concatenate([pack[0:CHANNELS, :], from_a[0:CHANNELS, :], from_b[0:CHANNELS, :]], axis=1)
     f32_rows = lambda ref: ref[ROW_POS:HALO_ROWS, :].astype(F32)
@@ -235,34 +244,36 @@
     hid = (pack[0:CHANNELS, :].astype(F32) + upd * gate(upd)).astype(BF16)
     hidden[...] = hid
     send_a[...] = dot(hid, list_a[...]).astype(BF16)
-    send_b[...] = dot(hid, list_b[...]).astype(BF16)
-
-
-def filters_kernel(pairs, in_t, out_t, slope_one, slope_two, filter_two):
+    send_b[0:CHANNELS, :] = dot(hid, list_b[...]).astype(BF16)
+    spare(send_b)
+
+
+def bend(pairs, in_t, layer, c, centre):
+    vec = pairs[:, chunk(c)]
+    sq = jnp.sum(vec * vec, axis=0, keepdims=True)
+    scaled = (sq - centre) * (1.0 / BASIS_WIDTH)
+    radial = jnp.exp(-scaled * scaled)
+    weight = in_t[layer * 128 : (layer + 1) * 128, 0 : 3 * BASIS]
+    half = dot(weight, stacked(radial))
+    change = dot(weight, stacked(radial * scaled * (-2.0 / BASIS_WIDTH)))
+    t = jnp.tanh(half)
+    bent = half * t
+    return half + bent, (1.0 + t) * (1.0 + half - bent) * change
+
+
+def filters_kernel(pairs, in_t, out_t, slope_two, filter_two):
     centre = centres()
     for c in range(CHUNKS):
-        vec = pairs[:, chunk(c)]
-        sq = jnp.sum(vec * vec, axis=0, keepdims=True)
-        scaled = (sq - centre) * (1.0 / BASIS_WIDTH)
-        radial = jnp.exp(-scaled * scaled)
-        tall = stacked(radial)
-        steep = stacked(radial * scaled * (-2.0 / BASIS_WIDTH))
-        for l, slope in ((0, slope_one), (1, slope_two)):
-            weight = in_t[l * 128 : (l + 1) * 128, 0 : 3 * BASIS]
-            half = dot(weight, tall)
-            change = dot(weight, steep)
-            t = jnp.tanh(half)
-            bent = half * t
-            slope[:, chunk(c)] = ((1.0 + t) * (1.0 + half - bent) * change).astype(slope.dtype)
-            if l == 1:
-                filter_two[:, chunk(c)] = dot(out_t[128:256, :], (half + bent).astype(BF16))
+        act, slope = bend(pairs, in_t, 1, c, centre)
+        slope_two[:, chunk(c)] = slope.astype(BF16)
+        filter_two[:, chunk(c)] = dot(out_t[128:256, :], act.astype(BF16))
 
 
 def second_kernel(
     hidden, from_a, from_b, hot, filter_two, update_t, update, read,
     energy, grad_two, rows_two, grad_own, grad_a, grad_b,
 ):
-    ext = jnp.concatenate([hidden[...], from_a[...], from_b[...]], axis=1)
+    ext = jnp.concatenate([hidden[...], from_a[...], from_b[0:CHANNELS, :]], axis=1)
     message = jnp.zeros((CHANNELS, ATOMS), F32)
     for c in range(CHUNKS):
         rows = dot(ext, hot[:, chunk(c)])
@@ -283,16 +294,19 @@
         total = total + dot_nt(part, hot[:, chunk(c)])
     grad_own[...] = total[:, 0:ATOMS]
     grad_a[...] = total[:, ATOMS : 2 * ATOMS].astype(BF16)
-    grad_b[...] = total[:, 2 * ATOMS :].astype(BF16)
-
-
-def slope_kernel(grad_two, rows_two, slope_two, filter_out, out):
+    grad_b[0:CHANNELS, :] = total[:, 2 * ATOMS :].astype(BF16)
+    spare(grad_b)
+
+
+def slope_kernel(grad_two, rows_two, slope_two, filter_out, pairs, in_t, out, slope_one):
+    centre = centres()
     wide = spread(grad_two[...])
     for c in range(CHUNKS):
         dfilt = (wide * rows_two[:, chunk(c)].astype(F32)).astype(BF16)
         dact = dot(filter_out[1], dfilt)
         part = jnp.sum(dact * slope_two[:, chunk(c)].astype(F32), axis=0, keepdims=True)
         out[:, chunk(c)] = jnp.broadcast_to(part, (8, CHUNK))
+        slope_one[:, chunk(c)] = bend(pairs, in_t, 0, c, centre)[1].astype(BF16)
 
 
 def third_kernel(
@@ -300,7 +314,7 @@
     filter_out, dsq_two, pairs, hot,
     force, send_a, send_b,
 ):
-    dhidden = grad_own[...] + dot_nt(from_a[...], list_a[...]) + dot_nt(from_b[...], list_b[...])
+    dhidden = grad_own[...] + dot_nt(from_a[...], list_a[...]) + dot_nt(from_b[0:CHANNELS, :], list_b[...])
     upd = update_one[...]
     g = gate(upd)
     dupd = (dhidden * (g + upd * g * (1.0 - g))).astype(BF16)
@@ -319,7 +333,8 @@
     ext = total[0:8] + total[8:16]
     force[...] = own - ext[:, 0:ATOMS]
     send_a[...] = -ext[:, ATOMS : 2 * ATOMS]
-    send_b[...] = -ext[:, 2 * ATOMS :]
+    send_b[0:8, :] = -ext[:, 2 * ATOMS :]
+    spare(send_b)
 
 
 def sums_kernel(force, from_a, from_b, list_a, list_b, own, energy, velocity, climb, out):
@@ -330,7 +345,7 @@
         got = dot_nt(both, chosen)
         return got[0:8] + got[8:16]
 
-    f = force[...] + returned(from_a[...], list_a[...]) + returned(from_b[...], list_b[...])
+    f = force[...] + returned(from_a[...], list_a[...]) + returned(from_b[0:8, :], list_b[...])
     speed = flat(velocity)
     movable = (image > 0) & (image < IMAGES - 1)
     speed_sq = jnp.where(movable, jnp.sum(speed * speed), 0.0)
@@ -460,6 +475,7 @@
 ):
     square = (ATOMS, ATOMS)
     wide = (CHANNELS, PAIRS)
+    longer = (CHANNELS + EXTRA, ATOMS)
     positions = positions.transpose(1, 0, 2)
     velocity = velocity.transpose(1, 0, 2)
     packed = pack_call(
@@ -479,47 +495,47 @@
     )
     list_a, list_b, send_a, send_b = call(
         lists_kernel,
-        [(square, BF16), (square, BF16), ((HALO_ROWS, ATOMS), BF16), ((HALO_ROWS, ATOMS), BF16)],
+        [(square, BF16), (square, BF16), ((HALO_ROWS, ATOMS), BF16), ((HALO_ROWS + EXTRA, ATOMS), BF16)],
         (pack,),
     )
-    from_a, from_b = move(send_a, SWAP_A), move(send_b, SWAP_B)
+    from_b, from_a = move(send_b, SWAP_B), move(send_a, SWAP_A)
     hot, own = call(slots_kernel, [((EXT, PAIRS), BF16), ((8, ATOMS), F32)], (pack,), flops=10**9)
     hidden, send_a, send_b, update_one, pairs, rows_one = call(
         first_kernel,
-        [(square, BF16), (square, BF16), (square, BF16), (square, F32), ((8, PAIRS), F32), (wide, BF16)],
+        [(square, BF16), (square, BF16), (longer, BF16), (square, F32), ((8, PAIRS), F32), (wide, BF16)],
         (pack, from_a, from_b, hot, list_a, list_b, in_t, out_t, update_t),
         flops=10**9,
     )
-    from_a, from_b = move(send_a, SWAP_A), move(send_b, SWAP_B)
-    slope_one, slope_two, filter_two = call(
+    from_b, from_a = move(send_b, SWAP_B), move(send_a, SWAP_A)
+    slope_two, filter_two = call(
         filters_kernel,
-        [(wide, BF16), (wide, BF16), (wide, F32)],
+        [(wide, BF16), (wide, F32)],
         (pairs, in_t, out_t),
         flops=10**9,
     )
     energy, grad_two, rows_two, grad_own, send_a, send_b = call(
         second_kernel,
-        [((8, ATOMS), F32), (square, F32), (wide, BF16), (square, F32), (square, BF16), (square, BF16)],
+        [((8, ATOMS), F32), (square, F32), (wide, BF16), (square, F32), (square, BF16), (longer, BF16)],
         (hidden, from_a, from_b, hot, filter_two, update_t, update_weight, read),
         flops=10**9,
     )
-    from_a, from_b = move(send_a, SWAP_A), move(send_b, SWAP_B)
-    (dsq_two,) = call(
+    from_b, from_a = move(send_b, SWAP_B), move(send_a, SWAP_A)
+    dsq_two, slope_one = call(
         slope_kernel,
-        [((8, PAIRS), F32)],
-        (grad_two, rows_two, slope_two, filter_out),
+        [((8, PAIRS), F32), (wide, BF16)],
+        (grad_two, rows_two, slope_two, filter_out, pairs, in_t),
         flops=10**9,
     )
     force, send_a, send_b = call(
         third_kernel,
-        [((8, ATOMS), F32)] * 3,
+        [((8, ATOMS), F32), ((8, ATOMS), F32), ((8 + EXTRA, ATOMS), F32)],
         (
             grad_own, from_a, from_b, list_a, list_b, update_one, update_weight, rows_one,
             slope_one, filter_out, dsq_two, pairs, hot,
         ),
         flops=10**9,
     )
-    from_a, from_b = move(send_a, SWAP_A), move(send_b, SWAP_B)
+    from_b, from_a = move(send_b, SWAP_B), move(send_a, SWAP_A)
     (blocks,) = call(
         sums_kernel,
         [((IMAGES * 8, ATOMS), F32)],

time: 96.7 us -> 92.7 us (0.959)
  waiting for transfers between devices: 7.72 us -> 0.38 us
  starting transfers between devices: 32.4 us -> 35.7 us
    ppermute x9, waiting for transfers between devices: 7.72 us -> 0.38 us  [move(): return lax.ppermute(values, AXES, pairs)]
    ppermute x9, starting transfers between devices: 32.4 us -> 35.7 us  [move(): return lax.ppermute(values, AXES, pairs)]
  transfers between devices with their start and end apart: 9 -> 9, of which waited for: 4 -> 1; matrix products, arithmetic and copies ran while one was open for 0% -> 0% of each run, Pallas kernels for 6% -> 6%
where the time goes in v4:
time: 92.7 us; the launch traced here: 92.1 us
  blocking collectives  37.6 us (41%)
  starting transfers between devices  35.7 us (39%)
  Pallas kernels  14.1 us (15%)
  between operations  4.13 us (4%)
    ppermute x9, starting transfers between devices, move(): return lax.ppermute(values, AXES, pairs)  35.7 us
    all_to_all x1, blocking collectives, per_device(): lax.all_to_all(blocks, AXES, 0, 0, tiled=True, axis_index_groups=COLUMNS)  22.2 us
    all_to_all x1, blocking collectives, per_device(): lax.all_to_all(blocks, AXES, 0, 0, tiled=True, axis_index_groups=LAYERS)  15.4 us
    pallas_call x11, Pallas kernels, call(): pl.pallas_call(kernel, out_shape=[jax.ShapeDtypeStruct(s, t) for s, t in...  12.6 us
  transfers between devices with their start and end apart: 9, of which 1 were waited for; matrix products, arithmetic and copies ran while one was open for 0% of the time, Pallas kernels for 6%

profile of v4, /device:TPU:1, one launch (start us, length us, event | category | flops | bytes accessed | tf_op | source)
XLA Modules:
  0.0 92.1 jit_solution(17808346423194017672)
XLA Ops:
  0.6 1.5 %pack_kernel.1.after = bf16[192,128]{1,0:T(8,128)(2,1)} custom-call(f32[3,1,128]{2,1,0:T(1,128)} %bitcast.20, bf16[128,128]{1,0:T(8,128)(2,1)} %embed_in.1, s32[32,128]{1,0:T(8,128)} %bitcast.22, s32[1,128]{1,0:T(1,128)} %bitcast.23, s32[1,128]{1,0:T(1,128)} %bitcast.24), custom_call_target="tpu_custom_call" | custom-call | tf_op jit(solution)/shard_map/pack_kernel/pallas_call | solution.py:460
  2.2 11.2 %collective-permute-start = (bf16[192,128]{1,0:T(8,128)(2,1)}, bf16[192,128]{1,0:T(8,128)(2,1)S(1)}, u32[]{:S(2)}, u32[]{:S(2)}) collective-permute-start(bf16[192,128]{1,0:T(8,128)(2,1)} %pack_kernel.1.after), channel_id=1, source_target_pairs={{0,266},{1,298},{2,394},{3,426},{4,386},{5,418},{6,258},{7,290},{8... | collective-permute-start | bytes 147464 | tf_op jit(solution)/shard_map/ppermute | solution.py:65
  16.0 1.7 %weights_kernel.1 = (bf16[256,128]{1,0:T(8,128)(2,1)}, bf16[256,128]{1,0:T(8,128)(2,1)}, bf16[256,128]{1,0:T(8,128)(2,1)}, f32[128,128]{1,0:T(8,128)}, f32[8,128]{1,0:T(8,128)}) custom-call(bf16[192,128]{1,0:T(8,128)(2,1)} %pack_kernel.1.after, f32[2,16,128]{2,1,0:T(8,128)} %filter_in.1, bf16[2,128,128]{2,1,0:T(8,128)(2,1)} %filter_out.5, ...), custom_call_target="tpu_custom_call" | custom-call | flops 100000000 | bytes 197136 | tf_op jit(solution)/shard_map/weights_kernel/pallas_call | solution.py:448
  17.7 0.0 copy-start.2
  17.7 0.0 copy-start.7
  17.7 0.0 collective-permute-done.pack
  17.7 0.2 lists_kernel.1
  17.9 1.9 %collective-permute-start.2 = (bf16[176,128]{1,0:T(8,128)(2,1)S(1)}, bf16[176,128]{1,0:T(8,128)(2,1)S(1)}, u32[]{:S(2)}, u32[]{:S(2)}) collective-permute-start(bf16[176,128]{1,0:T(8,128)(2,1)S(1)} %get-tuple-element.37), channel_id=1, source_target_pairs={{266,306},{298,394},{394,298},{426,386},{386,426},{418,258},{258,4... | collective-permute-start | bytes 135176 | tf_op jit(solution)/shard_map/ppermute | solution.py:65
  19.9 3.3 %collective-permute-start.1 = (bf16[160,128]{1,0:T(8,128)(2,1)S(1)}, bf16[160,128]{1,0:T(8,128)(2,1)S(1)}, u32[]{:S(2)}, u32[]{:S(2)}) collective-permute-start(bf16[160,128]{1,0:T(8,128)(2,1)S(1)} %get-tuple-element.36), channel_id=1, source_target_pairs={{266,298},{298,266},{394,426},{426,394},{386,418},{418,386},{258,2... | collective-permute-start | bytes 122888 | tf_op jit(solution)/shard_map/ppermute | solution.py:65
  23.1 1.0 %slots_kernel.1 = (bf16[384,4096]{1,0:T(8,128)(2,1)S(1)}, f32[8,128]{1,0:T(8,128)S(1)}) custom-call(bf16[192,128]{1,0:T(8,128)(2,1)S(1)} %collective-permute-done.pack), custom_call_target="tpu_custom_call" | custom-call | flops 1000000000 | bytes 49152 | tf_op jit(solution)/shard_map/slots_kernel/pallas_call | solution.py:448
  24.1 0.0 collective-permute-done.1.from_a
  24.2 0.0 collective-permute-done.2.from_b
  24.2 0.0 copy-done.2
  24.2 0.0 copy-done.7
  24.2 0.0 copy-done.8
  24.2 0.0 copy-start
  24.2 0.0 copy-start.3
  24.2 1.9 %first_kernel.1 = (bf16[128,128]{1,0:T(8,128)(2,1)S(1)}, bf16[128,128]{1,0:T(8,128)(2,1)S(1)}, bf16[144,128]{1,0:T(8,128)(2,1)S(1)}, f32[128,128]{1,0:T(8,128)S(...) custom-call(bf16[192,128]{1,0:T(8,128)(2,1)S(1)} %collective-permute-done.pack, ...), custom_call_target="tpu_custom_call" | custom-call | flops 1000000000 | bytes 3543040 | tf_op jit(solution)/shard_map/first_kernel/pallas_call | solution.py:448
  26.1 3.4 %collective-permute-start.4 = (bf16[144,128]{1,0:T(8,128)(2,1)S(1)}, bf16[144,128]{1,0:T(8,128)(2,1)S(1)}, u32[]{:S(2)}, u32[]{:S(2)}) collective-permute-start(bf16[144,128]{1,0:T(8,128)(2,1)S(1)} %get-tuple-element.46), channel_id=1, source_target_pairs={{266,306},{298,394},{394,298},{426,386},{386,426},{418,258},{258,4... | collective-permute-start | bytes 110600 | tf_op jit(solution)/shard_map/ppermute | solution.py:65
  29.5 6.5 %collective-permute-start.3 = (bf16[128,128]{1,0:T(8,128)(2,1)S(1)}, bf16[128,128]{1,0:T(8,128)(2,1)S(1)}, u32[]{:S(2)}, u32[]{:S(2)}) collective-permute-start(bf16[128,128]{1,0:T(8,128)(2,1)S(1)} %get-tuple-element.45), channel_id=1, source_target_pairs={{266,298},{298,266},{394,426},{426,394},{386,418},{418,386},{258,2... | collective-permute-start | bytes 98312 | tf_op jit(solution)/shard_map/ppermute | solution.py:65
  36.0 1.4 %filters_kernel.1 = (bf16[128,4096]{1,0:T(8,128)(2,1)S(1)}, f32[128,4096]{1,0:T(8,128)S(1)}) custom-call(f32[8,4096]{1,0:T(8,128)S(1)} %get-tuple-element.47.pairs, bf16[256,128]{1,0:T(8,128)(2,1)S(1)} %copy-done.7, bf16[256,128]{1,0:T(8,128)(2,1)S(1)} %copy-done.8), custom_call_target="tpu_custom_call" | custom-call | flops 1000000000 | bytes 262144 | tf_op jit(solution)/shard_map/filters_kernel/pallas_call | solution.py:448
  37.4 0.0 collective-permute-done.3.from_a
  37.4 0.0 collective-permute-done.4.from_b
  37.4 0.0 copy-done
  37.4 0.0 copy-done.3
  37.4 2.1 %second_kernel.1 = (f32[8,128]{1,0:T(8,128)S(1)}, f32[128,128]{1,0:T(8,128)S(1)}, bf16[128,4096]{1,0:T(8,128)(2,1)S(1)}, f32[128,128]{1,0:T(8,128)S(1)}, bf16[12...) custom-call(bf16[128,128]{1,0:T(8,128)(2,1)S(1)} %get-tuple-element.44.hidden, ...), custom_call_target="tpu_custom_call" | custom-call | flops 1000000000 | bytes 5541888 | tf_op jit(solution)/shard_map/second_kernel/pallas_call | solution.py:448
  39.5 1.9 %collective-permute-start.6 = (bf16[144,128]{1,0:T(8,128)(2,1)S(1)}, bf16[144,128]{1,0:T(8,128)(2,1)S(1)}, u32[]{:S(2)}, u32[]{:S(2)}) collective-permute-start(bf16[144,128]{1,0:T(8,128)(2,1)S(1)} %get-tuple-element.52), channel_id=1, source_target_pairs={{266,306},{298,394},{394,298},{426,386},{386,426},{418,258},{258,4... | collective-permute-start | bytes 110600 | tf_op jit(solution)/shard_map/ppermute | solution.py:65
  41.4 2.4 %collective-permute-start.5 = (bf16[128,128]{1,0:T(8,128)(2,1)S(1)}, bf16[128,128]{1,0:T(8,128)(2,1)S(1)}, u32[]{:S(2)}, u32[]{:S(2)}) collective-permute-start(bf16[128,128]{1,0:T(8,128)(2,1)S(1)} %get-tuple-element.51), channel_id=1, source_target_pairs={{266,298},{298,266},{394,426},{426,394},{386,418},{418,386},{258,2... | collective-permute-start | bytes 98312 | tf_op jit(solution)/shard_map/ppermute | solution.py:65
  43.8 0.0 copy-done.1
  43.8 1.5 %slope_kernel.1 = (f32[8,4096]{1,0:T(8,128)S(1)}, bf16[128,4096]{1,0:T(8,128)(2,1)S(1)}) custom-call(f32[128,128]{1,0:T(8,128)S(1)} %get-tuple-element.55.grad_two, bf16[128,4096]{1,0:T(8,128)(2,1)S(1)} %get-tuple-element.56.rows_two, bf16[128,4096]{1,0:T(8,128)(2,1)S(1)} %get-tuple-element.57.slope_two, bf16[2,128,128]{2,1,0:T(8,128)(2,1)S(1)} %copy-done.1, ...), custom_call_target="tpu_custom_call" | custom-call | flops 1000000000 | bytes 2424832 | tf_op jit(solution)/shard_map/slope_kernel/pallas_call | solution.py:448
  45.3 0.0 copy-start.4
  45.3 0.0 collective-permute-done.5.from_a
  45.3 0.0 collective-permute-done.6.from_b
  45.3 0.0 copy-start.5
  45.3 0.0 copy-start.6
  45.4 1.6 %third_kernel.1 = (f32[8,128]{1,0:T(8,128)S(1)}, f32[8,128]{1,0:T(8,128)S(1)}, f32[24,128]{1,0:T(8,128)S(1)}) custom-call(f32[128,128]{1,0:T(8,128)S(1)} %get-tuple-element.50.grad_own, bf16[128,128]{1,0:T(8,128)(2,1)S(1)} %collective-permute-done.5.from_a, bf16[144,128]{1,0:T(8,128)(2,1)S(1)} %collective-permute-done.6.from_b, ...), custom_call_target="tpu_custom_call" | custom-call | flops 1000000000 | bytes 5902336 | tf_op jit(solution)/shard_map/third_kernel/pallas_call | solution.py:448
  47.0 3.2 %collective-permute-start.8 = (f32[24,128]{1,0:T(8,128)S(1)}, f32[24,128]{1,0:T(8,128)S(1)}, u32[]{:S(2)}, u32[]{:S(2)}) collective-permute-start(f32[24,128]{1,0:T(8,128)S(1)} %get-tuple-element.62), channel_id=1, source_target_pairs={{266,306},{298,394},{394,298},{426,386},{386,426},{418,258},{258,4... | collective-permute-start | bytes 36872 | tf_op jit(solution)/shard_map/ppermute | solution.py:65
  50.2 2.0 %collective-permute-start.7 = (f32[8,128]{1,0:T(8,128)S(1)}, f32[8,128]{1,0:T(8,128)S(1)}, u32[]{:S(2)}, u32[]{:S(2)}) collective-permute-start(f32[8,128]{1,0:T(8,128)S(1)} %get-tuple-element.61), channel_id=1, source_target_pairs={{266,298},{298,266},{394,426},{426,394},{386,418},{418,386},{258,2... | collective-permute-start | bytes 12296 | tf_op jit(solution)/shard_map/ppermute | solution.py:65
  52.9 0.4 collective-permute-done.7.from_a
  53.3 0.0 collective-permute-done.8.from_b
  53.3 0.0 copy-done.4
  53.3 0.2 sums_kernel.1
  53.4 22.2 %all_to_all.16 = f32[16,8,128]{2,1,0:T(8,128)S(1)} all-to-all(f32[16,8,128]{2,1,0:T(8,128)S(1)} %bitcast.17), channel_id=1, replica_groups={{266,267,330,331,264,265,328,329,270,271,334,335,268,269,332,333},{298,..., dimensions={0} | all-to-all | bytes 131072 | tf_op jit(solution)/shard_map/all_to_all | solution.py:545
  75.7 0.1 column_kernel.1
  75.8 15.4 %all_to_all.17.blocks = f32[160,2,128]{2,1,0:T(2,128)S(1)} all-to-all(f32[160,2,128]{2,1,0:T(2,128)S(1)} %column_kernel.1), channel_id=1, replica_groups={{266,298,394,426,386,418,258,290,130,162,2,34,10,42,138,170,146,178,18,..., dimensions={0} | all-to-all | bytes 327680 | tf_op jit(solution)/shard_map/all_to_all | solution.py:547
  91.2 0.0 copy-done.5
  91.2 0.0 copy-done.6
  91.2 0.8 final_kernel.1
  (2 shorter events, 0.0 us)
Async XLA Ops:
  2.2 15.6 %collective-permute-start = (bf16[192,128]{1,0:T(8,128)(2,1)}, bf16[192,128]{1,0:T(8,128)(2,1)S(1)}, u32[]{:S(2)}, u32[]{:S(2)}) collective-permute-start(bf16[192,128]{1,0:T(8,128)(2,1)} %pack_kernel.1.after), channel_id=1, source_target_pairs={{0,266},{1,298},{2,394},{3,426},{4,386},{5,418},{6,258},{7,290},{8... | collective-permute-start | bytes 147464 | tf_op jit(solution)/shard_map/ppermute | solution.py:65
  17.7 6.4 %copy-start.2 = (bf16[256,128]{1,0:T(8,128)(2,1)S(1)}, bf16[256,128]{1,0:T(8,128)(2,1)}, u32[]{:S(2)}) copy-start(bf16[256,128]{1,0:T(8,128)(2,1)} %get-tuple-element.43.update_t) | copy-start | bytes 196612
  17.7 6.5 %copy-start.7 = (bf16[256,128]{1,0:T(8,128)(2,1)S(1)}, bf16[256,128]{1,0:T(8,128)(2,1)}, u32[]{:S(2)}) copy-start(bf16[256,128]{1,0:T(8,128)(2,1)} %get-tuple-element.41.in_t) | copy-start | bytes 196612
  17.7 6.5 %copy-start.8 = (bf16[256,128]{1,0:T(8,128)(2,1)S(1)}, bf16[256,128]{1,0:T(8,128)(2,1)}, u32[]{:S(2)}) copy-start(bf16[256,128]{1,0:T(8,128)(2,1)} %get-tuple-element.42.out_t) | copy-start | bytes 196612
  17.9 6.2 %collective-permute-start.2 = (bf16[176,128]{1,0:T(8,128)(2,1)S(1)}, bf16[176,128]{1,0:T(8,128)(2,1)S(1)}, u32[]{:S(2)}, u32[]{:S(2)}) collective-permute-start(bf16[176,128]{1,0:T(8,128)(2,1)S(1)} %get-tuple-element.37), channel_id=1, source_target_pairs={{266,306},{298,394},{394,298},{426,386},{386,426},{418,258},{258,4... | collective-permute-start | bytes 135176 | tf_op jit(solution)/shard_map/ppermute | solution.py:65
  19.9 4.3 %collective-permute-start.1 = (bf16[160,128]{1,0:T(8,128)(2,1)S(1)}, bf16[160,128]{1,0:T(8,128)(2,1)S(1)}, u32[]{:S(2)}, u32[]{:S(2)}) collective-permute-start(bf16[160,128]{1,0:T(8,128)(2,1)S(1)} %get-tuple-element.36), channel_id=1, source_target_pairs={{266,298},{298,266},{394,426},{426,394},{386,418},{418,386},{258,2... | collective-permute-start | bytes 122888 | tf_op jit(solution)/shard_map/ppermute | solution.py:65
  24.2 13.2 %copy-start = (bf16[2,128,128]{2,1,0:T(8,128)(2,1)S(1)}, bf16[2,128,128]{2,1,0:T(8,128)(2,1)}, u32[]{:S(2)}) copy-start(bf16[2,128,128]{2,1,0:T(8,128)(2,1)} %update.5) | copy-start | bytes 196612
  24.2 13.2 %copy-start.3 = (f32[128,128]{1,0:T(8,128)S(1)}, f32[128,128]{1,0:T(8,128)}, u32[]{:S(2)}) copy-start(f32[128,128]{1,0:T(8,128)} %get-tuple-element.49.read) | copy-start | bytes 196612
  26.1 11.3 %collective-permute-start.4 = (bf16[144,128]{1,0:T(8,128)(2,1)S(1)}, bf16[144,128]{1,0:T(8,128)(2,1)S(1)}, u32[]{:S(2)}, u32[]{:S(2)}) collective-permute-start(bf16[144,128]{1,0:T(8,128)(2,1)S(1)} %get-tuple-element.46), channel_id=1, source_target_pairs={{266,306},{298,394},{394,298},{426,386},{386,426},{418,258},{258,4... | collective-permute-start | bytes 110600 | tf_op jit(solution)/shard_map/ppermute | solution.py:65
  29.5 7.9 %collective-permute-start.3 = (bf16[128,128]{1,0:T(8,128)(2,1)S(1)}, bf16[128,128]{1,0:T(8,128)(2,1)S(1)}, u32[]{:S(2)}, u32[]{:S(2)}) collective-permute-start(bf16[128,128]{1,0:T(8,128)(2,1)S(1)} %get-tuple-element.45), channel_id=1, source_target_pairs={{266,298},{298,266},{394,426},{426,394},{386,418},{418,386},{258,2... | collective-permute-start | bytes 98312 | tf_op jit(solution)/shard_map/ppermute | solution.py:65
  37.4 6.4 %copy-start.1 = (bf16[2,128,128]{2,1,0:T(8,128)(2,1)S(1)}, bf16[2,128,128]{2,1,0:T(8,128)(2,1)}, u32[]{:S(2)}) copy-start(bf16[2,128,128]{2,1,0:T(8,128)(2,1)} %filter_out.5) | copy-start | bytes 196612
  39.5 5.8 %collective-permute-start.6 = (bf16[144,128]{1,0:T(8,128)(2,1)S(1)}, bf16[144,128]{1,0:T(8,128)(2,1)S(1)}, u32[]{:S(2)}, u32[]{:S(2)}) collective-permute-start(bf16[144,128]{1,0:T(8,128)(2,1)S(1)} %get-tuple-element.52), channel_id=1, source_target_pairs={{266,306},{298,394},{394,298},{426,386},{386,426},{418,258},{258,4... | collective-permute-start | bytes 110600 | tf_op jit(solution)/shard_map/ppermute | solution.py:65
  41.4 3.9 %collective-permute-start.5 = (bf16[128,128]{1,0:T(8,128)(2,1)S(1)}, bf16[128,128]{1,0:T(8,128)(2,1)S(1)}, u32[]{:S(2)}, u32[]{:S(2)}) collective-permute-start(bf16[128,128]{1,0:T(8,128)(2,1)S(1)} %get-tuple-element.51), channel_id=1, source_target_pairs={{266,298},{298,266},{394,426},{426,394},{386,418},{418,386},{258,2... | collective-permute-start | bytes 98312 | tf_op jit(solution)/shard_map/ppermute | solution.py:65
  45.3 8.0 %copy-start.4 = (f32[1,3,128]{2,0,1:T(1,128)S(1)}, f32[1,3,128]{2,0,1:T(1,128)}, u32[]{:S(2)}) copy-start(f32[1,3,128]{2,0,1:T(1,128)} %param.16) | copy-start | bytes 4612
  45.3 45.9 %copy-start.5 = (f32[1,3,128]{2,0,1:T(1,128)S(1)}, f32[1,3,128]{2,0,1:T(1,128)}, u32[]{:S(2)}) copy-start(f32[1,3,128]{2,0,1:T(1,128)} %param.15) | copy-start | bytes 4612
  45.3 45.9 %copy-start.6 = (f32[8,128]{1,0:T(8,128)S(1)}, f32[8,128]{1,0:T(8,128)}, u32[]{:S(2)}) copy-start(f32[8,128]{1,0:T(8,128)} %get-tuple-element.65.settings) | copy-start | bytes 12292
  47.0 6.3 %collective-permute-start.8 = (f32[24,128]{1,0:T(8,128)S(1)}, f32[24,128]{1,0:T(8,128)S(1)}, u32[]{:S(2)}, u32[]{:S(2)}) collective-permute-start(f32[24,128]{1,0:T(8,128)S(1)} %get-tuple-element.62), channel_id=1, source_target_pairs={{266,306},{298,394},{394,298},{426,386},{386,426},{418,258},{258,4... | collective-permute-start | bytes 36872 | tf_op jit(solution)/shard_map/ppermute | solution.py:65
  50.2 3.1 %collective-permute-start.7 = (f32[8,128]{1,0:T(8,128)S(1)}, f32[8,128]{1,0:T(8,128)S(1)}, u32[]{:S(2)}, u32[]{:S(2)}) collective-permute-start(f32[8,128]{1,0:T(8,128)S(1)} %get-tuple-element.61), channel_id=1, source_target_pairs={{266,298},{298,266},{394,426},{426,394},{386,418},{418,386},{258,2... | collective-permute-start | bytes 12296 | tf_op jit(solution)/shard_map/ppermute | solution.py:65

commit v5 on v4

--- a/solution.py
+++ b/solution.py
@@ -298,20 +298,22 @@
     spare(grad_b)
 
 
-def slope_kernel(grad_two, rows_two, slope_two, filter_out, pairs, in_t, out, slope_one):
+def slope_kernel(
+    grad_two, rows_two, slope_two, filter_out, pairs, in_t, out_t, rows_one, out, pull_one
+):
     centre = centres()
-    wide = spread(grad_two[...])
+    wide = spread(grad_two[...].astype(BF16))
     for c in range(CHUNKS):
-        dfilt = (wide * rows_two[:, chunk(c)].astype(F32)).astype(BF16)
+        dfilt = wide * rows_two[:, chunk(c)]
         dact = dot(filter_out[1], dfilt)
         part = jnp.sum(dact * slope_two[:, chunk(c)].astype(F32), axis=0, keepdims=True)
         out[:, chunk(c)] = jnp.broadcast_to(part, (8, CHUNK))
-        slope_one[:, chunk(c)] = bend(pairs, in_t, 0, c, centre)[1].astype(BF16)
+        turned = dot(out_t[0:128, :], bend(pairs, in_t, 0, c, centre)[1].astype(BF16))
+        pull_one[:, chunk(c)] = turned * rows_one[:, chunk(c)].astype(F32)
 
 
 def third_kernel(
-    grad_own, from_a, from_b, list_a, list_b, update_one, update, rows_one, slope_one,
-    filter_out, dsq_two, pairs, hot,
+    grad_own, from_a, from_b, list_a, list_b, update_one, update, pull_one, dsq_two, pairs, hot,
     force, send_a, send_b,
 ):
     dhidden = grad_own[...] + dot_nt(from_a[...], list_a[...]) + dot_nt(from_b[0:CHANNELS, :], list_b[...])
@@ -322,9 +324,7 @@
     own = jnp.zeros((8, ATOMS), F32)
     total = jnp.zeros((16, EXT), F32)
     for c in range(CHUNKS):
-        dfilt = (wide * rows_one[:, chunk(c)].astype(F32)).astype(BF16)
-        dact = dot(filter_out[0], dfilt)
-        part = jnp.sum(dact * slope_one[:, chunk(c)].astype(F32), axis=0, keepdims=True)
+        part = jnp.sum(wide * pull_one[:, chunk(c)], axis=0, keepdims=True)
         pull = 2.0 * (part + dsq_two[:, chunk(c)]) * pairs[:, chunk(c)]
         own = own + fold(pull)
         high, low = halves(pull)
@@ -520,18 +520,18 @@
         flops=10**9,
     )
     from_b, from_a = move(send_b, SWAP_B), move(send_a, SWAP_A)
-    dsq_two, slope_one = call(
+    dsq_two, pull_one = call(
         slope_kernel,
-        [((8, PAIRS), F32), (wide, BF16)],
-        (grad_two, rows_two, slope_two, filter_out, pairs, in_t),
+        [((8, PAIRS), F32), (wide, F32)],
+        (grad_two, rows_two, slope_two, filter_out, pairs, in_t, out_t, rows_one),
         flops=10**9,
     )
     force, send_a, send_b = call(
         third_kernel,
         [((8, ATOMS), F32), ((8, ATOMS), F32), ((8 + EXTRA, ATOMS), F32)],
         (
-            grad_own, from_a, from_b, list_a, list_b, update_one, update_weight, rows_one,
-            slope_one, filter_out, dsq_two, pairs, hot,
+            grad_own, from_a, from_b, list_a, list_b, update_one, update_weight,
+            pull_one, dsq_two, pairs, hot,
         ),
         flops=10**9,
     )

time: 92.7 us -> 92.6 us (level)
  no operation moved by 1% of the time
where the time goes in v5:
time: 92.6 us; the launch traced here: 92 us
  blocking collectives  37.6 us (41%)
  starting transfers between devices  35.9 us (39%)
  Pallas kernels  13.9 us (15%)
  between operations  4.13 us (4%)
    ppermute x9, starting transfers between devices, move(): return lax.ppermute(values, AXES, pairs)  35.9 us
    all_to_all x1, blocking collectives, per_device(): lax.all_to_all(blocks, AXES, 0, 0, tiled=True, axis_index_groups=COLUMNS)  22.2 us
    all_to_all x1, blocking collectives, per_device(): lax.all_to_all(blocks, AXES, 0, 0, tiled=True, axis_index_groups=LAYERS)  15.4 us
    pallas_call x11, Pallas kernels, call(): pl.pallas_call(kernel, out_shape=[jax.ShapeDtypeStruct(s, t) for s, t in...  12.3 us
  transfers between devices with their start and end apart: 9, of which 1 were waited for; matrix products, arithmetic and copies ran while one was open for 0% of the time, Pallas kernels for 6%

profile of v5, /device:TPU:1, one launch (start us, length us, event | category | flops | bytes accessed | tf_op | source)
XLA Modules:
  0.0 92.0 jit_solution(17808273202743011511)
XLA Ops:
  0.6 1.5 %pack_kernel.1.after = bf16[192,128]{1,0:T(8,128)(2,1)} custom-call(f32[3,1,128]{2,1,0:T(1,128)} %bitcast.20, bf16[128,128]{1,0:T(8,128)(2,1)} %embed_in.1, s32[32,128]{1,0:T(8,128)} %bitcast.22, s32[1,128]{1,0:T(1,128)} %bitcast.23, s32[1,128]{1,0:T(1,128)} %bitcast.24), custom_call_target="tpu_custom_call" | custom-call | tf_op jit(solution)/shard_map/pack_kernel/pallas_call | solution.py:460
  2.2 11.2 %collective-permute-start = (bf16[192,128]{1,0:T(8,128)(2,1)}, bf16[192,128]{1,0:T(8,128)(2,1)S(1)}, u32[]{:S(2)}, u32[]{:S(2)}) collective-permute-start(bf16[192,128]{1,0:T(8,128)(2,1)} %pack_kernel.1.after), channel_id=1, source_target_pairs={{0,266},{1,298},{2,394},{3,426},{4,386},{5,418},{6,258},{7,290},{8... | collective-permute-start | bytes 147464 | tf_op jit(solution)/shard_map/ppermute | solution.py:65
  16.0 1.7 %weights_kernel.1 = (bf16[256,128]{1,0:T(8,128)(2,1)}, bf16[256,128]{1,0:T(8,128)(2,1)}, bf16[256,128]{1,0:T(8,128)(2,1)}, f32[128,128]{1,0:T(8,128)}, f32[8,128]{1,0:T(8,128)}) custom-call(bf16[192,128]{1,0:T(8,128)(2,1)} %pack_kernel.1.after, f32[2,16,128]{2,1,0:T(8,128)} %filter_in.1, bf16[2,128,128]{2,1,0:T(8,128)(2,1)} %filter_out.3, ...), custom_call_target="tpu_custom_call" | custom-call | flops 100000000 | bytes 197136 | tf_op jit(solution)/shard_map/weights_kernel/pallas_call | solution.py:448
  17.7 0.0 copy-start.1
  17.7 0.0 copy-start.7
  17.7 0.0 collective-permute-done.pack
  17.7 0.2 lists_kernel.1
  17.9 1.9 %collective-permute-start.2 = (bf16[176,128]{1,0:T(8,128)(2,1)S(1)}, bf16[176,128]{1,0:T(8,128)(2,1)S(1)}, u32[]{:S(2)}, u32[]{:S(2)}) collective-permute-start(bf16[176,128]{1,0:T(8,128)(2,1)S(1)} %get-tuple-element.37), channel_id=1, source_target_pairs={{266,306},{298,394},{394,298},{426,386},{386,426},{418,258},{258,4... | collective-permute-start | bytes 135176 | tf_op jit(solution)/shard_map/ppermute | solution.py:65
  19.9 3.3 %collective-permute-start.1 = (bf16[160,128]{1,0:T(8,128)(2,1)S(1)}, bf16[160,128]{1,0:T(8,128)(2,1)S(1)}, u32[]{:S(2)}, u32[]{:S(2)}) collective-permute-start(bf16[160,128]{1,0:T(8,128)(2,1)S(1)} %get-tuple-element.36), channel_id=1, source_target_pairs={{266,298},{298,266},{394,426},{426,394},{386,418},{418,386},{258,2... | collective-permute-start | bytes 122888 | tf_op jit(solution)/shard_map/ppermute | solution.py:65
  23.1 1.0 %slots_kernel.1 = (bf16[384,4096]{1,0:T(8,128)(2,1)S(1)}, f32[8,128]{1,0:T(8,128)S(1)}) custom-call(bf16[192,128]{1,0:T(8,128)(2,1)S(1)} %collective-permute-done.pack), custom_call_target="tpu_custom_call" | custom-call | flops 1000000000 | bytes 49152 | tf_op jit(solution)/shard_map/slots_kernel/pallas_call | solution.py:448
  24.1 0.0 collective-permute-done.1.from_a
  24.2 0.0 collective-permute-done.2.from_b
  24.2 0.0 copy-done.1
  24.2 0.0 copy-done.7
  24.2 0.0 copy-done.8
  24.2 1.9 %first_kernel.1 = (bf16[128,128]{1,0:T(8,128)(2,1)S(1)}, bf16[128,128]{1,0:T(8,128)(2,1)S(1)}, bf16[144,128]{1,0:T(8,128)(2,1)S(1)}, f32[128,128]{1,0:T(8,128)S(...) custom-call(bf16[192,128]{1,0:T(8,128)(2,1)S(1)} %collective-permute-done.pack, ...), custom_call_target="tpu_custom_call" | custom-call | flops 1000000000 | bytes 3543040 | tf_op jit(solution)/shard_map/first_kernel/pallas_call | solution.py:448
  26.1 0.0 copy-start.2
  26.1 3.5 %collective-permute-start.4 = (bf16[144,128]{1,0:T(8,128)(2,1)S(1)}, bf16[144,128]{1,0:T(8,128)(2,1)S(1)}, u32[]{:S(2)}, u32[]{:S(2)}) collective-permute-start(bf16[144,128]{1,0:T(8,128)(2,1)S(1)} %get-tuple-element.46), channel_id=1, source_target_pairs={{266,306},{298,394},{394,298},{426,386},{386,426},{418,258},{258,4... | collective-permute-start | bytes 110600 | tf_op jit(solution)/shard_map/ppermute | solution.py:65
  29.6 6.5 %collective-permute-start.3 = (bf16[128,128]{1,0:T(8,128)(2,1)S(1)}, bf16[128,128]{1,0:T(8,128)(2,1)S(1)}, u32[]{:S(2)}, u32[]{:S(2)}) collective-permute-start(bf16[128,128]{1,0:T(8,128)(2,1)S(1)} %get-tuple-element.45), channel_id=1, source_target_pairs={{266,298},{298,266},{394,426},{426,394},{386,418},{418,386},{258,2... | collective-permute-start | bytes 98312 | tf_op jit(solution)/shard_map/ppermute | solution.py:65
  36.1 1.4 %filters_kernel.1 = (bf16[128,4096]{1,0:T(8,128)(2,1)S(1)}, f32[128,4096]{1,0:T(8,128)S(1)}) custom-call(f32[8,4096]{1,0:T(8,128)S(1)} %get-tuple-element.47.pairs, bf16[256,128]{1,0:T(8,128)(2,1)S(1)} %copy-done.7, bf16[256,128]{1,0:T(8,128)(2,1)S(1)} %copy-done.8), custom_call_target="tpu_custom_call" | custom-call | flops 1000000000 | bytes 262144 | tf_op jit(solution)/shard_map/filters_kernel/pallas_call | solution.py:448
  37.5 0.0 collective-permute-done.3.from_a
  37.5 0.0 collective-permute-done.4.from_b
  37.5 0.0 copy-done
  37.5 0.0 copy-done.2
  37.5 0.0 copy-start.6
  37.6 2.1 %second_kernel.1 = (f32[8,128]{1,0:T(8,128)S(1)}, f32[128,128]{1,0:T(8,128)S(1)}, bf16[128,4096]{1,0:T(8,128)(2,1)S(1)}, f32[128,128]{1,0:T(8,128)S(1)}, bf16[12...) custom-call(bf16[128,128]{1,0:T(8,128)(2,1)S(1)} %get-tuple-element.44.hidden, ...), custom_call_target="tpu_custom_call" | custom-call | flops 1000000000 | bytes 5541888 | tf_op jit(solution)/shard_map/second_kernel/pallas_call | solution.py:448
  39.6 1.9 %collective-permute-start.6 = (bf16[144,128]{1,0:T(8,128)(2,1)S(1)}, bf16[144,128]{1,0:T(8,128)(2,1)S(1)}, u32[]{:S(2)}, u32[]{:S(2)}) collective-permute-start(bf16[144,128]{1,0:T(8,128)(2,1)S(1)} %get-tuple-element.52), channel_id=1, source_target_pairs={{266,306},{298,394},{394,298},{426,386},{386,426},{418,258},{258,4... | collective-permute-start | bytes 110600 | tf_op jit(solution)/shard_map/ppermute | solution.py:65
  41.6 2.4 %collective-permute-start.5 = (bf16[128,128]{1,0:T(8,128)(2,1)S(1)}, bf16[128,128]{1,0:T(8,128)(2,1)S(1)}, u32[]{:S(2)}, u32[]{:S(2)}) collective-permute-start(bf16[128,128]{1,0:T(8,128)(2,1)S(1)} %get-tuple-element.51), channel_id=1, source_target_pairs={{266,298},{298,266},{394,426},{426,394},{386,418},{418,386},{258,2... | collective-permute-start | bytes 98312 | tf_op jit(solution)/shard_map/ppermute | solution.py:65
  43.9 0.0 copy-done.6
  44.0 1.6 %slope_kernel.1 = (f32[8,4096]{1,0:T(8,128)S(1)}, f32[128,4096]{1,0:T(8,128)S(1)}) custom-call(f32[128,128]{1,0:T(8,128)S(1)} %get-tuple-element.54.grad_two, bf16[128,4096]{1,0:T(8,128)(2,1)S(1)} %get-tuple-element.55.rows_two, bf16[128,4096]{1,0:T(8,128)(2,1)S(1)} %get-tuple-element.56.slope_two, bf16[2,128,128]{2,1,0:T(8,128)(2,1)S(1)} %copy-done.6, ...), custom_call_target="tpu_custom_call" | custom-call | flops 1000000000 | bytes 3538944 | tf_op jit(solution)/shard_map/slope_kernel/pallas_call | solution.py:448
  45.5 0.0 collective-permute-done.5.from_a
  45.5 0.0 collective-permute-done.6.from_b
  45.6 0.0 copy-start.3
  45.6 0.0 copy-start.4
  45.6 0.0 copy-start.5
  45.6 1.3 %third_kernel.1 = (f32[8,128]{1,0:T(8,128)S(1)}, f32[8,128]{1,0:T(8,128)S(1)}, f32[24,128]{1,0:T(8,128)S(1)}) custom-call(f32[128,128]{1,0:T(8,128)S(1)} %get-tuple-element.50.grad_own, bf16[128,128]{1,0:T(8,128)(2,1)S(1)} %collective-permute-done.5.from_a, bf16[144,128]{1,0:T(8,128)(2,1)S(1)} %collective-permute-done.6.from_b, ...), custom_call_target="tpu_custom_call" | custom-call | flops 1000000000 | bytes 5836800 | tf_op jit(solution)/shard_map/third_kernel/pallas_call | solution.py:448
  46.9 3.2 %collective-permute-start.8 = (f32[24,128]{1,0:T(8,128)S(1)}, f32[24,128]{1,0:T(8,128)S(1)}, u32[]{:S(2)}, u32[]{:S(2)}) collective-permute-start(f32[24,128]{1,0:T(8,128)S(1)} %get-tuple-element.62), channel_id=1, source_target_pairs={{266,306},{298,394},{394,298},{426,386},{386,426},{418,258},{258,4... | collective-permute-start | bytes 36872 | tf_op jit(solution)/shard_map/ppermute | solution.py:65
  50.1 2.1 %collective-permute-start.7 = (f32[8,128]{1,0:T(8,128)S(1)}, f32[8,128]{1,0:T(8,128)S(1)}, u32[]{:S(2)}, u32[]{:S(2)}) collective-permute-start(f32[8,128]{1,0:T(8,128)S(1)} %get-tuple-element.61), channel_id=1, source_target_pairs={{266,298},{298,266},{394,426},{426,394},{386,418},{418,386},{258,2... | collective-permute-start | bytes 12296 | tf_op jit(solution)/shard_map/ppermute | solution.py:65
  52.8 0.4 collective-permute-done.7.from_a
  53.2 0.0 collective-permute-done.8.from_b
  53.2 0.0 copy-done.3
  53.2 0.2 sums_kernel.1
  53.3 22.2 %all_to_all.16 = f32[16,8,128]{2,1,0:T(8,128)S(1)} all-to-all(f32[16,8,128]{2,1,0:T(8,128)S(1)} %bitcast.17), channel_id=1, replica_groups={{266,267,330,331,264,265,328,329,270,271,334,335,268,269,332,333},{298,..., dimensions={0} | all-to-all | bytes 131072 | tf_op jit(solution)/shard_map/all_to_all | solution.py:545
  75.6 0.1 column_kernel.1
  75.7 15.4 %all_to_all.17.blocks = f32[160,2,128]{2,1,0:T(2,128)S(1)} all-to-all(f32[160,2,128]{2,1,0:T(2,128)S(1)} %column_kernel.1), channel_id=1, replica_groups={{266,298,394,426,386,418,258,290,130,162,2,34,10,42,138,170,146,178,18,..., dimensions={0} | all-to-all | bytes 327680 | tf_op jit(solution)/shard_map/all_to_all | solution.py:547
  91.1 0.0 copy-done.4
  91.1 0.0 copy-done.5
  91.1 0.8 final_kernel.1
  (2 shorter events, 0.0 us)
Async XLA Ops:
  2.2 15.6 %collective-permute-start = (bf16[192,128]{1,0:T(8,128)(2,1)}, bf16[192,128]{1,0:T(8,128)(2,1)S(1)}, u32[]{:S(2)}, u32[]{:S(2)}) collective-permute-start(bf16[192,128]{1,0:T(8,128)(2,1)} %pack_kernel.1.after), channel_id=1, source_target_pairs={{0,266},{1,298},{2,394},{3,426},{4,386},{5,418},{6,258},{7,290},{8... | collective-permute-start | bytes 147464 | tf_op jit(solution)/shard_map/ppermute | solution.py:65
  17.7 6.4 %copy-start.1 = (bf16[256,128]{1,0:T(8,128)(2,1)S(1)}, bf16[256,128]{1,0:T(8,128)(2,1)}, u32[]{:S(2)}) copy-start(bf16[256,128]{1,0:T(8,128)(2,1)} %get-tuple-element.43.update_t) | copy-start | bytes 196612
  17.7 6.5 %copy-start.7 = (bf16[256,128]{1,0:T(8,128)(2,1)S(1)}, bf16[256,128]{1,0:T(8,128)(2,1)}, u32[]{:S(2)}) copy-start(bf16[256,128]{1,0:T(8,128)(2,1)} %get-tuple-element.41.in_t) | copy-start | bytes 196612
  17.7 6.5 %copy-start.8 = (bf16[256,128]{1,0:T(8,128)(2,1)S(1)}, bf16[256,128]{1,0:T(8,128)(2,1)}, u32[]{:S(2)}) copy-start(bf16[256,128]{1,0:T(8,128)(2,1)} %get-tuple-element.42.out_t) | copy-start | bytes 196612
  17.9 6.2 %collective-permute-start.2 = (bf16[176,128]{1,0:T(8,128)(2,1)S(1)}, bf16[176,128]{1,0:T(8,128)(2,1)S(1)}, u32[]{:S(2)}, u32[]{:S(2)}) collective-permute-start(bf16[176,128]{1,0:T(8,128)(2,1)S(1)} %get-tuple-element.37), channel_id=1, source_target_pairs={{266,306},{298,394},{394,298},{426,386},{386,426},{418,258},{258,4... | collective-permute-start | bytes 135176 | tf_op jit(solution)/shard_map/ppermute | solution.py:65
  19.9 4.3 %collective-permute-start.1 = (bf16[160,128]{1,0:T(8,128)(2,1)S(1)}, bf16[160,128]{1,0:T(8,128)(2,1)S(1)}, u32[]{:S(2)}, u32[]{:S(2)}) collective-permute-start(bf16[160,128]{1,0:T(8,128)(2,1)S(1)} %get-tuple-element.36), channel_id=1, source_target_pairs={{266,298},{298,266},{394,426},{426,394},{386,418},{418,386},{258,2... | collective-permute-start | bytes 122888 | tf_op jit(solution)/shard_map/ppermute | solution.py:65
  26.1 11.4 %copy-start = (bf16[2,128,128]{2,1,0:T(8,128)(2,1)S(1)}, bf16[2,128,128]{2,1,0:T(8,128)(2,1)}, u32[]{:S(2)}) copy-start(bf16[2,128,128]{2,1,0:T(8,128)(2,1)} %update.5) | copy-start | bytes 196612
  26.1 11.4 %copy-start.2 = (f32[128,128]{1,0:T(8,128)S(1)}, f32[128,128]{1,0:T(8,128)}, u32[]{:S(2)}) copy-start(f32[128,128]{1,0:T(8,128)} %get-tuple-element.49.read) | copy-start | bytes 196612
  26.1 11.4 %collective-permute-start.4 = (bf16[144,128]{1,0:T(8,128)(2,1)S(1)}, bf16[144,128]{1,0:T(8,128)(2,1)S(1)}, u32[]{:S(2)}, u32[]{:S(2)}) collective-permute-start(bf16[144,128]{1,0:T(8,128)(2,1)S(1)} %get-tuple-element.46), channel_id=1, source_target_pairs={{266,306},{298,394},{394,298},{426,386},{386,426},{418,258},{258,4... | collective-permute-start | bytes 110600 | tf_op jit(solution)/shard_map/ppermute | solution.py:65
  29.6 7.9 %collective-permute-start.3 = (bf16[128,128]{1,0:T(8,128)(2,1)S(1)}, bf16[128,128]{1,0:T(8,128)(2,1)S(1)}, u32[]{:S(2)}, u32[]{:S(2)}) collective-permute-start(bf16[128,128]{1,0:T(8,128)(2,1)S(1)} %get-tuple-element.45), channel_id=1, source_target_pairs={{266,298},{298,266},{394,426},{426,394},{386,418},{418,386},{258,2... | collective-permute-start | bytes 98312 | tf_op jit(solution)/shard_map/ppermute | solution.py:65
  37.5 6.4 %copy-start.6 = (bf16[2,128,128]{2,1,0:T(8,128)(2,1)S(1)}, bf16[2,128,128]{2,1,0:T(8,128)(2,1)}, u32[]{:S(2)}) copy-start(bf16[2,128,128]{2,1,0:T(8,128)(2,1)} %filter_out.3) | copy-start | bytes 196612
  39.6 5.9 %collective-permute-start.6 = (bf16[144,128]{1,0:T(8,128)(2,1)S(1)}, bf16[144,128]{1,0:T(8,128)(2,1)S(1)}, u32[]{:S(2)}, u32[]{:S(2)}) collective-permute-start(bf16[144,128]{1,0:T(8,128)(2,1)S(1)} %get-tuple-element.52), channel_id=1, source_target_pairs={{266,306},{298,394},{394,298},{426,386},{386,426},{418,258},{258,4... | collective-permute-start | bytes 110600 | tf_op jit(solution)/shard_map/ppermute | solution.py:65
  41.6 4.0 %collective-permute-start.5 = (bf16[128,128]{1,0:T(8,128)(2,1)S(1)}, bf16[128,128]{1,0:T(8,128)(2,1)S(1)}, u32[]{:S(2)}, u32[]{:S(2)}) collective-permute-start(bf16[128,128]{1,0:T(8,128)(2,1)S(1)} %get-tuple-element.51), channel_id=1, source_target_pairs={{266,298},{298,266},{394,426},{426,394},{386,418},{418,386},{258,2... | collective-permute-start | bytes 98312 | tf_op jit(solution)/shard_map/ppermute | solution.py:65
  45.6 7.6 %copy-start.3 = (f32[1,3,128]{2,0,1:T(1,128)S(1)}, f32[1,3,128]{2,0,1:T(1,128)}, u32[]{:S(2)}) copy-start(f32[1,3,128]{2,0,1:T(1,128)} %param.16) | copy-start | bytes 4612
  45.6 45.5 %copy-start.4 = (f32[1,3,128]{2,0,1:T(1,128)S(1)}, f32[1,3,128]{2,0,1:T(1,128)}, u32[]{:S(2)}) copy-start(f32[1,3,128]{2,0,1:T(1,128)} %param.15) | copy-start | bytes 4612
  45.6 45.5 %copy-start.5 = (f32[8,128]{1,0:T(8,128)S(1)}, f32[8,128]{1,0:T(8,128)}, u32[]{:S(2)}) copy-start(f32[8,128]{1,0:T(8,128)} %get-tuple-element.65.settings) | copy-start | bytes 12292
  46.9 6.3 %collective-permute-start.8 = (f32[24,128]{1,0:T(8,128)S(1)}, f32[24,128]{1,0:T(8,128)S(1)}, u32[]{:S(2)}, u32[]{:S(2)}) collective-permute-start(f32[24,128]{1,0:T(8,128)S(1)} %get-tuple-element.62), channel_id=1, source_target_pairs={{266,306},{298,394},{394,298},{426,386},{386,426},{418,258},{258,4... | collective-permute-start | bytes 36872 | tf_op jit(solution)/shard_map/ppermute | solution.py:65
  50.1 3.1 %collective-permute-start.7 = (f32[8,128]{1,0:T(8,128)S(1)}, f32[8,128]{1,0:T(8,128)S(1)}, u32[]{:S(2)}, u32[]{:S(2)}) collective-permute-start(f32[8,128]{1,0:T(8,128)S(1)} %get-tuple-element.61), channel_id=1, source_target_pairs={{266,298},{298,266},{394,426},{426,394},{386,418},{418,386},{258,2... | collective-permute-start | bytes 12296 | tf_op jit(solution)/shard_map/ppermute | solution.py:65

commit v6 on v5

--- a/solution.py
+++ b/solution.py
@@ -41,10 +41,10 @@
 
 
 RING = [
-    (1, 2), (1, 3), (0, 3), (0, 2), (0, 1), (0, 0), (1, 0), (1, 1),
-    (2, 1), (2, 0), (3, 0), (3, 1), (3, 2), (3, 3), (2, 3), (2, 2),
+    (2, 2), (1, 2), (1, 3), (0, 3), (0, 2), (0, 1), (0, 0), (1, 0),
+    (1, 1), (2, 1), (2, 0), (3, 0), (3, 1), (3, 2), (3, 3), (2, 3),
 ]
-LAYER_PAIR = (1, 0, 3, 2)
+LAYER_PAIR = (0, 2, 3, 1)
 
 
 def worker(image, domain):
@@ -145,8 +145,6 @@
     copies = [pltpu.make_async_copy(a, b, sems.at[i]) for i, (a, b) in enumerate(pairs)]
     for copy in copies:
         copy.start()
-    copies[0].wait()
-    out[0:CHANNELS, :] = embed[...].astype(F32).T.astype(BF16)
     copies[1].wait()
     out[ROW_NEAR:PACK_ROWS, :] = (near[...].astype(F32) - float(ATOMS)).astype(BF16)
     for copy in copies[2:]:
@@ -155,6 +153,8 @@
     parts = [jnp.concatenate([p.astype(F32), zeros], axis=0) for p in thirds(flat(pos))]
     aux = jnp.concatenate([up[...].astype(F32), down[...].astype(F32), zeros, zeros[:1]], axis=0)
     out[ROW_POS:ROW_NEAR, :] = jnp.concatenate(parts + [aux], axis=0).astype(BF16)
+    copies[0].wait()
+    out[0:CHANNELS, :] = embed[...].astype(F32).T.astype(BF16)
 
 
 def weights_kernel(

time: 92.6 us -> 91.5 us (0.988)
  blocking collectives: 37.6 us -> 35 us
  starting transfers between devices: 35.9 us -> 37.3 us
    all_to_all x1, blocking collectives: 15.4 us -> 12.8 us  [per_device(): lax.all_to_all(blocks, AXES, 0, 0, tiled=True, axis_index_groups=LAYERS)]
    ppermute x9, starting transfers between devices: 35.9 us -> 37.3 us  [move(): return lax.ppermute(values, AXES, pairs)]
  transfers between devices with their start and end apart: 9 -> 9, of which waited for: 1 -> 2; matrix products, arithmetic and copies ran while one was open for 0% -> 0% of each run, Pallas kernels for 6% -> 6%
where the time goes in v6:
time: 91.5 us; the launch traced here: 90.9 us
  starting transfers between devices  37.3 us (41%)
  blocking collectives  35 us (38%)
  Pallas kernels  13.9 us (15%)
  between operations  4.13 us (5%)
    ppermute x9, starting transfers between devices, move(): return lax.ppermute(values, AXES, pairs)  37.3 us
    all_to_all x1, blocking collectives, per_device(): lax.all_to_all(blocks, AXES, 0, 0, tiled=True, axis_index_groups=COLUMNS)  22.2 us
    all_to_all x1, blocking collectives, per_device(): lax.all_to_all(blocks, AXES, 0, 0, tiled=True, axis_index_groups=LAYERS)  12.8 us
    pallas_call x11, Pallas kernels, call(): pl.pallas_call(kernel, out_shape=[jax.ShapeDtypeStruct(s, t) for s, t in...  12.3 us
  transfers between devices with their start and end apart: 9, of which 2 were waited for; matrix products, arithmetic and copies ran while one was open for 0% of the time, Pallas kernels for 6%

profile of v6, /device:TPU:1, one launch (start us, length us, event | category | flops | bytes accessed | tf_op | source)
XLA Modules:
  0.0 90.9 jit_solution(12299584233070020179)
XLA Ops:
  0.6 1.5 %pack_kernel.1.after = bf16[192,128]{1,0:T(8,128)(2,1)} custom-call(f32[3,1,128]{2,1,0:T(1,128)} %bitcast.20, bf16[128,128]{1,0:T(8,128)(2,1)} %embed_in.1, s32[32,128]{1,0:T(8,128)} %bitcast.22, s32[1,128]{1,0:T(1,128)} %bitcast.23, s32[1,128]{1,0:T(1,128)} %bitcast.24), custom_call_target="tpu_custom_call" | custom-call | tf_op jit(solution)/shard_map/pack_kernel/pallas_call | solution.py:460
  2.2 10.0 %collective-permute-start = (bf16[192,128]{1,0:T(8,128)(2,1)}, bf16[192,128]{1,0:T(8,128)(2,1)S(1)}, u32[]{:S(2)}, u32[]{:S(2)}) collective-permute-start(bf16[192,128]{1,0:T(8,128)(2,1)} %pack_kernel.1.after), channel_id=1, source_target_pairs={{0,272},{1,304},{2,264},{3,296},{4,392},{5,424},{6,384},{7,416},{8... | collective-permute-start | bytes 147464 | tf_op jit(solution)/shard_map/ppermute | solution.py:65
  14.8 1.7 %weights_kernel.1 = (bf16[256,128]{1,0:T(8,128)(2,1)}, bf16[256,128]{1,0:T(8,128)(2,1)}, bf16[256,128]{1,0:T(8,128)(2,1)}, f32[128,128]{1,0:T(8,128)}, f32[8,128]{1,0:T(8,128)}) custom-call(bf16[192,128]{1,0:T(8,128)(2,1)} %pack_kernel.1.after, f32[2,16,128]{2,1,0:T(8,128)} %filter_in.1, bf16[2,128,128]{2,1,0:T(8,128)(2,1)} %filter_out.3, ...), custom_call_target="tpu_custom_call" | custom-call | flops 100000000 | bytes 197136 | tf_op jit(solution)/shard_map/weights_kernel/pallas_call | solution.py:448
  16.5 0.0 copy-start.1
  16.5 0.0 copy-start.7
  16.5 0.1 collective-permute-done.pack
  16.6 0.2 lists_kernel.1
  16.8 4.1 %collective-permute-start.2 = (bf16[176,128]{1,0:T(8,128)(2,1)S(1)}, bf16[176,128]{1,0:T(8,128)(2,1)S(1)}, u32[]{:S(2)}, u32[]{:S(2)}) collective-permute-start(bf16[176,128]{1,0:T(8,128)(2,1)S(1)} %get-tuple-element.37), channel_id=1, source_target_pairs={{272,432},{304,264},{264,304},{296,392},{392,296},{424,384},{384,4... | collective-permute-start | bytes 135176 | tf_op jit(solution)/shard_map/ppermute | solution.py:65
  20.9 6.3 %collective-permute-start.1 = (bf16[160,128]{1,0:T(8,128)(2,1)S(1)}, bf16[160,128]{1,0:T(8,128)(2,1)S(1)}, u32[]{:S(2)}, u32[]{:S(2)}) collective-permute-start(bf16[160,128]{1,0:T(8,128)(2,1)S(1)} %get-tuple-element.36), channel_id=1, source_target_pairs={{272,304},{304,272},{264,296},{296,264},{392,424},{424,392},{384,4... | collective-permute-start | bytes 122888 | tf_op jit(solution)/shard_map/ppermute | solution.py:65
  27.3 1.0 %slots_kernel.1 = (bf16[384,4096]{1,0:T(8,128)(2,1)S(1)}, f32[8,128]{1,0:T(8,128)S(1)}) custom-call(bf16[192,128]{1,0:T(8,128)(2,1)S(1)} %collective-permute-done.pack), custom_call_target="tpu_custom_call" | custom-call | flops 1000000000 | bytes 49152 | tf_op jit(solution)/shard_map/slots_kernel/pallas_call | solution.py:448
  28.3 0.0 collective-permute-done.1.from_a
  28.3 0.0 collective-permute-done.2.from_b
  28.3 0.0 copy-done.1
  28.3 0.0 copy-done.7
  28.3 0.0 copy-done.8
  28.3 1.9 %first_kernel.1 = (bf16[128,128]{1,0:T(8,128)(2,1)S(1)}, bf16[128,128]{1,0:T(8,128)(2,1)S(1)}, bf16[144,128]{1,0:T(8,128)(2,1)S(1)}, f32[128,128]{1,0:T(8,128)S(...) custom-call(bf16[192,128]{1,0:T(8,128)(2,1)S(1)} %collective-permute-done.pack, ...), custom_call_target="tpu_custom_call" | custom-call | flops 1000000000 | bytes 3543040 | tf_op jit(solution)/shard_map/first_kernel/pallas_call | solution.py:448
  30.3 0.0 copy-start.2
  30.3 2.1 %collective-permute-start.4 = (bf16[144,128]{1,0:T(8,128)(2,1)S(1)}, bf16[144,128]{1,0:T(8,128)(2,1)S(1)}, u32[]{:S(2)}, u32[]{:S(2)}) collective-permute-start(bf16[144,128]{1,0:T(8,128)(2,1)S(1)} %get-tuple-element.46), channel_id=1, source_target_pairs={{272,432},{304,264},{264,304},{296,392},{392,296},{424,384},{384,4... | collective-permute-start | bytes 110600 | tf_op jit(solution)/shard_map/ppermute | solution.py:65
  32.3 5.3 %collective-permute-start.3 = (bf16[128,128]{1,0:T(8,128)(2,1)S(1)}, bf16[128,128]{1,0:T(8,128)(2,1)S(1)}, u32[]{:S(2)}, u32[]{:S(2)}) collective-permute-start(bf16[128,128]{1,0:T(8,128)(2,1)S(1)} %get-tuple-element.45), channel_id=1, source_target_pairs={{272,304},{304,272},{264,296},{296,264},{392,424},{424,392},{384,4... | collective-permute-start | bytes 98312 | tf_op jit(solution)/shard_map/ppermute | solution.py:65
  37.6 1.4 %filters_kernel.1 = (bf16[128,4096]{1,0:T(8,128)(2,1)S(1)}, f32[128,4096]{1,0:T(8,128)S(1)}) custom-call(f32[8,4096]{1,0:T(8,128)S(1)} %get-tuple-element.47.pairs, bf16[256,128]{1,0:T(8,128)(2,1)S(1)} %copy-done.7, bf16[256,128]{1,0:T(8,128)(2,1)S(1)} %copy-done.8), custom_call_target="tpu_custom_call" | custom-call | flops 1000000000 | bytes 262144 | tf_op jit(solution)/shard_map/filters_kernel/pallas_call | solution.py:448
  39.0 0.0 collective-permute-done.3.from_a
  39.0 0.0 collective-permute-done.4.from_b
  39.0 0.0 copy-done
  39.0 0.0 copy-done.2
  39.1 0.0 copy-start.6
  39.1 2.1 %second_kernel.1 = (f32[8,128]{1,0:T(8,128)S(1)}, f32[128,128]{1,0:T(8,128)S(1)}, bf16[128,4096]{1,0:T(8,128)(2,1)S(1)}, f32[128,128]{1,0:T(8,128)S(1)}, bf16[12...) custom-call(bf16[128,128]{1,0:T(8,128)(2,1)S(1)} %get-tuple-element.44.hidden, ...), custom_call_target="tpu_custom_call" | custom-call | flops 1000000000 | bytes 5541888 | tf_op jit(solution)/shard_map/second_kernel/pallas_call | solution.py:448
  41.2 1.9 %collective-permute-start.6 = (bf16[144,128]{1,0:T(8,128)(2,1)S(1)}, bf16[144,128]{1,0:T(8,128)(2,1)S(1)}, u32[]{:S(2)}, u32[]{:S(2)}) collective-permute-start(bf16[144,128]{1,0:T(8,128)(2,1)S(1)} %get-tuple-element.52), channel_id=1, source_target_pairs={{272,432},{304,264},{264,304},{296,392},{392,296},{424,384},{384,4... | collective-permute-start | bytes 110600 | tf_op jit(solution)/shard_map/ppermute | solution.py:65
  43.1 2.4 %collective-permute-start.5 = (bf16[128,128]{1,0:T(8,128)(2,1)S(1)}, bf16[128,128]{1,0:T(8,128)(2,1)S(1)}, u32[]{:S(2)}, u32[]{:S(2)}) collective-permute-start(bf16[128,128]{1,0:T(8,128)(2,1)S(1)} %get-tuple-element.51), channel_id=1, source_target_pairs={{272,304},{304,272},{264,296},{296,264},{392,424},{424,392},{384,4... | collective-permute-start | bytes 98312 | tf_op jit(solution)/shard_map/ppermute | solution.py:65
  45.5 0.0 copy-done.6
  45.5 1.6 %slope_kernel.1 = (f32[8,4096]{1,0:T(8,128)S(1)}, f32[128,4096]{1,0:T(8,128)S(1)}) custom-call(f32[128,128]{1,0:T(8,128)S(1)} %get-tuple-element.54.grad_two, bf16[128,4096]{1,0:T(8,128)(2,1)S(1)} %get-tuple-element.55.rows_two, bf16[128,4096]{1,0:T(8,128)(2,1)S(1)} %get-tuple-element.56.slope_two, bf16[2,128,128]{2,1,0:T(8,128)(2,1)S(1)} %copy-done.6, ...), custom_call_target="tpu_custom_call" | custom-call | flops 1000000000 | bytes 3538944 | tf_op jit(solution)/shard_map/slope_kernel/pallas_call | solution.py:448
  47.0 0.0 collective-permute-done.5.from_a
  47.1 0.0 collective-permute-done.6.from_b
  47.1 0.0 copy-start.3
  47.1 0.0 copy-start.4
  47.1 0.0 copy-start.5
  47.1 1.3 %third_kernel.1 = (f32[8,128]{1,0:T(8,128)S(1)}, f32[8,128]{1,0:T(8,128)S(1)}, f32[24,128]{1,0:T(8,128)S(1)}) custom-call(f32[128,128]{1,0:T(8,128)S(1)} %get-tuple-element.50.grad_own, bf16[128,128]{1,0:T(8,128)(2,1)S(1)} %collective-permute-done.5.from_a, bf16[144,128]{1,0:T(8,128)(2,1)S(1)} %collective-permute-done.6.from_b, ...), custom_call_target="tpu_custom_call" | custom-call | flops 1000000000 | bytes 5836800 | tf_op jit(solution)/shard_map/third_kernel/pallas_call | solution.py:448
  48.4 3.2 %collective-permute-start.8 = (f32[24,128]{1,0:T(8,128)S(1)}, f32[24,128]{1,0:T(8,128)S(1)}, u32[]{:S(2)}, u32[]{:S(2)}) collective-permute-start(f32[24,128]{1,0:T(8,128)S(1)} %get-tuple-element.62), channel_id=1, source_target_pairs={{272,432},{304,264},{264,304},{296,392},{392,296},{424,384},{384,4... | collective-permute-start | bytes 36872 | tf_op jit(solution)/shard_map/ppermute | solution.py:65
  51.6 2.0 %collective-permute-start.7 = (f32[8,128]{1,0:T(8,128)S(1)}, f32[8,128]{1,0:T(8,128)S(1)}, u32[]{:S(2)}, u32[]{:S(2)}) collective-permute-start(f32[8,128]{1,0:T(8,128)S(1)} %get-tuple-element.61), channel_id=1, source_target_pairs={{272,304},{304,272},{264,296},{296,264},{392,424},{424,392},{384,4... | collective-permute-start | bytes 12296 | tf_op jit(solution)/shard_map/ppermute | solution.py:65
  54.3 0.4 collective-permute-done.7.from_a
  54.7 0.0 collective-permute-done.8.from_b
  54.7 0.0 copy-done.3
  54.7 0.2 sums_kernel.1
  54.9 22.2 %all_to_all.16 = f32[16,8,128]{2,1,0:T(8,128)S(1)} all-to-all(f32[16,8,128]{2,1,0:T(8,128)S(1)} %bitcast.17), channel_id=1, replica_groups={{272,273,336,337,276,277,340,341,278,279,342,343,274,275,338,339},{304,..., dimensions={0} | all-to-all | bytes 131072 | tf_op jit(solution)/shard_map/all_to_all | solution.py:545
  77.1 0.1 column_kernel.1
  77.3 12.8 %all_to_all.17.blocks = f32[160,2,128]{2,1,0:T(2,128)S(1)} all-to-all(f32[160,2,128]{2,1,0:T(2,128)S(1)} %column_kernel.1), channel_id=1, replica_groups={{272,304,264,296,392,424,384,416,256,288,128,160,0,32,8,40,136,168,144,..., dimensions={0} | all-to-all | bytes 327680 | tf_op jit(solution)/shard_map/all_to_all | solution.py:547
  90.0 0.0 copy-done.4
  90.1 0.0 copy-done.5
  90.1 0.8 final_kernel.1
  (2 shorter events, 0.0 us)
Async XLA Ops:
  2.2 14.5 %collective-permute-start = (bf16[192,128]{1,0:T(8,128)(2,1)}, bf16[192,128]{1,0:T(8,128)(2,1)S(1)}, u32[]{:S(2)}, u32[]{:S(2)}) collective-permute-start(bf16[192,128]{1,0:T(8,128)(2,1)} %pack_kernel.1.after), channel_id=1, source_target_pairs={{0,272},{1,304},{2,264},{3,296},{4,392},{5,424},{6,384},{7,416},{8... | collective-permute-start | bytes 147464 | tf_op jit(solution)/shard_map/ppermute | solution.py:65
  16.5 11.8 %copy-start.1 = (bf16[256,128]{1,0:T(8,128)(2,1)S(1)}, bf16[256,128]{1,0:T(8,128)(2,1)}, u32[]{:S(2)}) copy-start(bf16[256,128]{1,0:T(8,128)(2,1)} %get-tuple-element.43.update_t) | copy-start | bytes 196612
  16.5 11.8 %copy-start.7 = (bf16[256,128]{1,0:T(8,128)(2,1)S(1)}, bf16[256,128]{1,0:T(8,128)(2,1)}, u32[]{:S(2)}) copy-start(bf16[256,128]{1,0:T(8,128)(2,1)} %get-tuple-element.41.in_t) | copy-start | bytes 196612
  16.5 11.8 %copy-start.8 = (bf16[256,128]{1,0:T(8,128)(2,1)S(1)}, bf16[256,128]{1,0:T(8,128)(2,1)}, u32[]{:S(2)}) copy-start(bf16[256,128]{1,0:T(8,128)(2,1)} %get-tuple-element.42.out_t) | copy-start | bytes 196612
  16.8 11.5 %collective-permute-start.2 = (bf16[176,128]{1,0:T(8,128)(2,1)S(1)}, bf16[176,128]{1,0:T(8,128)(2,1)S(1)}, u32[]{:S(2)}, u32[]{:S(2)}) collective-permute-start(bf16[176,128]{1,0:T(8,128)(2,1)S(1)} %get-tuple-element.37), channel_id=1, source_target_pairs={{272,432},{304,264},{264,304},{296,392},{392,296},{424,384},{384,4... | collective-permute-start | bytes 135176 | tf_op jit(solution)/shard_map/ppermute | solution.py:65
  20.9 7.4 %collective-permute-start.1 = (bf16[160,128]{1,0:T(8,128)(2,1)S(1)}, bf16[160,128]{1,0:T(8,128)(2,1)S(1)}, u32[]{:S(2)}, u32[]{:S(2)}) collective-permute-start(bf16[160,128]{1,0:T(8,128)(2,1)S(1)} %get-tuple-element.36), channel_id=1, source_target_pairs={{272,304},{304,272},{264,296},{296,264},{392,424},{424,392},{384,4... | collective-permute-start | bytes 122888 | tf_op jit(solution)/shard_map/ppermute | solution.py:65
  30.2 8.8 %copy-start = (bf16[2,128,128]{2,1,0:T(8,128)(2,1)S(1)}, bf16[2,128,128]{2,1,0:T(8,128)(2,1)}, u32[]{:S(2)}) copy-start(bf16[2,128,128]{2,1,0:T(8,128)(2,1)} %update.5) | copy-start | bytes 196612
  30.3 8.8 %copy-start.2 = (f32[128,128]{1,0:T(8,128)S(1)}, f32[128,128]{1,0:T(8,128)}, u32[]{:S(2)}) copy-start(f32[128,128]{1,0:T(8,128)} %get-tuple-element.49.read) | copy-start | bytes 196612
  30.3 8.8 %collective-permute-start.4 = (bf16[144,128]{1,0:T(8,128)(2,1)S(1)}, bf16[144,128]{1,0:T(8,128)(2,1)S(1)}, u32[]{:S(2)}, u32[]{:S(2)}) collective-permute-start(bf16[144,128]{1,0:T(8,128)(2,1)S(1)} %get-tuple-element.46), channel_id=1, source_target_pairs={{272,432},{304,264},{264,304},{296,392},{392,296},{424,384},{384,4... | collective-permute-start | bytes 110600 | tf_op jit(solution)/shard_map/ppermute | solution.py:65
  32.3 6.7 %collective-permute-start.3 = (bf16[128,128]{1,0:T(8,128)(2,1)S(1)}, bf16[128,128]{1,0:T(8,128)(2,1)S(1)}, u32[]{:S(2)}, u32[]{:S(2)}) collective-permute-start(bf16[128,128]{1,0:T(8,128)(2,1)S(1)} %get-tuple-element.45), channel_id=1, source_target_pairs={{272,304},{304,272},{264,296},{296,264},{392,424},{424,392},{384,4... | collective-permute-start | bytes 98312 | tf_op jit(solution)/shard_map/ppermute | solution.py:65
  39.1 6.4 %copy-start.6 = (bf16[2,128,128]{2,1,0:T(8,128)(2,1)S(1)}, bf16[2,128,128]{2,1,0:T(8,128)(2,1)}, u32[]{:S(2)}) copy-start(bf16[2,128,128]{2,1,0:T(8,128)(2,1)} %filter_out.3) | copy-start | bytes 196612
  41.2 5.9 %collective-permute-start.6 = (bf16[144,128]{1,0:T(8,128)(2,1)S(1)}, bf16[144,128]{1,0:T(8,128)(2,1)S(1)}, u32[]{:S(2)}, u32[]{:S(2)}) collective-permute-start(bf16[144,128]{1,0:T(8,128)(2,1)S(1)} %get-tuple-element.52), channel_id=1, source_target_pairs={{272,432},{304,264},{264,304},{296,392},{392,296},{424,384},{384,4... | collective-permute-start | bytes 110600 | tf_op jit(solution)/shard_map/ppermute | solution.py:65
  43.1 4.0 %collective-permute-start.5 = (bf16[128,128]{1,0:T(8,128)(2,1)S(1)}, bf16[128,128]{1,0:T(8,128)(2,1)S(1)}, u32[]{:S(2)}, u32[]{:S(2)}) collective-permute-start(bf16[128,128]{1,0:T(8,128)(2,1)S(1)} %get-tuple-element.51), channel_id=1, source_target_pairs={{272,304},{304,272},{264,296},{296,264},{392,424},{424,392},{384,4... | collective-permute-start | bytes 98312 | tf_op jit(solution)/shard_map/ppermute | solution.py:65
  47.1 7.6 %copy-start.3 = (f32[1,3,128]{2,0,1:T(1,128)S(1)}, f32[1,3,128]{2,0,1:T(1,128)}, u32[]{:S(2)}) copy-start(f32[1,3,128]{2,0,1:T(1,128)} %param.16) | copy-start | bytes 4612
  47.1 43.0 %copy-start.4 = (f32[1,3,128]{2,0,1:T(1,128)S(1)}, f32[1,3,128]{2,0,1:T(1,128)}, u32[]{:S(2)}) copy-start(f32[1,3,128]{2,0,1:T(1,128)} %param.15) | copy-start | bytes 4612
  47.1 43.0 %copy-start.5 = (f32[8,128]{1,0:T(8,128)S(1)}, f32[8,128]{1,0:T(8,128)}, u32[]{:S(2)}) copy-start(f32[8,128]{1,0:T(8,128)} %get-tuple-element.65.settings) | copy-start | bytes 12292
  48.4 6.3 %collective-permute-start.8 = (f32[24,128]{1,0:T(8,128)S(1)}, f32[24,128]{1,0:T(8,128)S(1)}, u32[]{:S(2)}, u32[]{:S(2)}) collective-permute-start(f32[24,128]{1,0:T(8,128)S(1)} %get-tuple-element.62), channel_id=1, source_target_pairs={{272,432},{304,264},{264,304},{296,392},{392,296},{424,384},{384,4... | collective-permute-start | bytes 36872 | tf_op jit(solution)/shard_map/ppermute | solution.py:65
  51.6 3.1 %collective-permute-start.7 = (f32[8,128]{1,0:T(8,128)S(1)}, f32[8,128]{1,0:T(8,128)S(1)}, u32[]{:S(2)}, u32[]{:S(2)}) collective-permute-start(f32[8,128]{1,0:T(8,128)S(1)} %get-tuple-element.61), channel_id=1, source_target_pairs={{272,304},{304,272},{264,296},{296,264},{392,424},{424,392},{384,4... | collective-permute-start | bytes 12296 | tf_op jit(solution)/shard_map/ppermute | solution.py:65

commit v7 on v6

--- a/solution.py
+++ b/solution.py
@@ -158,12 +158,13 @@
 
 
 def weights_kernel(
-    after, filter_in, filter_out, update, readout, reset, spring, time_step, mixing,
+    after, filter_in, filter_out, update, readout, reset, spring, time_step, mixing, climb,
     in_t, out_t, update_t, read, settings,
 ):
-    for j, value in enumerate((reset[0].astype(F32), spring[0], time_step[0], mixing[0])):
+    values = (reset[0].astype(F32), spring[0], time_step[0], mixing[0], climb[0].astype(F32))
+    for j, value in enumerate(values):
         settings[j : j + 1, :] = jnp.full((1, ATOMS), value, F32)
-    settings[4:8, :] = jnp.zeros((4, ATOMS), F32)
+    settings[5:8, :] = jnp.zeros((3, ATOMS), F32)
     for l in range(2):
         rows = pl.ds(l * 128, 128)
         high, low = halves(0.5 * filter_in[l])
@@ -337,7 +338,7 @@
     spare(send_b)
 
 
-def sums_kernel(force, from_a, from_b, list_a, list_b, own, energy, velocity, climb, out):
+def sums_kernel(force, from_a, from_b, list_a, list_b, own, energy, velocity, settings, out):
     image, _, _ = place()
 
     def returned(block, chosen):
@@ -351,7 +352,7 @@
     speed_sq = jnp.where(movable, jnp.sum(speed * speed), 0.0)
     lane = lax.broadcasted_iota(jnp.int32, (1, ATOMS), 1)
     last = jnp.where(lane == 6 * IMAGES, speed_sq, 0.0)
-    last = jnp.where(lane == 7 * IMAGES + image, climb[0].astype(F32), last)
+    last = jnp.where(lane == 7 * IMAGES + image, settings[4:5, :], last)
     block = jnp.concatenate([f[0:3], own[0:3, :], energy[0:1, :], last], axis=0)
     for j in range(IMAGES):
         out[j * 8 : (j + 1) * 8, :] = block
@@ -487,9 +488,9 @@
         [((256, 128), BF16), ((256, 128), BF16), ((256, 128), BF16), (square, F32), ((8, ATOMS), F32)],
         (
             packed, filter_in, filter_out, update_weight, readout.reshape(1, CHANNELS),
-            reset, spring.reshape(1), time_step.reshape(1), mixing.reshape(1),
+            reset, spring.reshape(1), time_step.reshape(1), mixing.reshape(1), climb,
         ),
-        scalars=(5, 6, 7, 8),
+        scalars=(5, 6, 7, 8, 9),
         flops=10**8,
         limit=60 << 20,
     )
@@ -539,8 +540,7 @@
     (blocks,) = call(
         sums_kernel,
         [((IMAGES * 8, ATOMS), F32)],
-        (force, from_a, from_b, list_a, list_b, own, energy, velocity, climb),
-        scalars=(8,),
+        (force, from_a, from_b, list_a, list_b, own, energy, velocity, settings),
     )
     column = lax.all_to_all(blocks, AXES, 0, 0, tiled=True, axis_index_groups=COLUMNS)
     (blocks,) = call(column_kernel, [((DOMAINS * BLOCK, 2, ATOMS), F32)], (column,))

time: 91.5 us -> 94.6 us (1.034)
  waiting for transfers between devices: 0.5 us -> 6.93 us
  starting transfers between devices: 37.3 us -> 34.3 us
    ppermute x9, waiting for transfers between devices: 0.5 us -> 6.93 us  [move(): return lax.ppermute(values, AXES, pairs)]
    ppermute x9, starting transfers between devices: 37.3 us -> 34.3 us  [move(): return lax.ppermute(values, AXES, pairs)]
    all_to_all x1, blocking collectives: 22.2 us -> 20.4 us  [per_device(): lax.all_to_all(blocks, AXES, 0, 0, tiled=True, axis_index_groups=COLUMNS)]
    all_to_all x1, blocking collectives: 12.8 us -> 14.4 us  [per_device(): lax.all_to_all(blocks, AXES, 0, 0, tiled=True, axis_index_groups=LAYERS)]
  transfers between devices with their start and end apart: 9 -> 9, of which waited for: 2 -> 4; matrix products, arithmetic and copies ran while one was open for 0% -> 0% of each run, Pallas kernels for 6% -> 6%
where the time goes in v7:
time: 94.6 us; the launch traced here: 94 us
  blocking collectives  34.8 us (37%)
  starting transfers between devices  34.3 us (36%)
  Pallas kernels  13.9 us (15%)
  waiting for transfers between devices  6.93 us (7%)
  between operations  4.04 us (4%)
    ppermute x9, starting transfers between devices, move(): return lax.ppermute(values, AXES, pairs)  34.3 us
    all_to_all x1, blocking collectives, per_device(): lax.all_to_all(blocks, AXES, 0, 0, tiled=True, axis_index_groups=COLUMNS)  20.4 us
    all_to_all x1, blocking collectives, per_device(): lax.all_to_all(blocks, AXES, 0, 0, tiled=True, axis_index_groups=LAYERS)  14.4 us
    pallas_call x11, Pallas kernels, call(): pl.pallas_call(kernel, out_shape=[jax.ShapeDtypeStruct(s, t) for s, t in...  12.4 us
    ppermute x9, waiting for transfers between devices, move(): return lax.ppermute(values, AXES, pairs)  6.93 us
  transfers between devices with their start and end apart: 9, of which 4 were waited for; matrix products, arithmetic and copies ran while one was open for 0% of the time, Pallas kernels for 6%

profile of v7, /device:TPU:1, one launch (start us, length us, event | category | flops | bytes accessed | tf_op | source)
XLA Modules:
  0.0 94.0 jit_solution(4938620848933757887)
XLA Ops:
  0.6 1.5 %pack_kernel.1.after = bf16[192,128]{1,0:T(8,128)(2,1)} custom-call(f32[3,1,128]{2,1,0:T(1,128)} %bitcast.20, bf16[128,128]{1,0:T(8,128)(2,1)} %embed_in.1, s32[32,128]{1,0:T(8,128)} %bitcast.22, s32[1,128]{1,0:T(1,128)} %bitcast.23, s32[1,128]{1,0:T(1,128)} %bitcast.24), custom_call_target="tpu_custom_call" | custom-call | tf_op jit(solution)/shard_map/pack_kernel/pallas_call | solution.py:461
  2.2 10.0 %collective-permute-start = (bf16[192,128]{1,0:T(8,128)(2,1)}, bf16[192,128]{1,0:T(8,128)(2,1)S(1)}, u32[]{:S(2)}, u32[]{:S(2)}) collective-permute-start(bf16[192,128]{1,0:T(8,128)(2,1)} %pack_kernel.1.after), channel_id=1, source_target_pairs={{0,272},{1,304},{2,264},{3,296},{4,392},{5,424},{6,384},{7,416},{8... | collective-permute-start | bytes 147464 | tf_op jit(solution)/shard_map/ppermute | solution.py:65
  15.4 1.7 %weights_kernel.1 = (bf16[256,128]{1,0:T(8,128)(2,1)}, bf16[256,128]{1,0:T(8,128)(2,1)}, bf16[256,128]{1,0:T(8,128)(2,1)}, f32[128,128]{1,0:T(8,128)}, f32[8,128]{1,0:T(8,128)}) custom-call(bf16[192,128]{1,0:T(8,128)(2,1)} %pack_kernel.1.after, f32[2,16,128]{2,1,0:T(8,128)} %filter_in.1, bf16[2,128,128]{2,1,0:T(8,128)(2,1)} %filter_out.3, ...), custom_call_target="tpu_custom_call" | custom-call | flops 100000000 | bytes 197140 | tf_op jit(solution)/shard_map/weights_kernel/pallas_call | solution.py:449
  17.2 0.0 copy-start.1
  17.2 0.0 copy-start.7
  17.2 0.0 copy-start.8
  17.2 0.0 collective-permute-done.pack
  17.2 0.2 lists_kernel.1
  17.4 5.2 %collective-permute-start.1 = (bf16[160,128]{1,0:T(8,128)(2,1)S(1)}, bf16[160,128]{1,0:T(8,128)(2,1)S(1)}, u32[]{:S(2)}, u32[]{:S(2)}) collective-permute-start(bf16[160,128]{1,0:T(8,128)(2,1)S(1)} %get-tuple-element.36), channel_id=1, source_target_pairs={{272,304},{304,272},{264,296},{296,264},{392,424},{424,392},{384,4... | collective-permute-start | bytes 122888 | tf_op jit(solution)/shard_map/ppermute | solution.py:65
  22.6 1.9 %collective-permute-start.2 = (bf16[176,128]{1,0:T(8,128)(2,1)S(1)}, bf16[176,128]{1,0:T(8,128)(2,1)S(1)}, u32[]{:S(2)}, u32[]{:S(2)}) collective-permute-start(bf16[176,128]{1,0:T(8,128)(2,1)S(1)} %get-tuple-element.37), channel_id=1, source_target_pairs={{272,432},{304,264},{264,304},{296,392},{392,296},{424,384},{384,4... | collective-permute-start | bytes 135176 | tf_op jit(solution)/shard_map/ppermute | solution.py:65
  24.6 1.0 %slots_kernel.1 = (bf16[384,4096]{1,0:T(8,128)(2,1)S(1)}, f32[8,128]{1,0:T(8,128)S(1)}) custom-call(bf16[192,128]{1,0:T(8,128)(2,1)S(1)} %collective-permute-done.pack), custom_call_target="tpu_custom_call" | custom-call | flops 1000000000 | bytes 49152 | tf_op jit(solution)/shard_map/slots_kernel/pallas_call | solution.py:449
  25.6 0.0 collective-permute-done.1.from_a
  25.6 2.4 %collective-permute-done.2.from_b = bf16[176,128]{1,0:T(8,128)(2,1)S(1)} collective-permute-done((bf16[176,128]{1,0:T(8,128)(2,1)S(1)}, bf16[176,128]{1,0:T(8,128)(2,1)S(1)}, u32[]{:S(2)}, u32[]{:S(2)}) %collective-permute-start.2) | collective-permute-done | bytes 45088 | tf_op jit(solution)/shard_map/ppermute | solution.py:65
  28.0 0.0 copy-done.1
  28.0 0.0 copy-done.7
  28.0 0.0 copy-done.8
  28.0 1.9 %first_kernel.1 = (bf16[128,128]{1,0:T(8,128)(2,1)S(1)}, bf16[128,128]{1,0:T(8,128)(2,1)S(1)}, bf16[144,128]{1,0:T(8,128)(2,1)S(1)}, f32[128,128]{1,0:T(8,128)S(...) custom-call(bf16[192,128]{1,0:T(8,128)(2,1)S(1)} %collective-permute-done.pack, ...), custom_call_target="tpu_custom_call" | custom-call | flops 1000000000 | bytes 3543040 | tf_op jit(solution)/shard_map/first_kernel/pallas_call | solution.py:449
  29.9 0.0 copy-start
  29.9 0.0 copy-start.2
  29.9 3.7 %collective-permute-start.3 = (bf16[128,128]{1,0:T(8,128)(2,1)S(1)}, bf16[128,128]{1,0:T(8,128)(2,1)S(1)}, u32[]{:S(2)}, u32[]{:S(2)}) collective-permute-start(bf16[128,128]{1,0:T(8,128)(2,1)S(1)} %get-tuple-element.45), channel_id=1, source_target_pairs={{272,304},{304,272},{264,296},{296,264},{392,424},{424,392},{384,4... | collective-permute-start | bytes 98312 | tf_op jit(solution)/shard_map/ppermute | solution.py:65
  33.6 1.9 %collective-permute-start.4 = (bf16[144,128]{1,0:T(8,128)(2,1)S(1)}, bf16[144,128]{1,0:T(8,128)(2,1)S(1)}, u32[]{:S(2)}, u32[]{:S(2)}) collective-permute-start(bf16[144,128]{1,0:T(8,128)(2,1)S(1)} %get-tuple-element.46), channel_id=1, source_target_pairs={{272,432},{304,264},{264,304},{296,392},{392,296},{424,384},{384,4... | collective-permute-start | bytes 110600 | tf_op jit(solution)/shard_map/ppermute | solution.py:65
  35.6 1.4 %filters_kernel.1 = (bf16[128,4096]{1,0:T(8,128)(2,1)S(1)}, f32[128,4096]{1,0:T(8,128)S(1)}) custom-call(f32[8,4096]{1,0:T(8,128)S(1)} %get-tuple-element.47.pairs, bf16[256,128]{1,0:T(8,128)(2,1)S(1)} %copy-done.7, bf16[256,128]{1,0:T(8,128)(2,1)S(1)} %copy-done.8), custom_call_target="tpu_custom_call" | custom-call | flops 1000000000 | bytes 262144 | tf_op jit(solution)/shard_map/filters_kernel/pallas_call | solution.py:449
  37.0 0.0 collective-permute-done.3.from_a
  37.0 1.9 %collective-permute-done.4.from_b = bf16[144,128]{1,0:T(8,128)(2,1)S(1)} collective-permute-done((bf16[144,128]{1,0:T(8,128)(2,1)S(1)}, bf16[144,128]{1,0:T(8,128)(2,1)S(1)}, u32[]{:S(2)}, u32[]{:S(2)}) %collective-permute-start.4) | collective-permute-done | bytes 36896 | tf_op jit(solution)/shard_map/ppermute | solution.py:65
  38.9 0.0 copy-done
  38.9 0.0 copy-done.2
  38.9 0.0 copy-start.6
  38.9 2.1 %second_kernel.1 = (f32[8,128]{1,0:T(8,128)S(1)}, f32[128,128]{1,0:T(8,128)S(1)}, bf16[128,4096]{1,0:T(8,128)(2,1)S(1)}, f32[128,128]{1,0:T(8,128)S(1)}, bf16[12...) custom-call(bf16[128,128]{1,0:T(8,128)(2,1)S(1)} %get-tuple-element.44.hidden, ...), custom_call_target="tpu_custom_call" | custom-call | flops 1000000000 | bytes 5541888 | tf_op jit(solution)/shard_map/second_kernel/pallas_call | solution.py:449
  41.0 3.6 %collective-permute-start.5 = (bf16[128,128]{1,0:T(8,128)(2,1)S(1)}, bf16[128,128]{1,0:T(8,128)(2,1)S(1)}, u32[]{:S(2)}, u32[]{:S(2)}) collective-permute-start(bf16[128,128]{1,0:T(8,128)(2,1)S(1)} %get-tuple-element.51), channel_id=1, source_target_pairs={{272,304},{304,272},{264,296},{296,264},{392,424},{424,392},{384,4... | collective-permute-start | bytes 98312 | tf_op jit(solution)/shard_map/ppermute | solution.py:65
  44.6 1.9 %collective-permute-start.6 = (bf16[144,128]{1,0:T(8,128)(2,1)S(1)}, bf16[144,128]{1,0:T(8,128)(2,1)S(1)}, u32[]{:S(2)}, u32[]{:S(2)}) collective-permute-start(bf16[144,128]{1,0:T(8,128)(2,1)S(1)} %get-tuple-element.52), channel_id=1, source_target_pairs={{272,432},{304,264},{264,304},{296,392},{392,296},{424,384},{384,4... | collective-permute-start | bytes 110600 | tf_op jit(solution)/shard_map/ppermute | solution.py:65
  46.5 0.0 copy-done.6
  46.5 1.6 %slope_kernel.1 = (f32[8,4096]{1,0:T(8,128)S(1)}, f32[128,4096]{1,0:T(8,128)S(1)}) custom-call(f32[128,128]{1,0:T(8,128)S(1)} %get-tuple-element.54.grad_two, bf16[128,4096]{1,0:T(8,128)(2,1)S(1)} %get-tuple-element.55.rows_two, bf16[128,4096]{1,0:T(8,128)(2,1)S(1)} %get-tuple-element.56.slope_two, bf16[2,128,128]{2,1,0:T(8,128)(2,1)S(1)} %copy-done.6, ...), custom_call_target="tpu_custom_call" | custom-call | flops 1000000000 | bytes 3538944 | tf_op jit(solution)/shard_map/slope_kernel/pallas_call | solution.py:449
  48.1 0.0 collective-permute-done.5.from_a
  48.1 1.8 %collective-permute-done.6.from_b = bf16[144,128]{1,0:T(8,128)(2,1)S(1)} collective-permute-done((bf16[144,128]{1,0:T(8,128)(2,1)S(1)}, bf16[144,128]{1,0:T(8,128)(2,1)S(1)}, u32[]{:S(2)}, u32[]{:S(2)}) %collective-permute-start.6) | collective-permute-done | bytes 36896 | tf_op jit(solution)/shard_map/ppermute | solution.py:65
  49.9 0.0 copy-start.3
  49.9 1.3 %third_kernel.1 = (f32[8,128]{1,0:T(8,128)S(1)}, f32[8,128]{1,0:T(8,128)S(1)}, f32[24,128]{1,0:T(8,128)S(1)}) custom-call(f32[128,128]{1,0:T(8,128)S(1)} %get-tuple-element.50.grad_own, bf16[128,128]{1,0:T(8,128)(2,1)S(1)} %collective-permute-done.5.from_a, bf16[144,128]{1,0:T(8,128)(2,1)S(1)} %collective-permute-done.6.from_b, ...), custom_call_target="tpu_custom_call" | custom-call | flops 1000000000 | bytes 5836800 | tf_op jit(solution)/shard_map/third_kernel/pallas_call | solution.py:449
  51.2 1.9 %collective-permute-start.8 = (f32[24,128]{1,0:T(8,128)S(1)}, f32[24,128]{1,0:T(8,128)S(1)}, u32[]{:S(2)}, u32[]{:S(2)}) collective-permute-start(f32[24,128]{1,0:T(8,128)S(1)} %get-tuple-element.62), channel_id=1, source_target_pairs={{272,432},{304,264},{264,304},{296,392},{392,296},{424,384},{384,4... | collective-permute-start | bytes 36872 | tf_op jit(solution)/shard_map/ppermute | solution.py:65
  53.2 4.0 %collective-permute-start.7 = (f32[8,128]{1,0:T(8,128)S(1)}, f32[8,128]{1,0:T(8,128)S(1)}, u32[]{:S(2)}, u32[]{:S(2)}) collective-permute-start(f32[8,128]{1,0:T(8,128)S(1)} %get-tuple-element.61), channel_id=1, source_target_pairs={{272,304},{304,272},{264,296},{296,264},{392,424},{424,392},{384,4... | collective-permute-start | bytes 12296 | tf_op jit(solution)/shard_map/ppermute | solution.py:65
  57.2 0.8 collective-permute-done.7.from_a
  58.0 0.0 collective-permute-done.8.from_b
  58.0 0.0 copy-done.3
  58.0 0.0 copy-done.4
  58.0 0.2 sums_kernel.1
  58.2 20.4 %all_to_all.16 = f32[16,8,128]{2,1,0:T(8,128)S(1)} all-to-all(f32[16,8,128]{2,1,0:T(8,128)S(1)} %bitcast.17), channel_id=1, replica_groups={{272,273,336,337,276,277,340,341,278,279,342,343,274,275,338,339},{304,..., dimensions={0} | all-to-all | bytes 131072 | tf_op jit(solution)/shard_map/all_to_all | solution.py:545
  78.6 0.1 column_kernel.1
  78.8 14.4 %all_to_all.17.blocks = f32[160,2,128]{2,1,0:T(2,128)S(1)} all-to-all(f32[160,2,128]{2,1,0:T(2,128)S(1)} %column_kernel.1), channel_id=1, replica_groups={{272,304,264,296,392,424,384,416,256,288,128,160,0,32,8,40,136,168,144,..., dimensions={0} | all-to-all | bytes 327680 | tf_op jit(solution)/shard_map/all_to_all | solution.py:547
  93.2 0.0 copy-done.5
  93.2 0.8 final_kernel.1
  (2 shorter events, 0.0 us)
Async XLA Ops:
  2.2 15.0 %collective-permute-start = (bf16[192,128]{1,0:T(8,128)(2,1)}, bf16[192,128]{1,0:T(8,128)(2,1)S(1)}, u32[]{:S(2)}, u32[]{:S(2)}) collective-permute-start(bf16[192,128]{1,0:T(8,128)(2,1)} %pack_kernel.1.after), channel_id=1, source_target_pairs={{0,272},{1,304},{2,264},{3,296},{4,392},{5,424},{6,384},{7,416},{8... | collective-permute-start | bytes 147464 | tf_op jit(solution)/shard_map/ppermute | solution.py:65
  17.2 10.8 %copy-start.1 = (bf16[256,128]{1,0:T(8,128)(2,1)S(1)}, bf16[256,128]{1,0:T(8,128)(2,1)}, u32[]{:S(2)}) copy-start(bf16[256,128]{1,0:T(8,128)(2,1)} %get-tuple-element.43.update_t) | copy-start | bytes 196612
  17.2 10.8 %copy-start.7 = (bf16[256,128]{1,0:T(8,128)(2,1)S(1)}, bf16[256,128]{1,0:T(8,128)(2,1)}, u32[]{:S(2)}) copy-start(bf16[256,128]{1,0:T(8,128)(2,1)} %get-tuple-element.41.in_t) | copy-start | bytes 196612
  17.2 10.8 %copy-start.8 = (bf16[256,128]{1,0:T(8,128)(2,1)S(1)}, bf16[256,128]{1,0:T(8,128)(2,1)}, u32[]{:S(2)}) copy-start(bf16[256,128]{1,0:T(8,128)(2,1)} %get-tuple-element.42.out_t) | copy-start | bytes 196612
  17.4 8.2 %collective-permute-start.1 = (bf16[160,128]{1,0:T(8,128)(2,1)S(1)}, bf16[160,128]{1,0:T(8,128)(2,1)S(1)}, u32[]{:S(2)}, u32[]{:S(2)}) collective-permute-start(bf16[160,128]{1,0:T(8,128)(2,1)S(1)} %get-tuple-element.36), channel_id=1, source_target_pairs={{272,304},{304,272},{264,296},{296,264},{392,424},{424,392},{384,4... | collective-permute-start | bytes 122888 | tf_op jit(solution)/shard_map/ppermute | solution.py:65
  22.6 5.4 %collective-permute-start.2 = (bf16[176,128]{1,0:T(8,128)(2,1)S(1)}, bf16[176,128]{1,0:T(8,128)(2,1)S(1)}, u32[]{:S(2)}, u32[]{:S(2)}) collective-permute-start(bf16[176,128]{1,0:T(8,128)(2,1)S(1)} %get-tuple-element.37), channel_id=1, source_target_pairs={{272,432},{304,264},{264,304},{296,392},{392,296},{424,384},{384,4... | collective-permute-start | bytes 135176 | tf_op jit(solution)/shard_map/ppermute | solution.py:65
  29.9 9.0 %copy-start = (bf16[2,128,128]{2,1,0:T(8,128)(2,1)S(1)}, bf16[2,128,128]{2,1,0:T(8,128)(2,1)}, u32[]{:S(2)}) copy-start(bf16[2,128,128]{2,1,0:T(8,128)(2,1)} %update.5) | copy-start | bytes 196612
  29.9 9.0 %copy-start.2 = (f32[128,128]{1,0:T(8,128)S(1)}, f32[128,128]{1,0:T(8,128)}, u32[]{:S(2)}) copy-start(f32[128,128]{1,0:T(8,128)} %get-tuple-element.49.read) | copy-start | bytes 196612
  29.9 7.1 %collective-permute-start.3 = (bf16[128,128]{1,0:T(8,128)(2,1)S(1)}, bf16[128,128]{1,0:T(8,128)(2,1)S(1)}, u32[]{:S(2)}, u32[]{:S(2)}) collective-permute-start(bf16[128,128]{1,0:T(8,128)(2,1)S(1)} %get-tuple-element.45), channel_id=1, source_target_pairs={{272,304},{304,272},{264,296},{296,264},{392,424},{424,392},{384,4... | collective-permute-start | bytes 98312 | tf_op jit(solution)/shard_map/ppermute | solution.py:65
  33.6 5.3 %collective-permute-start.4 = (bf16[144,128]{1,0:T(8,128)(2,1)S(1)}, bf16[144,128]{1,0:T(8,128)(2,1)S(1)}, u32[]{:S(2)}, u32[]{:S(2)}) collective-permute-start(bf16[144,128]{1,0:T(8,128)(2,1)S(1)} %get-tuple-element.46), channel_id=1, source_target_pairs={{272,432},{304,264},{264,304},{296,392},{392,296},{424,384},{384,4... | collective-permute-start | bytes 110600 | tf_op jit(solution)/shard_map/ppermute | solution.py:65
  38.9 7.6 %copy-start.6 = (bf16[2,128,128]{2,1,0:T(8,128)(2,1)S(1)}, bf16[2,128,128]{2,1,0:T(8,128)(2,1)}, u32[]{:S(2)}) copy-start(bf16[2,128,128]{2,1,0:T(8,128)(2,1)} %filter_out.3) | copy-start | bytes 196612
  41.0 7.1 %collective-permute-start.5 = (bf16[128,128]{1,0:T(8,128)(2,1)S(1)}, bf16[128,128]{1,0:T(8,128)(2,1)S(1)}, u32[]{:S(2)}, u32[]{:S(2)}) collective-permute-start(bf16[128,128]{1,0:T(8,128)(2,1)S(1)} %get-tuple-element.51), channel_id=1, source_target_pairs={{272,304},{304,272},{264,296},{296,264},{392,424},{424,392},{384,4... | collective-permute-start | bytes 98312 | tf_op jit(solution)/shard_map/ppermute | solution.py:65
  44.6 5.4 %collective-permute-start.6 = (bf16[144,128]{1,0:T(8,128)(2,1)S(1)}, bf16[144,128]{1,0:T(8,128)(2,1)S(1)}, u32[]{:S(2)}, u32[]{:S(2)}) collective-permute-start(bf16[144,128]{1,0:T(8,128)(2,1)S(1)} %get-tuple-element.52), channel_id=1, source_target_pairs={{272,432},{304,264},{264,304},{296,392},{392,296},{424,384},{384,4... | collective-permute-start | bytes 110600 | tf_op jit(solution)/shard_map/ppermute | solution.py:65
  49.9 8.1 %copy-start.3 = (f32[8,128]{1,0:T(8,128)S(1)}, f32[8,128]{1,0:T(8,128)}, u32[]{:S(2)}) copy-start(f32[8,128]{1,0:T(8,128)} %get-tuple-element.65.settings) | copy-start | bytes 12292
  49.9 8.1 %copy-start.4 = (f32[1,3,128]{2,0,1:T(1,128)S(1)}, f32[1,3,128]{2,0,1:T(1,128)}, u32[]{:S(2)}) copy-start(f32[1,3,128]{2,0,1:T(1,128)} %param.16) | copy-start | bytes 4612
  49.9 43.2 %copy-start.5 = (f32[1,3,128]{2,0,1:T(1,128)S(1)}, f32[1,3,128]{2,0,1:T(1,128)}, u32[]{:S(2)}) copy-start(f32[1,3,128]{2,0,1:T(1,128)} %param.15) | copy-start | bytes 4612
  51.2 6.8 %collective-permute-start.8 = (f32[24,128]{1,0:T(8,128)S(1)}, f32[24,128]{1,0:T(8,128)S(1)}, u32[]{:S(2)}, u32[]{:S(2)}) collective-permute-start(f32[24,128]{1,0:T(8,128)S(1)} %get-tuple-element.62), channel_id=1, source_target_pairs={{272,432},{304,264},{264,304},{296,392},{392,296},{424,384},{384,4... | collective-permute-start | bytes 36872 | tf_op jit(solution)/shard_map/ppermute | solution.py:65
  53.2 4.8 %collective-permute-start.7 = (f32[8,128]{1,0:T(8,128)S(1)}, f32[8,128]{1,0:T(8,128)S(1)}, u32[]{:S(2)}, u32[]{:S(2)}) collective-permute-start(f32[8,128]{1,0:T(8,128)S(1)} %get-tuple-element.61), channel_id=1, source_target_pairs={{272,304},{304,272},{264,296},{296,264},{392,424},{424,392},{384,4... | collective-permute-start | bytes 12296 | tf_op jit(solution)/shard_map/ppermute | solution.py:65
